TPU v7x, 32 devices: a whole 2x2x4 slice. The times are simulated.
32 devices in a mesh: group: 4 (over y, core), dp: 8 (over z, x).
Axes of the slice: x: 2, y: 2, z: 4, core: 2. Of those that a mesh axis runs over, the one named last changes fastest.
Arguments:
- pixels: bfloat16 [1, 2, 128, 49, 3072], P(None, None, ('group', 'dp')), may hold values from -6 to 6
- counts: int32 [1, 2, 32], P(None, None, ('group', 'dp')), may hold values from 1 to 4, as said below
- labels: int32 [1, 2, 128], P(None, None, ('group', 'dp')), may hold values from 0 to 999
- text: bfloat16 [1000, 512], replicated, may hold values from -0.25 to 0.25
- master: float32 [22272, 768], P('dp')
- outer_momentum: float32 [22272, 768], P('dp'), may hold values from -0.06 to 0.06
- first_moment: float32 [4, 22272, 768], P('group', 'dp')
- second_moment: float32 [4, 22272, 768], P('group', 'dp')
- eval_pixels: bfloat16 [128, 49, 3072], P(('group', 'dp')), may hold values from -6 to 6
- eval_counts: int32 [32], P(('group', 'dp')), may hold values from 1 to 4, as said below
- eval_labels: int32 [128], P(('group', 'dp')), may hold values from 0 to 999
Outputs:
- new_master: float32 [22272, 768], P('dp')
- new_outer: float32 [22272, 768], P('dp')
- new_first: float32 [4, 22272, 768], P('group', 'dp')
- new_second: float32 [4, 22272, 768], P('group', 'dp')
- clip_norms: float32 [4, 1], P('group')
- loss_sums: float32 [4, 1], P('group')
- image_counts: float32 [4, 1], P('group')
- post_grads: float32 [4, 1, 2, 768], P('group')
- eval_losses: float32 [128], P(('group', 'dp'))
Inputs may be any that keep to these rules, and one draw needn't show every extreme that they name: `counts`: real images of a device in a micro-batch; slots at or past it are padding; the last device of each worker along dp is full. `eval_counts`: real held-out images of a device; slots at or past it are padding; the last device of each worker along dp is full.
All inputs are finite; a program needn't handle non-finite values.
Results may differ from a plain program's by a relative error of at most 0.019.
Values may be sent and summed in bfloat16 or wider, within the bound.
A program may use at most 576 MiB of HBM per device.

v0:
```python
import jax
import jax.numpy as jnp
from jax import lax
from jax.sharding import PartitionSpec as P

D = 768
HEADS = 12
HEAD = 64
FF = 3072
PATCH_IN = 3072
EMB = 512
CLASSES = 1000
LAYERS = 2
MICRO = 2
STEP = 10
SEQ = 50
ROWS_RAW = 22079


LN_EPS = 1e-05
NORM_EPS = 1e-06
LOGIT_SCALE = 50.0
SMOOTH = 0.1
CLIP_MAX = 0.02
BETA_ONE = 0.9
BETA_TWO = 0.98
ADAM_EPS = 1e-08
RATE = 0.02
DECAY = 0.1
OUTER_RATE = 0.7
OUTER_MOM = 0.9
GELU_SLOPE = 1.702


def product(pattern, first_arg, second_arg):
    return jnp.einsum(pattern, first_arg, second_arg, preferred_element_type=jnp.float32)


def layer_norm(values, gain_row, bias_row):
    row_mean = jnp.mean(values, -1, keepdims=True)
    centred = values - row_mean
    row_var = jnp.mean(centred * centred, -1, keepdims=True)
    return centred * lax.rsqrt(row_var + LN_EPS) * gain_row + bias_row


def quick_gelu(inner_pre):
    return inner_pre * jax.nn.sigmoid(GELU_SLOPE * inner_pre)


def unit_length(embedded):
    return embedded * lax.rsqrt(jnp.sum(embedded * embedded, -1, keepdims=True) + NORM_EPS)


def layout_rows():
    table_start = PATCH_IN
    layer_start = table_start + SEQ + 1
    block_size = 4 * D + 2 * FF
    norm_start = layer_start + LAYERS * block_size
    head_start = norm_start + 4 * LAYERS + 4
    return (table_start, layer_start, block_size, norm_start, head_start)


def split_block(block_rows):
    return (
        block_rows[: 3 * D].reshape(3, D, D),
        block_rows[3 * D : 4 * D],
        block_rows[4 * D : 4 * D + FF],
        block_rows[4 * D + FF :],
    )


def split_heads(qkv_rows):
    shaped = qkv_rows.reshape(qkv_rows.shape[0], SEQ, 3, HEADS, HEAD)
    return (shaped[:, :, 0], shaped[:, :, 1], shaped[:, :, 2])


def layer_forward(hidden, block_rows, norm_rows):
    w_qkv, w_out, w_in, w_back = split_block(block_rows)
    batch_size = hidden.shape[0]
    normed, first_back = jax.vjp(layer_norm, hidden, norm_rows[0], norm_rows[1])
    normed = normed.astype(jnp.bfloat16)
    qkv_rows = product("btd,jde->btje", normed, w_qkv).astype(jnp.bfloat16)
    query_rows, key_rows, value_rows = split_heads(qkv_rows)
    scores = product("bqhd,bkhd->bhqk", query_rows, key_rows) * HEAD ** (-0.5)
    log_total = jax.nn.logsumexp(scores, axis=-1, keepdims=True)
    attn_probs = jnp.exp(scores - log_total).astype(jnp.bfloat16)
    mixed_rows = product("bhqk,bkhd->bqhd", attn_probs, value_rows).astype(jnp.bfloat16)
    mixed_rows = mixed_rows.reshape(batch_size, SEQ, D)
    after_attn = hidden + product("btd,de->bte", mixed_rows, w_out)
    normed_two, second_back = jax.vjp(layer_norm, after_attn, norm_rows[2], norm_rows[3])
    normed_two = normed_two.astype(jnp.bfloat16)
    inner_pre = product("btd,fd->btf", normed_two, w_in)
    activated, gelu_back = jax.vjp(quick_gelu, inner_pre)
    activated = activated.astype(jnp.bfloat16)
    output = after_attn + product("btf,fd->btd", activated, w_back)
    kept_state = (
        first_back,
        normed,
        qkv_rows,
        log_total,
        mixed_rows,
        second_back,
        normed_two,
        gelu_back,
        activated,
    )
    return (output, kept_state)


def layer_backward(grad_out, kept_state, block_rows):
    w_qkv, w_out, w_in, w_back = split_block(block_rows)
    (
        first_back,
        normed,
        qkv_rows,
        log_total,
        mixed_rows,
        second_back,
        normed_two,
        gelu_back,
        activated,
    ) = kept_state
    batch_size = grad_out.shape[0]
    grad_branch = grad_out.astype(jnp.bfloat16)
    grad_act = product("btd,fd->btf", grad_branch, w_back)
    grad_w_back = product("btf,btd->fd", activated, grad_branch)
    grad_pre = gelu_back(grad_act)[0].astype(jnp.bfloat16)
    grad_w_in = product("btf,btd->fd", grad_pre, normed_two)
    grad_normed_two = product("btf,fd->btd", grad_pre, w_in)
    grad_attn_in, grad_gain_two, grad_bias_two = second_back(grad_normed_two)
    grad_after = grad_out + grad_attn_in
    grad_proj = grad_after.astype(jnp.bfloat16)
    grad_w_out = product("btd,bte->de", mixed_rows, grad_proj)
    grad_mixed = product("bte,de->btd", grad_proj, w_out).astype(jnp.bfloat16)
    grad_mixed = grad_mixed.reshape(batch_size, SEQ, HEADS, HEAD)
    query_rows, key_rows, value_rows = split_heads(qkv_rows)
    scale_factor = HEAD ** (-0.5)
    scores = product("bqhd,bkhd->bhqk", query_rows, key_rows) * scale_factor
    soft_rows = jnp.exp(scores - log_total)
    grad_soft = product("bqhd,bkhd->bhqk", grad_mixed, value_rows)
    grad_value = product("bhqk,bqhd->bkhd", soft_rows.astype(jnp.bfloat16), grad_mixed)
    grad_scores = soft_rows * (grad_soft - jnp.sum(grad_soft * soft_rows, -1, keepdims=True))
    grad_scores = grad_scores.astype(jnp.bfloat16)
    grad_query = product("bhqk,bkhd->bqhd", grad_scores, key_rows) * scale_factor
    grad_key = product("bhqk,bqhd->bkhd", grad_scores, query_rows) * scale_factor
    grad_qkv = jnp.stack([grad_query, grad_key, grad_value], axis=2)
    grad_qkv = grad_qkv.reshape(batch_size, SEQ, 3, D).astype(jnp.bfloat16)
    grad_w_qkv = product("btd,btje->jde", normed, grad_qkv).reshape(3 * D, D)
    grad_normed = product("btje,jde->btd", grad_qkv, w_qkv)
    grad_in, grad_gain_one, grad_bias_one = first_back(grad_normed)
    weight_grads = jnp.concatenate([grad_w_qkv, grad_w_out, grad_w_in, grad_w_back], axis=0)
    norm_grads = jnp.stack([grad_gain_one, grad_bias_one, grad_gain_two, grad_bias_two])
    return (grad_after + grad_in, weight_grads, norm_grads)


def micro_step(weights, pixel_block, image_count, label_row, text, with_grads):
    table_start, layer_start, block_size, norm_start, head_start = layout_rows()
    batch_size = pixel_block.shape[0]
    table_rows = weights[table_start:layer_start].astype(jnp.float32)
    norm_rows = weights[norm_start:head_start].astype(jnp.float32)
    head_rows = weights[head_start : head_start + EMB]
    patches = product("bpi,id->bpd", pixel_block, weights[:PATCH_IN])
    class_rows = jnp.broadcast_to(table_rows[0], (batch_size, 1, D))
    embedded_in = jnp.concatenate([class_rows, patches], axis=1) + table_rows[1:]
    hidden, pre_back = jax.vjp(layer_norm, embedded_in, norm_rows[0], norm_rows[1])
    kept_layers = []
    for layer_index in range(LAYERS):
        block_rows = weights[
            layer_start + layer_index * block_size : layer_start + (layer_index + 1) * block_size
        ]
        hidden, kept_state = layer_forward(
            hidden, block_rows, norm_rows[2 + 4 * layer_index : 6 + 4 * layer_index]
        )
        kept_layers.append(kept_state)
    pooled, post_back = jax.vjp(layer_norm, hidden[:, 0], norm_rows[-2], norm_rows[-1])
    pooled = pooled.astype(jnp.bfloat16)
    embedded = product("bd,ed->be", pooled, head_rows)
    unit_rows, unit_back = jax.vjp(unit_length, embedded)
    logits = LOGIT_SCALE * product("be,ce->bc", unit_rows.astype(jnp.bfloat16), text)
    log_probs = jax.nn.log_softmax(logits, axis=-1)
    onehot = (label_row[:, None] == jnp.arange(CLASSES)[None, :]).astype(jnp.float32)
    target = (1.0 - SMOOTH) * onehot + SMOOTH / CLASSES
    live_mask = (jnp.arange(batch_size) < image_count).astype(jnp.float32)
    image_losses = -live_mask * jnp.sum(target * log_probs, -1)
    if not with_grads:
        return (image_losses, None)
    loss_sum = jnp.sum(image_losses)
    grad_logits = (jnp.exp(log_probs) - target) * live_mask[:, None]
    grad_raw = (LOGIT_SCALE * grad_logits).astype(jnp.bfloat16)
    grad_unit = product("bc,ce->be", grad_raw, text)
    grad_embed = unit_back(grad_unit)[0].astype(jnp.bfloat16)
    grad_head = product("be,bd->ed", grad_embed, pooled)
    grad_pooled = product("be,ed->bd", grad_embed, head_rows)
    grad_class, grad_gain_post, grad_bias_post = post_back(grad_pooled)
    grad_hidden = jnp.concatenate(
        [grad_class[:, None], jnp.zeros((batch_size, SEQ - 1, D), jnp.float32)], axis=1
    )
    layer_grads = [None] * LAYERS
    layer_norm_grads = [None] * LAYERS
    for layer_index in reversed(range(LAYERS)):
        block_rows = weights[
            layer_start + layer_index * block_size : layer_start + (layer_index + 1) * block_size
        ]
        grad_hidden, layer_grads[layer_index], layer_norm_grads[layer_index] = layer_backward(
            grad_hidden, kept_layers[layer_index], block_rows
        )
    grad_embedded, grad_gain_pre, grad_bias_pre = pre_back(grad_hidden)
    grad_patches = grad_embedded[:, 1:].astype(jnp.bfloat16)
    grad_patch_w = product("bpi,bpd->id", pixel_block, grad_patches)
    grad_table = jnp.concatenate(
        [jnp.sum(grad_embedded[:, 0], axis=0)[None], jnp.sum(grad_embedded, axis=0)], axis=0
    )
    grad_norms = jnp.concatenate(
        [jnp.stack([grad_gain_pre, grad_bias_pre])]
        + layer_norm_grads
        + [jnp.stack([grad_gain_post, grad_bias_post])],
        axis=0,
    )
    padding = jnp.zeros((weights.shape[0] - ROWS_RAW, D), jnp.float32)
    grad_rows = jnp.concatenate(
        [grad_patch_w, grad_table] + layer_grads + [grad_norms, grad_head, padding], axis=0
    )
    return (loss_sum, grad_rows)


def fetch_weights(params):
    return lax.all_gather(params.astype(jnp.bfloat16), "dp", axis=0, tiled=True)


def reduce_rows(grad_rows):
    return lax.psum_scatter(
        grad_rows.astype(jnp.bfloat16), "dp", scatter_dimension=0, tiled=True
    ).astype(jnp.float32)


def adam_update(params, moment_one, moment_two, clipped, step_number):
    moment_one = BETA_ONE * moment_one + (1.0 - BETA_ONE) * clipped
    moment_two = BETA_TWO * moment_two + (1.0 - BETA_TWO) * clipped * clipped
    corrected_one = moment_one / (1.0 - BETA_ONE**step_number)
    corrected_two = moment_two / (1.0 - BETA_TWO**step_number)
    params = params - RATE * (corrected_one / (jnp.sqrt(corrected_two) + ADAM_EPS) + DECAY * params)
    return (params, moment_one, moment_two)


def nesterov(master_rows, momentum_rows, mean_delta):
    momentum_next = OUTER_MOM * momentum_rows + mean_delta
    return (master_rows - OUTER_RATE * (mean_delta + OUTER_MOM * momentum_next), momentum_next)


def post_rows_local(reduced):
    head_start = layout_rows()[4]
    local_rows = reduced.shape[0]
    row_start = lax.axis_index("dp") * local_rows
    wanted = head_start - 2 + jnp.arange(2)
    picker = (row_start + jnp.arange(local_rows)[None, :] == wanted[:, None]).astype(jnp.float32)
    return jnp.dot(
        picker, reduced, precision=lax.Precision.HIGHEST, preferred_element_type=jnp.float32
    )


def per_device(
    pixels,
    counts,
    labels,
    text,
    master,
    outer_momentum,
    first_moment,
    second_moment,
    eval_pixels,
    eval_counts,
    eval_labels,
):
    params = master
    moment_one = first_moment[0]
    moment_two = second_moment[0]
    norm_list, loss_list, count_list, post_list = ([], [], [], [])
    weights = fetch_weights(params)
    grad_total = None
    loss_total = jnp.zeros((), jnp.float32)
    for micro_index in range(MICRO):
        loss_part, grad_rows = micro_step(
            weights,
            pixels[0, micro_index],
            counts[0, micro_index, 0],
            labels[0, micro_index],
            text,
            True,
        )
        loss_total = loss_total + loss_part
        grad_total = grad_rows if micro_index == 0 else grad_total + grad_rows
    reduced = reduce_rows(grad_total)
    image_total = jnp.sum(counts[0]).astype(jnp.float32)
    squares = jnp.sum(reduced * reduced)
    post_local = post_rows_local(reduced)
    loss_all, count_all, square_all, post_all = lax.psum(
        (loss_total, image_total, squares, post_local), "dp"
    )
    gradient = reduced / count_all
    grad_norm = jnp.sqrt(square_all) / count_all
    clip_factor = CLIP_MAX / jnp.maximum(grad_norm, CLIP_MAX)
    clipped = gradient * clip_factor
    params, moment_one, moment_two = adam_update(params, moment_one, moment_two, clipped, STEP)
    norm_list.append(grad_norm)
    loss_list.append(loss_all)
    count_list.append(count_all)
    post_list.append(post_all / count_all * clip_factor)
    delta = master - params
    groups = lax.axis_size("group")
    mean_delta = lax.psum(delta.astype(jnp.bfloat16), "group").astype(jnp.float32) / groups
    new_master, new_outer = nesterov(master, outer_momentum, mean_delta)
    soup_rows = lax.all_gather(new_master.astype(jnp.bfloat16), "dp", axis=0, tiled=True)
    eval_losses, unused_grads = micro_step(
        soup_rows, eval_pixels, eval_counts[0], eval_labels, text, False
    )
    return (
        new_master,
        new_outer,
        moment_one[None],
        moment_two[None],
        jnp.stack(norm_list)[None],
        jnp.stack(loss_list)[None],
        jnp.stack(count_list)[None],
        jnp.stack(post_list)[None],
        eval_losses,
    )


def solution(mesh):
    return jax.shard_map(
        per_device,
        mesh=mesh,
        in_specs=(
            P(None, None, ("group", "dp"), None, None),
            P(None, None, ("group", "dp")),
            P(None, None, ("group", "dp")),
            P(),
            P("dp", None),
            P("dp", None),
            P("group", "dp", None),
            P("group", "dp", None),
            P(("group", "dp"), None, None),
            P(("group", "dp")),
            P(("group", "dp")),
        ),
        out_specs=(
            P("dp", None),
            P("dp", None),
            P("group", "dp", None),
            P("group", "dp", None),
            P("group", None),
            P("group", None),
            P("group", None),
            P("group", None, None, None),
            P(("group", "dp")),
        ),
        check_vma=False,
    )
```

profile of v0, /device:TPU:25, one launch (start us, length us, event | category | flops | bytes accessed | tf_op | source)
XLA Modules:
  0.0 2910.7 jit_solution(5120858827231465442)
XLA Ops:
  20.8 643.8 %all-gather.3.cloned.1.call-done = bf16[22272,768]{1,0:T(8,128)(2,1)} async-done(((bf16[2784,768]{1,0:T(8,128)(2,1)}), bf16[22272,768]{1,0:T(8,128)(2,1)}) %all-gather.3.cloned.1.call-update) | async-done | bytes 34209808 | tf_op jit(solution)/shard_map/all_gather | solution.py:227
  1143.4 8.0 copy.866
  1151.4 8.1 copy.870
  1172.0 8.2 copy.760
  1180.2 8.0 copy.764
  1199.4 94.0 %concatenate.34 = f32[22272,768]{0,1:T(8,128)} concatenate(f32[3072,768]{0,1:T(8,128)} %convolution_bitcast_fusion.4, f32[1,768]{0,1:T(8,128)S(1)} %broadcast_in_dim.206, f32[50,768]{0,1:T(8,128)S(1)} %copy.865, f32[2304,768]{0,1:T(8,128)} %copy.866, f32[768,768]{0,1:T(8,128)} %convolution_bitcast_fusion.11, f32[3072,768]{0,1:T(8,128)} %convolution_bitcast_fusion.3, ...), dimensions={0} | concatenate | bytes 136839168 | tf_op jit(solution)/shard_map/concatenate | solution.py:220
  1293.4 95.1 %concatenate.31 = f32[22272,768]{0,1:T(8,128)} concatenate(f32[3072,768]{0,1:T(8,128)} %convolution_bitcast_fusion.9, f32[1,768]{0,1:T(8,128)} %broadcast_in_dim.104, f32[50,768]{0,1:T(8,128)} %copy.759, f32[2304,768]{0,1:T(8,128)} %copy.760, f32[768,768]{0,1:T(8,128)} %convolution_bitcast_fusion.13, f32[3072,768]{0,1:T(8,128)} %convolution_bitcast_fusion.8, ...), dimensions={0} | concatenate | bytes 136839168 | tf_op jit(solution)/shard_map/concatenate | solution.py:220
  1388.5 53.5 %add_convert_fusion = bf16[22272,768]{0,1:T(8,128)(2,1)} fusion(f32[22272,768]{0,1:T(8,128)} %concatenate.31, f32[22272,768]{0,1:T(8,128)} %concatenate.34), kind=kLoop, calls=%fused_computation | loop fusion | flops 34209792 | bytes 171048960 | tf_op jit(solution)/shard_map/convert_element_type | solution.py:232
  1442.0 44.5 %copy.983 = bf16[22272,768]{1,0:T(8,128)(2,1)} copy(bf16[22272,768]{0,1:T(8,128)(2,1)} %add_convert_fusion) | data formatting | bytes 68419584
  1486.6 9.1 copy.892
  1497.0 9.1 copy.656
  1506.1 9.1 copy.887
  1519.3 511.8 %reduce-scatter.4.cloned.1.call-done = bf16[2784,768]{1,0:T(8,128)(2,1)} async-done(((bf16[22272,768]{1,0:T(8,128)(2,1)}), bf16[2784,768]{1,0:T(8,128)(2,1)}) %reduce-scatter.4.cloned.1.call-update) | async-done | bytes 4276240
  2043.4 14.7 all-reduce.2
  2059.5 23.3 fusion.263
  2082.9 9.5 copy.891
  2092.4 83.4 %all-reduce.5.cloned.1.call-done = bf16[2784,768]{0,1:T(8,128)(2,1)} async-done(((bf16[2784,768]{0,1:T(8,128)(2,1)}), bf16[2784,768]{0,1:T(8,128)(2,1)}) %all-reduce.5.cloned.1.call-update) | async-done | bytes 4276240 | tf_op jit(solution)/shard_map/psum | solution.py:310
  2175.8 14.3 fusion.268
  2197.3 9.2 copy.911
  2206.5 9.2 copy.912
  2216.9 9.1 copy.909
  2226.0 9.0 copy.910
  2235.0 612.3 %all-gather.5.cloned.1.call-done = bf16[22272,768]{1,0:T(8,128)(2,1)} async-done(((bf16[2784,768]{1,0:T(8,128)(2,1)}), bf16[22272,768]{1,0:T(8,128)(2,1)}) %all-gather.5.cloned.1.call-update) | async-done | bytes 34209808 | tf_op jit(solution)/shard_map/all_gather | solution.py:312
  2871.8 7.6 fusion.314
  (927 shorter events, 584.5 us)
Async XLA Ops:
  7.2 2841.1 %copy-start = (bf16[4,49,3072]{2,0,1:T(4,128)(2,1)S(1)}, bf16[4,49,3072]{2,0,1:T(4,128)(2,1)}, u32[]{:S(2)}) copy-start(bf16[4,49,3072]{2,0,1:T(4,128)(2,1)} %param.20) | copy-start | bytes 3612676
  7.2 657.4 %all-gather.3.cloned.1.call-start = ((), (), s32[]{:S(2)}) async-start(), calls=%async_computation.1 | async-start | bytes 38486016 | tf_op jit(solution)/shard_map/all_gather | solution.py:227
  13.2 2017.9 %reduce-scatter.4.cloned.1.call-start = ((), (), s32[]{:S(2)}) async-start(), calls=%async_computation.4 | async-start | bytes 38486016
  20.8 648.6 %copy-start.106 = (bf16[1,1,4,49,3072]{4,2,3,1,0:T(4,128)(2,1)}, bf16[1,1,4,49,3072]{4,2,3,1,0:T(4,128)(2,1)S(1)}, u32[]{:S(2)}) copy-start(bf16[1,1,4,49,3072]{4,2,3,1,0:T(4,128)(2,1)S(1)} %get-tuple-element.174) | copy-start | bytes 3612676
  751.0 11.8 copy-start.243
  880.8 12.3 copy-start.157
  895.9 9.9 copy-start.114
  912.1 10.4 copy-start.116
  947.9 12.6 copy-start.248
  960.5 16.6 copy-start.133
  1151.4 11.4 copy-start.199
  1159.5 9.8 copy-start.215
  1180.2 9.9 copy-start.194
  1180.2 10.8 copy-start.214
  1180.2 11.7 copy-start.193
  1180.2 12.7 copy-start.213
  1180.2 13.6 copy-start.192
  1188.2 9.3 copy-start.210
  1188.2 10.2 copy-start.209
  1486.5 689.2 %all-reduce.5.cloned.1.call-start = ((), (), s32[]{:S(2)}) async-start(), calls=%async_computation.2 | async-start | bytes 8650752 | tf_op jit(solution)/shard_map/psum | solution.py:310
  1506.1 9.2 copy-start.225
  1506.1 9.2 copy-start.227
  1506.1 9.2 copy-start.234
  2082.9 764.4 %all-gather.5.cloned.1.call-start = ((), (), s32[]{:S(2)}) async-start(), calls=%async_computation.3 | async-start | bytes 38486016 | tf_op jit(solution)/shard_map/all_gather | solution.py:312
  (230 other events, 857.3 us)
Sparse Core Ops, SparseCore 0:
  13.4 651.1 all-gather.2
  1486.7 544.3 reduce-scatter.3
  2083.0 92.7 all-reduce.4
  2196.8 650.4 all-gather.4
where the time goes:
time: 2930 us; the launch traced here: 2910 us
  waiting for transfers between devices  1850 us (63%)
  local copies, waits for them, and re-layouts  551 us (19%)
  matrix products  279 us (10%)
  other arithmetic  191 us (7%)
    all_gather x1, waiting for transfers between devices, fetch_weights(): return lax.all_gather(params.astype(jnp.bfloat16), 'dp', axis=0, tiled=True)  644 us
    all_gather x1, waiting for transfers between devices, per_device(): lax.all_gather(new_master.astype(jnp.bfloat16), 'dp', axis=0, tiled=True)  612 us
    unnamed x5, waiting for transfers between devices  512 us
    dot_general x99, matrix products, product(): jnp.einsum(pattern, first_arg, second_arg, preferred_element_type=jnp.flo...  279 us
    concatenate x2, local copies, waits for them, and re-layouts, micro_step(): jnp.concatenate([grad_patch_w, grad_table] + layer_grads + [grad_norms, g...  189 us
    unnamed x518, local copies, waits for them, and re-layouts  155 us
    psum x1, waiting for transfers between devices, per_device(): lax.psum(delta.astype(jnp.bfloat16), 'group').astype(jnp.float32) / groups  83.4 us
  transfers between devices with their start and end apart: 4, of which 4 were waited for; matrix products, arithmetic and copies ran while one was open for 3% of the time, Pallas kernels for 0%

commit v1 on v0

--- a/solution.py
+++ b/solution.py
@@ -1,7 +1,13 @@
+import functools
+
 import jax
 import jax.numpy as jnp
 from jax import lax
+from jax.experimental import pallas as pl
+from jax.experimental.pallas import tpu as pltpu
 from jax.sharding import PartitionSpec as P
+
+MESH = pl.DeviceIdType.MESH
 
 D = 768
 HEADS = 12
@@ -30,6 +36,7 @@
 OUTER_RATE = 0.7
 OUTER_MOM = 0.9
 GELU_SLOPE = 1.702
+SPARE = 13
 
 
 def product(pattern, first_arg, second_arg):
@@ -148,12 +155,14 @@
     grad_w_qkv = product("btd,btje->jde", normed, grad_qkv).reshape(3 * D, D)
     grad_normed = product("btje,jde->btd", grad_qkv, w_qkv)
     grad_in, grad_gain_one, grad_bias_one = first_back(grad_normed)
-    weight_grads = jnp.concatenate([grad_w_qkv, grad_w_out, grad_w_in, grad_w_back], axis=0)
+    weight_grads = jnp.concatenate(
+        [piece.astype(jnp.bfloat16) for piece in (grad_w_qkv, grad_w_out, grad_w_in, grad_w_back)], axis=0
+    )
     norm_grads = jnp.stack([grad_gain_one, grad_bias_one, grad_gain_two, grad_bias_two])
     return (grad_after + grad_in, weight_grads, norm_grads)
 
 
-def micro_step(weights, pixel_block, image_count, label_row, text, with_grads):
+def micro_step(weights, pixel_block, live_mask, label_row, text, with_grads):
     table_start, layer_start, block_size, norm_start, head_start = layout_rows()
     batch_size = pixel_block.shape[0]
     table_rows = weights[table_start:layer_start].astype(jnp.float32)
@@ -180,7 +189,6 @@
     log_probs = jax.nn.log_softmax(logits, axis=-1)
     onehot = (label_row[:, None] == jnp.arange(CLASSES)[None, :]).astype(jnp.float32)
     target = (1.0 - SMOOTH) * onehot + SMOOTH / CLASSES
-    live_mask = (jnp.arange(batch_size) < image_count).astype(jnp.float32)
     image_losses = -live_mask * jnp.sum(target * log_probs, -1)
     if not with_grads:
         return (image_losses, None)
@@ -216,21 +224,400 @@
         + [jnp.stack([grad_gain_post, grad_bias_post])],
         axis=0,
     )
-    padding = jnp.zeros((weights.shape[0] - ROWS_RAW, D), jnp.float32)
+    spare = jnp.zeros((SPARE, D), jnp.float32)
+    padding = jnp.zeros((weights.shape[0] - ROWS_RAW - SPARE, D), jnp.float32)
+    table_block = jnp.concatenate([grad_table, spare], axis=0)
+    tail_block = jnp.concatenate([grad_norms, grad_head, padding], axis=0)
     grad_rows = jnp.concatenate(
-        [grad_patch_w, grad_table] + layer_grads + [grad_norms, grad_head, padding], axis=0
+        [
+            piece.astype(jnp.bfloat16)
+            for piece in [grad_patch_w, table_block] + layer_grads + [tail_block]
+        ],
+        axis=0,
     )
     return (loss_sum, grad_rows)
 
 
+def on_grid():
+    return lax.axis_size("group") == 4 and lax.axis_size("dp") == 8
+
+
+def place():
+    worker = lax.axis_index("group")
+    rank = lax.axis_index("dp")
+    return (worker // 2, worker % 2, rank // 2, rank % 2)
+
+
+def device_at(y, c, z, x):
+    return (y * 2 + c, z * 2 + x)
+
+
+def chunk_rows(total, count):
+    units = total // 16
+    chunks = []
+    start = 0
+    for index in range(count):
+        size = units * (index + 1) // count - units * index // count
+        first = size // 2 if index % 2 else size - size // 2
+        chunks.append((start * 16, first * 16, (size - first) * 16))
+        start += size
+    return chunks
+
+
+def gather_kernel(chunks, part_ref, full_ref, local_sem, sends, recvs):
+    half_cols = part_ref.shape[1]
+    y, c, z, x = place()
+    cols = pl.ds(pl.multiple_of(c * half_cols, half_cols), half_cols)
+    over_x = device_at(y, c, z, 1 - x)
+    over_y = device_at(1 - y, c, z, x)
+    sibling = device_at(y, 1 - c, z, x)
+    along_z = [device_at(y, c, (z + step) % 4, x) for step in (1, 2, 3)]
+    barrier = pltpu.get_barrier_semaphore()
+    for other in [over_x, over_y, sibling] + along_z:
+        pl.semaphore_signal(barrier, inc=1, device_id=other, device_id_type=MESH)
+    local = pltpu.make_async_copy(part_ref, full_ref.at[z, x, y, :, cols], local_sem)
+    local.start()
+    pl.semaphore_wait(barrier, 6)
+
+    def send(piece, other, stage, index):
+        pltpu.make_async_remote_copy(
+            src_ref=piece,
+            dst_ref=piece,
+            send_sem=sends.at[stage, index],
+            recv_sem=recvs.at[stage, index],
+            device_id=other,
+            device_id_type=MESH,
+        ).start()
+
+    def arrived(piece, stage, index):
+        pltpu.make_async_copy(piece, piece, recvs.at[stage, index]).wait()
+
+    def sent(piece, stage, index):
+        pltpu.make_async_copy(piece, piece, sends.at[stage, index]).wait()
+
+    def pieces(index):
+        start, first, second = chunks[index]
+        rows = pl.ds(start, first + second)
+        rows_a = pl.ds(start, first)
+        rows_b = pl.ds(start + first, second)
+        return {
+            0: full_ref.at[pl.ds(0, 3), 0, 0, rows, cols],
+            1: full_ref.at[:, x, y, rows_a, cols],
+            2: full_ref.at[:, x, y, rows_b, cols],
+            3: full_ref.at[:, x, :, rows_a, cols],
+            4: full_ref.at[:, :, y, rows_b, cols],
+            5: full_ref.at[:, :, :, rows, cols],
+        }
+
+    total = len(chunks)
+    for step in range(total + 5):
+        if step < total:
+            start, first, second = chunks[step]
+            rows = pl.ds(start, first + second)
+            for other in along_z:
+                pltpu.make_async_remote_copy(
+                    src_ref=part_ref.at[rows],
+                    dst_ref=full_ref.at[z, x, y, rows, cols],
+                    send_sem=sends.at[0, step],
+                    recv_sem=recvs.at[0, step],
+                    device_id=other,
+                    device_id_type=MESH,
+                ).start()
+        if step == 0:
+            local.wait()
+        index = step - 1
+        if 0 <= index < total:
+            block = pieces(index)
+            arrived(block[0], 0, index)
+            send(block[1], over_y, 1, index)
+            send(block[2], over_x, 2, index)
+        index = step - 2
+        if 0 <= index < total:
+            block = pieces(index)
+            arrived(block[1], 1, index)
+            send(block[3], over_x, 3, index)
+            arrived(block[2], 2, index)
+            send(block[4], over_y, 4, index)
+        index = step - 3
+        if 0 <= index < total:
+            block = pieces(index)
+            arrived(block[3], 3, index)
+            arrived(block[4], 4, index)
+            send(block[5], sibling, 5, index)
+    for index in range(total):
+        block = pieces(index)
+        arrived(block[5], 5, index)
+        for stage in range(6):
+            sent(block[stage], stage, index)
+
+
+def gather_rows(part, shard_rows):
+    chunks = chunk_rows(part.shape[0], 8)
+    full = pl.pallas_call(
+        functools.partial(gather_kernel, chunks),
+        out_shape=jax.ShapeDtypeStruct((4, 2, 2, part.shape[0], 2 * part.shape[1]), part.dtype),
+        in_specs=[pl.BlockSpec(memory_space=pl.ANY)],
+        out_specs=pl.BlockSpec(memory_space=pl.ANY),
+        scratch_shapes=[
+            pltpu.SemaphoreType.DMA,
+            pltpu.SemaphoreType.DMA((6, len(chunks))),
+            pltpu.SemaphoreType.DMA((6, len(chunks))),
+        ],
+        compiler_params=pltpu.CompilerParams(collective_id=0, has_side_effects=True),
+        name="gather",
+    )(part)
+    return full.reshape(8 * shard_rows, 2 * part.shape[1])
+
+
+def reduce_kernel(
+    chunks,
+    grad_ref,
+    own_ref,
+    mine,
+    first_sum,
+    sum_a,
+    sum_b,
+    last_sum,
+    load_sems,
+    sends,
+    recvs,
+):
+    half_cols = mine.shape[-1]
+    y, c, z, x = place()
+    home_y, home_c = z % 2, z // 2
+    at_home = jnp.logical_and(home_y == y, home_c == c)
+    from_plane = 2 * c + y
+    my_cols = pl.ds(pl.multiple_of(c * half_cols, half_cols), half_cols)
+    other_cols = pl.ds(pl.multiple_of((1 - c) * half_cols, half_cols), half_cols)
+    over_x = device_at(y, c, z, 1 - x)
+    over_y = device_at(1 - y, c, z, x)
+    sibling = device_at(y, 1 - c, z, x)
+    barrier = pltpu.get_barrier_semaphore()
+    for other in (over_x, over_y, sibling):
+        pl.semaphore_signal(barrier, inc=1, device_id=other, device_id_type=MESH)
+    for other_y in range(2):
+        for other_c in range(2):
+            itself = jnp.logical_and(at_home, jnp.logical_and(y == other_y, c == other_c))
+
+            @pl.when(jnp.logical_not(itself))
+            def _():
+                pl.semaphore_signal(
+                    barrier,
+                    inc=1,
+                    device_id=device_at(other_y, other_c, from_plane, x),
+                    device_id_type=MESH,
+                )
+
+    def spans(index):
+        start, first, second = chunks[index]
+        start_a = sum(chunk[1] for chunk in chunks[:index])
+        start_b = sum(chunk[2] for chunk in chunks[:index])
+        return (
+            pl.ds(start, first + second),
+            pl.ds(start, first),
+            pl.ds(start + first, second),
+            pl.ds(start_a, first),
+            pl.ds(start_b, second),
+        )
+
+    def send(source, target, other, stage, index):
+        pltpu.make_async_remote_copy(
+            src_ref=source,
+            dst_ref=target,
+            send_sem=sends.at[stage, index],
+            recv_sem=recvs.at[stage, index],
+            device_id=other,
+            device_id_type=MESH,
+        ).start()
+
+    def arrived(piece, stage, index):
+        pltpu.make_async_copy(piece, piece, recvs.at[stage, index]).wait()
+
+    def sent(piece, stage, index):
+        pltpu.make_async_copy(piece, piece, sends.at[stage, index]).wait()
+
+    def load(index):
+        rows = spans(index)[0]
+        return pltpu.make_async_copy(
+            grad_ref.at[:, :, :, rows, my_cols],
+            mine.at[index % 2, :, :, :, pl.ds(0, rows.size)],
+            load_sems.at[index % 2],
+        )
+
+    def send_core(index):
+        rows = spans(index)[0]
+        send(
+            grad_ref.at[:, :, :, rows, other_cols],
+            first_sum.at[:, :, :, rows],
+            sibling,
+            0,
+            index,
+        )
+
+    def add(target, source):
+        summed = target[...].astype(jnp.float32) + source[...].astype(jnp.float32)
+        target[...] = summed.astype(target.dtype)
+
+    total = len(chunks)
+    load(0).start()
+    pl.semaphore_wait(barrier, 3 + jnp.where(at_home, 3, 4))
+    send_core(0)
+    send_core(1)
+    for step in range(total + 4):
+        index = step
+        if index < total:
+            if index + 1 < total:
+                load(index + 1).start()
+            if index + 2 < total:
+                send_core(index + 2)
+            rows, rows_a, rows_b, in_a, in_b = spans(index)
+            load(index).wait()
+            arrived(first_sum.at[:, :, :, rows], 0, index)
+
+            @pl.loop(0, 16)
+            def _(block):
+                zz, rest = block // 4, block % 4
+                add(
+                    first_sum.at[zz, rest // 2, rest % 2, rows],
+                    mine.at[index % 2, zz, rest // 2, rest % 2, pl.ds(0, rows.size)],
+                )
+
+            send(first_sum.at[:, 1 - x, :, rows_a], sum_a.at[:, :, in_a], over_x, 1, index)
+            send(first_sum.at[:, :, 1 - y, rows_b], sum_b.at[:, :, in_b], over_y, 2, index)
+        index = step - 1
+        if 0 <= index < total:
+            rows, rows_a, rows_b, in_a, in_b = spans(index)
+            arrived(sum_a.at[:, :, in_a], 1, index)
+
+            @pl.loop(0, 8)
+            def _(block):
+                add(
+                    sum_a.at[block // 2, block % 2, in_a],
+                    first_sum.at[block // 2, x, block % 2, rows_a],
+                )
+
+            send(sum_a.at[:, 1 - y, in_a], last_sum.at[:, rows_a], over_y, 3, index)
+            arrived(sum_b.at[:, :, in_b], 2, index)
+
+            @pl.loop(0, 8)
+            def _(block):
+                add(
+                    sum_b.at[block // 2, block % 2, in_b],
+                    first_sum.at[block // 2, block % 2, y, rows_b],
+                )
+
+            send(sum_b.at[:, 1 - x, in_b], last_sum.at[:, rows_b], over_x, 4, index)
+        index = step - 2
+        if 0 <= index < total:
+            rows, rows_a, rows_b, in_a, in_b = spans(index)
+            arrived(last_sum.at[:, rows_a], 3, index)
+            arrived(last_sum.at[:, rows_b], 4, index)
+
+            @pl.loop(0, 4)
+            def _(block):
+                add(last_sum.at[block, rows_a], sum_a.at[block, y, in_a])
+                add(last_sum.at[block, rows_b], sum_b.at[block, x, in_b])
+
+            for to_z in range(4):
+                itself = jnp.logical_and(at_home, z == to_z)
+                source = last_sum.at[to_z, rows]
+                target = own_ref.at[y, rows, my_cols]
+
+                @pl.when(jnp.logical_not(itself))
+                def _():
+                    send(source, target, device_at(home_y, home_c, to_z, x), 5, index)
+
+                @pl.when(itself)
+                def _():
+                    pltpu.make_async_copy(source, target, recvs.at[5, index]).start()
+
+    for index in range(total):
+        rows, rows_a, rows_b, in_a, in_b = spans(index)
+        arrived(own_ref.at[:, rows], 5, index)
+        sent(first_sum.at[:, :, :, rows], 0, index)
+        sent(sum_a.at[:, :, in_a], 1, index)
+        sent(sum_b.at[:, :, in_b], 2, index)
+        sent(last_sum.at[:, rows_a], 3, index)
+        sent(last_sum.at[:, rows_b], 4, index)
+
+        @pl.when(at_home)
+        def _():
+            sent(last_sum.at[pl.ds(0, 3), rows], 5, index)
+
+        @pl.when(jnp.logical_not(at_home))
+        def _():
+            sent(last_sum.at[:, rows], 5, index)
+
+
+def reduce_chunks(total, count, share):
+    units = total // 16
+    chunks = []
+    start = 0
+    for index in range(count):
+        size = units * (index + 1) // count - units * index // count
+        first = int(round(size * share))
+        chunks.append((start * 16, first * 16, (size - first) * 16))
+        start += size
+    return chunks
+
+
+def sum_on_plane(grad_rows):
+    half_rows, width = grad_rows.shape[0] // 16, grad_rows.shape[1]
+    chunks = reduce_chunks(half_rows, 8, 0.75)
+    most = max(first + second for _, first, second in chunks)
+    half_cols = width // 2
+    dtype = grad_rows.dtype
+    own = pl.pallas_call(
+        functools.partial(reduce_kernel, chunks),
+        out_shape=jax.ShapeDtypeStruct((2, half_rows, width), dtype),
+        in_specs=[pl.BlockSpec(memory_space=pl.ANY)],
+        out_specs=pl.BlockSpec(memory_space=pl.ANY),
+        scratch_shapes=[
+            pltpu.VMEM((2, 4, 2, 2, most, half_cols), dtype),
+            pltpu.VMEM((4, 2, 2, half_rows, half_cols), dtype),
+            pltpu.VMEM((4, 2, sum(chunk[1] for chunk in chunks), half_cols), dtype),
+            pltpu.VMEM((4, 2, sum(chunk[2] for chunk in chunks), half_cols), dtype),
+            pltpu.VMEM((4, half_rows, half_cols), dtype),
+            pltpu.SemaphoreType.DMA((2,)),
+            pltpu.SemaphoreType.DMA((6, len(chunks))),
+            pltpu.SemaphoreType.DMA((6, len(chunks))),
+        ],
+        compiler_params=pltpu.CompilerParams(
+            collective_id=1, has_side_effects=True, vmem_limit_bytes=56 * 2**20
+        ),
+        name="reduce",
+    )(grad_rows.reshape(4, 2, 2, half_rows, width))
+    return own.reshape(2 * half_rows, width)
+
+
+def to_planes(values):
+    pairs = []
+    for source in range(32):
+        y, c, z, x = source // 16, source // 8 % 2, source // 2 % 4, source % 2
+        pairs.append((source, (z % 2 * 2 + z // 2) * 8 + (2 * c + y) * 2 + x))
+    return lax.ppermute(values, ("group", "dp"), pairs)
+
+
 def fetch_weights(params):
-    return lax.all_gather(params.astype(jnp.bfloat16), "dp", axis=0, tiled=True)
+    if not on_grid():
+        return lax.all_gather(params.astype(jnp.bfloat16), "dp", axis=0, tiled=True)
+    y, c, _, _ = place()
+    rows, width = params.shape
+    part = lax.dynamic_slice(params, (y * (rows // 2), c * (width // 2)), (rows // 2, width // 2))
+    return gather_rows(part.astype(jnp.bfloat16), rows)
 
 
 def reduce_rows(grad_rows):
-    return lax.psum_scatter(
-        grad_rows.astype(jnp.bfloat16), "dp", scatter_dimension=0, tiled=True
-    ).astype(jnp.float32)
+    if on_grid():
+        shard = sum_on_plane(grad_rows)
+    else:
+        shard = lax.psum_scatter(grad_rows, "dp", scatter_dimension=0, tiled=True)
+    ranks, rank = lax.axis_size("dp"), lax.axis_index("dp")
+    count = shard.shape[0]
+    following = lax.ppermute(shard[:16], "dp", [(source, source - 1) for source in range(1, ranks)])
+    shifted = jnp.concatenate([shard[SPARE:], following[:SPARE]], axis=0)
+    flat_row = rank * count + jnp.arange(count)
+    return jnp.where((flat_row < layout_rows()[1])[:, None], shard, shifted).astype(jnp.float32)
 
 
 def adam_update(params, moment_one, moment_two, clipped, step_number):
@@ -249,12 +636,13 @@
 
 def post_rows_local(reduced):
     head_start = layout_rows()[4]
-    local_rows = reduced.shape[0]
-    row_start = lax.axis_index("dp") * local_rows
-    wanted = head_start - 2 + jnp.arange(2)
-    picker = (row_start + jnp.arange(local_rows)[None, :] == wanted[:, None]).astype(jnp.float32)
-    return jnp.dot(
-        picker, reduced, precision=lax.Precision.HIGHEST, preferred_element_type=jnp.float32
+    rank, count = lax.axis_index("dp"), reduced.shape[0]
+    return jnp.concatenate(
+        [
+            jnp.where(rank == row // count, reduced[row % count : row % count + 1], 0.0)
+            for row in (head_start - 2, head_start - 1)
+        ],
+        axis=0,
     )
 
 
@@ -276,26 +664,36 @@
     moment_two = second_moment[0]
     norm_list, loss_list, count_list, post_list = ([], [], [], [])
     weights = fetch_weights(params)
-    grad_total = None
-    loss_total = jnp.zeros((), jnp.float32)
-    for micro_index in range(MICRO):
-        loss_part, grad_rows = micro_step(
-            weights,
-            pixels[0, micro_index],
-            counts[0, micro_index, 0],
-            labels[0, micro_index],
-            text,
-            True,
-        )
-        loss_total = loss_total + loss_part
-        grad_total = grad_rows if micro_index == 0 else grad_total + grad_rows
+    slots = pixels.shape[2]
+    step_pixels, step_counts, step_labels = pixels[0], counts[0], labels[0]
+    group, worker = lax.axis_index("group"), lax.axis_index("group")
+    if on_grid():
+        step_pixels = to_planes(step_pixels)
+        step_counts, step_labels = to_planes(step_counts), to_planes(step_labels)
+        plane = place()[2]
+        worker = plane % 2 * 2 + plane // 2
+    live = (jnp.arange(slots)[None, :] < step_counts).astype(jnp.float32).reshape(-1)
+    loss_total, grad_total = micro_step(
+        weights,
+        step_pixels.reshape((-1,) + pixels.shape[3:]),
+        live,
+        step_labels.reshape(-1),
+        text,
+        True,
+    )
     reduced = reduce_rows(grad_total)
     image_total = jnp.sum(counts[0]).astype(jnp.float32)
     squares = jnp.sum(reduced * reduced)
     post_local = post_rows_local(reduced)
-    loss_all, count_all, square_all, post_all = lax.psum(
-        (loss_total, image_total, squares, post_local), "dp"
-    )
+    groups = lax.axis_size("group")
+    at_worker = (jnp.arange(groups) == worker).astype(jnp.float32)
+    at_group = (jnp.arange(groups) == group).astype(jnp.float32)
+    figures = jnp.stack([at_group * image_total, at_group * squares, at_worker * loss_total])
+    figures, posts = lax.psum(
+        (figures, jnp.where(at_group[:, None, None] > 0, post_local[None], 0.0)), ("group", "dp")
+    )
+    count_all, square_all, loss_all = [jnp.sum(row * at_group) for row in figures]
+    post_all = lax.dynamic_index_in_dim(posts, group, keepdims=False)
     gradient = reduced / count_all
     grad_norm = jnp.sqrt(square_all) / count_all
     clip_factor = CLIP_MAX / jnp.maximum(grad_norm, CLIP_MAX)
@@ -306,12 +704,12 @@
     count_list.append(count_all)
     post_list.append(post_all / count_all * clip_factor)
     delta = master - params
-    groups = lax.axis_size("group")
     mean_delta = lax.psum(delta.astype(jnp.bfloat16), "group").astype(jnp.float32) / groups
     new_master, new_outer = nesterov(master, outer_momentum, mean_delta)
-    soup_rows = lax.all_gather(new_master.astype(jnp.bfloat16), "dp", axis=0, tiled=True)
+    soup_rows = fetch_weights(new_master)
+    eval_live = (jnp.arange(eval_pixels.shape[0]) < eval_counts[0]).astype(jnp.float32)
     eval_losses, unused_grads = micro_step(
-        soup_rows, eval_pixels, eval_counts[0], eval_labels, text, False
+        soup_rows, eval_pixels, eval_live, eval_labels, text, False
     )
     return (
         new_master,

time: 2930 us -> 1340 us (0.46)
  waiting for transfers between devices: 1850 us -> 69.1 us
  Pallas kernels: 0 us -> 611 us
  local copies, waits for them, and re-layouts: 551 us -> 256 us
  matrix products: 279 us -> 185 us
  other arithmetic: 191 us -> 121 us
    all_gather x2 -> x0, waiting for transfers between devices: 1260 us -> none  [the longest x1 644 us: fetch_weights(): return lax.all_gather(params.astype(jnp.bfloat16), 'dp', axis=0, tiled=True)]
    pallas_call x0 -> x3, Pallas kernels: none -> 611 us  [the longest x2 423 us: gather_rows(): pl.pallas_call(functools.partial(gather_kernel, chunks), out_shape=jax.Sh...]
    unnamed x5 -> x1, waiting for transfers between devices: 512 us -> 0.02 us
    unnamed x518 -> x276, local copies, waits for them, and re-layouts: 155 us -> 18.6 us
    dot_general x99 -> x56, matrix products: 279 us -> 185 us  [product(): jnp.einsum(pattern, first_arg, second_arg, preferred_element_type=jnp.flo...]
    concatenate x2 -> x4, local copies, waits for them, and re-layouts: 189 us -> 117 us  [the longest x2 112 us: micro_step(): jnp.concatenate([piece.astype(jnp.bfloat16) for piece in [grad_patch_w, t...]
    convert_element_type x5 -> x4, other arithmetic: 76.1 us -> 24.9 us  [the longest x1 16.8 us: per_device(): delta.astype(jnp.bfloat16)]
    reshape x4 -> x0, local copies, waits for them, and re-layouts: 32.2 us -> none  [layer_backward(): grad_w_qkv = product('btd,btje->jde', normed, grad_qkv).reshape(3 * D, D)]
  transfers between devices with their start and end apart: 4 -> 5, of which waited for: 4 -> 2; matrix products, arithmetic and copies ran while one was open for 3% -> 3% of each run, Pallas kernels for 0% -> 18%
where the time goes in v1:
time: 1340 us; the launch traced here: 1320 us
  Pallas kernels  611 us (46%)
  local copies, waits for them, and re-layouts  256 us (19%)
  matrix products  185 us (14%)
  other arithmetic  121 us (9%)
  waiting for transfers between devices  69.1 us (5%)
  blocking collectives  43.6 us (3%)
  between operations  20.1 us (2%)
    pallas_call x2, Pallas kernels, gather_rows(): pl.pallas_call(functools.partial(gather_kernel, chunks), out_shape=jax.Sh...  423 us
    pallas_call x1, Pallas kernels, sum_on_plane(): pl.pallas_call(functools.partial(reduce_kernel, chunks), out_shape=jax.Sh...  188 us
    dot_general x56, matrix products, product(): jnp.einsum(pattern, first_arg, second_arg, preferred_element_type=jnp.flo...  185 us
    concatenate x2, local copies, waits for them, and re-layouts, micro_step(): jnp.concatenate([piece.astype(jnp.bfloat16) for piece in [grad_patch_w, t...  112 us
    psum x1, waiting for transfers between devices, per_device(): lax.psum(delta.astype(jnp.bfloat16), 'group').astype(jnp.float32) / groups  66.9 us
    psum x1, blocking collectives, per_device(): lax.psum((figures, jnp.where(at_group[:, None, None] > 0, post_local[None...  43.6 us
    another operation x14, local copies, waits for them, and re-layouts, layer_backward(): grad_qkv = jnp.stack([grad_query, grad_key, grad_value], axis=2)  28.8 us
  transfers between devices with their start and end apart: 5, of which 2 were waited for; matrix products, arithmetic and copies ran while one was open for 3% of the time, Pallas kernels for 18%

profile of v1, /device:TPU:25, one launch (start us, length us, event | category | flops | bytes accessed | tf_op | source)
XLA Modules:
  0.0 1317.3 jit_solution(4722717233074295685)
XLA Ops:
  20.7 235.4 %gather.2 = bf16[4,2,2,1392,768]{4,3,2,1,0:T(8,128)(2,1)} custom-call(bf16[1392,384]{1,0:T(8,128)(2,1)} %dynamic_slice.17.part_ref), custom_call_target="tpu_custom_call" | custom-call | tf_op jit(solution)/shard_map/gather/pallas_call | solution.py:356
  260.5 7.7 fusion.180
  283.6 7.0 reshape.752
  314.3 8.8 fusion.186
  332.9 6.7 reshape.753
  363.3 7.6 fusion.29
  377.4 6.5 fusion.12
  383.9 6.5 fusion.191
  446.5 8.8 fusion.16
  455.3 6.4 fusion.189
  557.0 5.8 copy.514
  571.7 67.1 %concatenate.48 = bf16[22272,768]{0,1:T(8,128)(2,1)} concatenate(bf16[3072,768]{0,1:T(8,128)(2,1)} %fusion.23, bf16[1,768]{0,1:T(8,128)(2,1)S(1)} %broadcast_in_dim.177, bf16[50,768]{0,1:T(8,128)(2,1)S(1)} %copy.512, bf16[13,768]{0,1:T(8,128)(2,1)} %broadcast_in_dim.168, bf16[2304,768]{0,1:T(8,128)(2,1)} %copy.513, bf16[768,768]{0,1:T(8,128)(2,1)} %bitcast_convert_fusion.8, ...), dimensions={0} | concatenate | bytes 68419584 | tf_op jit(solution)/shard_map/concatenate | solution.py:231
  638.8 44.5 %copy.527 = bf16[22272,768]{1,0:T(8,128)(2,1)} copy(bf16[22272,768]{0,1:T(8,128)(2,1)} %concatenate.48) | data formatting | bytes 68419584 | tf_op jit(solution)/shard_map/concatenate | solution.py:231
  683.3 187.7 %reduce.62 = bf16[2,1392,768]{2,1,0:T(8,128)(2,1)} custom-call(bf16[4,2,2,1392,768]{4,3,2,1,0:T(8,128)(2,1)} %bitcast.359), custom_call_target="tpu_custom_call" | custom-call | tf_op jit(solution)/shard_map/reduce/pallas_call | solution.py:570
  884.6 7.9 select_convert_fusion
  897.1 43.6 %all-reduce.1 = (f32[3,4]{1,0:T(4,128)S(1)}, f32[4,2,768]{2,1,0:T(2,128)S(1)}) all-reduce(f32[3,4]{1,0:T(4,128)S(1)} %pad_maximum_fusion.2, f32[4,2,768]{2,1,0:T(2,128)S(1)} %broadcast_select_fusion), channel_id=1, replica_groups=mesh['group'=4,'dp'=8] {'group','dp'}, use_global_device_ids=true, to_apply=%region_52.53 | all-reduce | flops 6156 | bytes 49248 | tf_op jit(solution)/shard_map/psum | solution.py:692
  942.7 16.8 %fusion.6 = bf16[2784,768]{1,0:T(8,128)(2,1)} fusion(f32[2784,768]{1,0:T(8,128)} %param.15, f32[2784,768]{1,0:T(8,128)} %copy-done.7, f32[1,2784,768]{2,1,0:T(8,128)} %param.18, f32[1,2784,768]{2,1,0:T(8,128)} %param.17, f32[]{:T(128)S(6)} %div.292, f32[]{:T(128)} %get-tuple-element.52), kind=kLoop, calls=%fused_computation.14 | loop fusion | flops 40624128 | bytes 38486024 | tf_op jit(solution)/shard_map/convert_element_type | solution.py:707
  961.5 20.3 %fusion.7 = (f32[1,2784,768]{2,1,0:T(8,128)}, f32[1,2784,768]{2,1,0:T(8,128)}) fusion(f32[1,2784,768]{2,1,0:T(8,128)} %param.18, f32[]{:T(128)S(6)} %div.292, f32[]{:T(128)} %get-tuple-element.52, bf16[1,13,768]{2,1,0:T(8,128)(2,1)S(1)} %get-tuple-element.96, bf16[1,2771,768]{2,1,0:T(8,128)(2,1)} %get-tuple-element.88, pred[2784]{0:T(1024)(128)(4,1)S(1)} %copy-done.100, ...), kind=kLoop, calls=%fused_computation.15 | loop fusion | flops 32071680 | bytes 42765032 | tf_op jit(solution)/shard_map/add | solution.py:625
  981.8 66.9 %all-reduce.4.cloned.1.call-done = bf16[2784,768]{1,0:T(8,128)(2,1)} async-done(((bf16[2784,768]{1,0:T(8,128)(2,1)}), bf16[2784,768]{1,0:T(8,128)(2,1)}) %all-reduce.4.cloned.1.call-update) | async-done | bytes 4276240 | tf_op jit(solution)/shard_map/psum | solution.py:707
  1048.7 12.1 multiply_subtract_fusion
  1065.3 188.0 %gather.3 = bf16[4,2,2,1392,768]{4,3,2,1,0:T(8,128)(2,1)} custom-call(bf16[1392,384]{1,0:T(8,128)(2,1)} %dynamic_slice.16.part_ref), custom_call_target="tpu_custom_call" | custom-call | tf_op jit(solution)/shard_map/gather/pallas_call | solution.py:356
  1253.3 6.6 fusion.179
  1278.1 7.6 fusion.194
  1298.4 7.3 fusion.17
  (539 shorter events, 313.4 us)
Async XLA Ops:
  7.2 1254.6 %copy-start = (bf16[4,49,3072]{2,0,1:T(4,128)(2,1)S(1)}, bf16[4,49,3072]{2,0,1:T(4,128)(2,1)}, u32[]{:S(2)}) copy-start(bf16[4,49,3072]{2,0,1:T(4,128)(2,1)} %param.19) | copy-start | bytes 3612676
  7.2 1041.5 %all-reduce.4.cloned.1.call-start = ((), (), s32[]{:S(2)}) async-start(), calls=%async_computation | async-start | bytes 8552448 | tf_op jit(solution)/shard_map/psum | solution.py:707
  7.2 262.2 %collective-permute-start = (bf16[2,4,49,3072]{3,1,2,0:T(4,128)(2,1)}, bf16[2,4,49,3072]{3,1,2,0:T(4,128)(2,1)}, u32[]{:S(2)}, u32[]{:S(2)}) collective-permute-start(bf16[2,4,49,3072]{3,1,2,0:T(4,128)(2,1)} %bitcast.403), channel_id=1, source_target_pairs={{0,0},{1,1},{2,16},{3,17},{4,8},{5,9},{6,24},{7,25},{8,4},{9,5},{1... | collective-permute-start | bytes 7225352 | tf_op jit(solution)/shard_map/ppermute | solution.py:598
  10.4 257.8 %collective-permute-start.2 = (s32[2,1]{0,1:T(1,128)}, s32[2,1]{0,1:T(1,128)S(1)}, u32[]{:S(2)}, u32[]{:S(2)}) collective-permute-start(s32[2,1]{0,1:T(1,128)} %bitcast.405), channel_id=1, source_target_pairs={{0,0},{1,1},{2,16},{3,17},{4,8},{5,9},{6,24},{7,25},{8,4},{9,5},{1... | collective-permute-start | bytes 32 | tf_op jit(solution)/shard_map/ppermute | solution.py:598
  13.6 255.3 %collective-permute-start.1 = (s32[2,4]{1,0:T(2,128)}, s32[2,4]{1,0:T(2,128)S(1)}, u32[]{:S(2)}, u32[]{:S(2)}) collective-permute-start(s32[2,4]{1,0:T(2,128)} %bitcast.404), channel_id=1, source_target_pairs={{0,0},{1,1},{2,16},{3,17},{4,8},{5,9},{6,24},{7,25},{8,4},{9,5},{1... | collective-permute-start | bytes 104 | tf_op jit(solution)/shard_map/ppermute | solution.py:598
  259.8 19.9 %copy-start.86 = (f32[768]{0:T(1024)}, f32[768]{0:T(1024)S(1)}, u32[]{:S(2)}) copy-start(f32[768]{0:T(1024)S(1)} %get-tuple-element.46) | copy-start | bytes 9220
  259.8 19.9 %copy-start.111 = (f32[768]{0:T(1024)}, f32[768]{0:T(1024)S(1)}, u32[]{:S(2)}) copy-start(f32[768]{0:T(1024)S(1)} %get-tuple-element.45) | copy-start | bytes 9220
  259.8 41.9 %copy-start.74 = (f32[768]{0:T(1024)}, f32[768]{0:T(1024)S(1)}, u32[]{:S(2)}) copy-start(f32[768]{0:T(1024)S(1)} %get-tuple-element.48) | copy-start | bytes 9220
  259.8 41.9 %copy-start.76 = (f32[768]{0:T(1024)}, f32[768]{0:T(1024)S(1)}, u32[]{:S(2)}) copy-start(f32[768]{0:T(1024)S(1)} %get-tuple-element.47) | copy-start | bytes 9220
  259.8 47.7 %copy-start.78 = (f32[768]{0:T(1024)}, f32[768]{0:T(1024)S(1)}, u32[]{:S(2)}) copy-start(f32[768]{0:T(1024)S(1)} %get-tuple-element.44) | copy-start | bytes 9220
  259.8 65.8 %copy-start.82 = (f32[768]{0:T(1024)}, f32[768]{0:T(1024)S(1)}, u32[]{:S(2)}) copy-start(f32[768]{0:T(1024)S(1)} %get-tuple-element.42) | copy-start | bytes 9220
  259.9 111.5 %copy-start.102 = (f32[768]{0:T(1024)}, f32[768]{0:T(1024)S(1)}, u32[]{:S(2)}) copy-start(f32[768]{0:T(1024)S(1)} %get-tuple-element.38) | copy-start | bytes 9220
  259.9 117.1 %copy-start.92 = (f32[768]{0:T(1024)}, f32[768]{0:T(1024)S(1)}, u32[]{:S(2)}) copy-start(f32[768]{0:T(1024)S(1)} %get-tuple-element.37) | copy-start | bytes 9220
  277.9 23.8 %copy-start.68 = (f32[8,50]{1,0:T(8,128)}, f32[8,50]{1,0:T(8,128)S(1)}, u32[]{:S(2)}) copy-start(f32[8,50]{1,0:T(8,128)S(1)} %broadcast_multiply_fusion.4) | copy-start | bytes 4804
  278.4 23.4 %copy-start.72 = (f32[8,50]{1,0:T(8,128)}, f32[8,50]{1,0:T(8,128)S(1)}, u32[]{:S(2)}) copy-start(f32[8,50]{1,0:T(8,128)S(1)} %fusion.140) | copy-start | bytes 4804
  363.3 14.1 %copy-start.125 = (f32[8,50,3072]{2,1,0:T(8,128)}, f32[8,50,3072]{2,1,0:T(8,128)S(1)}, u32[]{:S(2)}) copy-start(f32[8,50,3072]{2,1,0:T(8,128)S(1)} %fusion.28) | copy-start | bytes 14745604
  520.0 11.0 slice-start.2
  535.5 10.2 slice-start.4
  557.0 9.8 copy-start.116
  557.0 10.6 copy-start.104
  871.1 13.5 %slice-start = ((s8[4276224]{0:T(1024)(128)(4,1)}), s8[4194304]{0:T(1024)(128)(4,1)S(1)}, s32[]{:S(2)}) async-start(s8[4276224]{0:T(1024)(128)(4,1)} %bitcast.363), calls=%async_computation.1 | async-start | bytes 8388608
  872.0 12.6 slice-start.1
  872.0 12.6 copy-start.100
  878.5 6.0 collective-permute-start.3
  (117 other events, 454.2 us)
Sparse Core Ops, SparseCore 0:
  959.7 88.9 all-reduce.3

commit v2 on v1

v2 whole, which is shorter than its diff:
```python
import functools

import jax
import jax.numpy as jnp
from jax import lax
from jax.experimental import pallas as pl
from jax.experimental.pallas import tpu as pltpu
from jax.sharding import PartitionSpec as P

MESH = pl.DeviceIdType.MESH

D = 768
HEADS = 12
HEAD = 64
FF = 3072
PATCH_IN = 3072
EMB = 512
CLASSES = 1000
LAYERS = 2
MICRO = 2
STEP = 10
SEQ = 50
ROWS_RAW = 22079


LN_EPS = 1e-05
NORM_EPS = 1e-06
LOGIT_SCALE = 50.0
SMOOTH = 0.1
CLIP_MAX = 0.02
BETA_ONE = 0.9
BETA_TWO = 0.98
ADAM_EPS = 1e-08
RATE = 0.02
DECAY = 0.1
OUTER_RATE = 0.7
OUTER_MOM = 0.9
GELU_SLOPE = 1.702
SPARE = 13


def layout_rows():
    table_start = PATCH_IN
    layer_start = table_start + SEQ + 1
    block_size = 4 * D + 2 * FF
    norm_start = layer_start + LAYERS * block_size
    head_start = norm_start + 4 * LAYERS + 4
    return (table_start, layer_start, block_size, norm_start, head_start)


TOKENS = 56
CLASS_AT = 49
PAIR = 2 * TOKENS
BLOCK = 3072
TAIL_START = BLOCK + SEQ + 1 + SPARE + LAYERS * (4 * D + 2 * FF)
TAIL_ROWS = 544
HEAD_AT = 4 * LAYERS + 4
TABLE_ROWS = SEQ + 1 + SPARE
LOW_COLS = 2 * FF
FIRST_LAYER = BLOCK + TABLE_ROWS
DENSE_END = FIRST_LAYER + 4 * D + 2 * FF + 3 * D


def dot(first, second, first_dim=1, second_dim=0):
    return lax.dot_general(
        first,
        second,
        (((first_dim,), (second_dim,)), ((), ())),
        preferred_element_type=jnp.float32,
    )


def low(values):
    return values.astype(jnp.bfloat16)


def norm_parts(values):
    centred = values - jnp.mean(values, -1, keepdims=True)
    scale = lax.rsqrt(jnp.mean(centred * centred, -1, keepdims=True) + LN_EPS)
    return (centred * scale, scale)


def norm_back(values, gain, grad):
    unit, scale = norm_parts(values)
    weighted = grad * gain
    mean_one = jnp.mean(weighted, -1, keepdims=True)
    mean_two = jnp.mean(weighted * unit, -1, keepdims=True)
    return (scale * (weighted - mean_one - unit * mean_two), grad * unit)


def wide(values, rows):
    return jnp.concatenate(
        [values, jnp.zeros((rows - values.shape[0], values.shape[1]), values.dtype)], axis=0
    )


def head_mask(rows, lanes, first_head):
    row = lax.broadcasted_iota(jnp.int32, (rows, lanes), 0)
    lane = lax.broadcasted_iota(jnp.int32, (rows, lanes), 1)
    return (lane // HEAD + first_head) == row


def lane_pick(values, head):
    lane = lax.broadcasted_iota(jnp.int32, values.shape, 1)
    return jnp.where(lane // HEAD == head, values, jnp.zeros_like(values))


def stack_heads(values):
    return jnp.concatenate([lane_pick(values, head) for head in range(4)], axis=0)


def fold_heads(values):
    rows = values.shape[0] // 4
    total = lane_pick(values[:rows], 0)
    for head in range(1, 4):
        total = total + lane_pick(values[head * rows : (head + 1) * rows], head)
    return total


def soft(scores):
    scores = scores - jnp.max(scores, -1, keepdims=True)
    grown = jnp.exp(scores)
    return grown / jnp.sum(grown, -1, keepdims=True)


def pair_bias():
    row = lax.broadcasted_iota(jnp.int32, (PAIR, PAIR), 0)
    col = lax.broadcasted_iota(jnp.int32, (PAIR, PAIR), 1)
    fits = (row // TOKENS == col // TOKENS) & (col % TOKENS < SEQ)
    return jnp.where(fits, 0.0, -1e30)


def class_bias():
    row = lax.broadcasted_iota(jnp.int32, (32, PAIR), 0)
    col = lax.broadcasted_iota(jnp.int32, (32, PAIR), 1)
    fits = (row // 16 == col // TOKENS) & (col % TOKENS < SEQ)
    return jnp.where(fits, 0.0, -1e30)


def spread_heads(values):
    keep = head_mask(16, D, 0)
    rows = jnp.broadcast_to(values[:, None, :], (8, 16, D))
    return jnp.where(keep[None], rows, 0.0).reshape(128, D)


def unspread_heads(values):
    keep = head_mask(16, D, 0)
    return jnp.sum(jnp.where(keep[None], values.reshape(8, 16, D), 0.0), axis=1)


def tower_kernel(images, with_grads, *refs):
    rows_all = images * TOKENS
    pairs = images // 2
    (w_hbm, pix_hbm, text_ref, label_ref, live_ref), refs = refs[:5], refs[5:]
    if with_grads:
        (g_hbm, factor_ref, extra_ref), refs = refs[:3], refs[3:]
    else:
        (loss_ref,), refs = refs[:1], refs[1:]
    (wbuf, tail, table, pix, emb, hid0, mid0, hid1, acc, qkv, norm_a, norm_b, mixed, pre, act), refs = (
        refs[:15],
        refs[15:],
    )
    (norm_c, kv), refs = refs[:2], refs[2:]
    if with_grads:
        (dhid, dqkv, gb, dmix, stage, stage_sem), refs = refs[:6], refs[6:]
    (wsem, small_sem) = refs

    layer_at = [FIRST_LAYER + index * (4 * D + 2 * FF) for index in range(LAYERS)]
    order = [0]
    for start in layer_at:
        order += [start, start + 4 * D, start + 4 * D + FF]
    if with_grads:
        order += [layer_at[0] + 4 * D + FF, layer_at[0] + 4 * D, layer_at[0]]
    slot_of = [0, 1, 2, 0, 1, 2, 0, 0, 2, 1]

    def fetch(index):
        return pltpu.make_async_copy(
            w_hbm.at[pl.ds(order[index], BLOCK)], wbuf.at[slot_of[index]], wsem.at[slot_of[index]]
        )

    load_pix = pltpu.make_async_copy(pix_hbm, pix, small_sem.at[0])
    load_tail = pltpu.make_async_copy(
        w_hbm.at[pl.ds(TAIL_START, TAIL_ROWS)], tail, small_sem.at[1]
    )
    load_table = pltpu.make_async_copy(w_hbm.at[pl.ds(BLOCK, TABLE_ROWS)], table, small_sem.at[2])
    fetch(0).start()
    load_pix.start()
    load_table.start()
    load_tail.start()
    fetch(1).start()
    fetch(2).start()

    def chunks_of(count=rows_all // PAIR):
        return pl.loop(0, count)

    def rows_at(index):
        return pl.ds(pl.multiple_of(index * PAIR, PAIR), PAIR)

    def norm_row(index):
        return tail[0:16, :].astype(jnp.float32)[index : index + 1]

    def class_rows(ref):
        picked = [ref[TOKENS * i + CLASS_AT : TOKENS * i + CLASS_AT + 1, :] for i in range(images)]
        if images < 8:
            picked.append(jnp.zeros((8 - images, ref.shape[1]), ref.dtype))
        return jnp.concatenate(picked, axis=0)

    def add_class_rows(ref, values):
        for i in range(images):
            at = slice(TOKENS * i + CLASS_AT, TOKENS * i + CLASS_AT + 1)
            ref[at, :] = ref[at, :] + values[i : i + 1]

    def layer_norm_into(source, target, gain_row):
        gain, bias = norm_row(gain_row), norm_row(gain_row + 1)

        @chunks_of()
        def _(index):
            rows = rows_at(index)
            unit, _ = norm_parts(source[rows, :])
            target[rows, :] = (unit * gain + bias).astype(target.dtype)

    load_table.wait()
    load_tail.wait()
    load_pix.wait()
    fetch(0).wait()
    emb[...] = dot(pix[...], wbuf[0])
    fetch(3).start()
    rows_table = table[...].astype(jnp.float32)
    added = pltpu.roll(rows_table, TABLE_ROWS - 2, 0)[:TOKENS]
    token = lax.broadcasted_iota(jnp.int32, (TOKENS, D), 0)
    added = jnp.where(token == CLASS_AT, rows_table[0:1] + rows_table[1:2], added)
    added = jnp.where(token < SEQ, added, 0.0)

    gain, bias = norm_row(0), norm_row(1)

    @chunks_of()
    def _(index):
        rows = rows_at(index)
        values = emb[rows, :] + jnp.concatenate([added, added], axis=0)
        emb[rows, :] = values
        unit, _ = norm_parts(values)
        hid0[rows, :] = unit * gain + bias

    layer_norm_into(hid0, norm_a, 2)
    fetch(1).wait()

    @pl.loop(0, 3)
    def _(part):
        at = pl.ds(pl.multiple_of(part * D, D), D)
        qkv[:, at] = low(dot(norm_a[...], wbuf[1, at, :]))

    bias_pair = pair_bias()

    def lanes(part, group):
        return slice(part * D + group * 256, part * D + (group + 1) * 256)

    def pair_soft(queries, keys):
        scores = dot(queries, keys, 1, 1) * HEAD ** (-0.5)
        scores = scores.reshape(4, PAIR, PAIR) + bias_pair[None]
        return soft(scores).reshape(4 * PAIR, PAIR)

    @pl.loop(0, pairs)
    def _(index):
        rows = rows_at(index)
        for group in range(3):
            queries = stack_heads(qkv[rows, lanes(0, group)])
            probs = low(pair_soft(queries, qkv[rows, lanes(1, group)]))
            out = dot(probs, qkv[rows, lanes(2, group)])
            mixed[rows, lanes(0, group)] = low(fold_heads(out))

    acc[...] = dot(mixed[...], wbuf[1, 3 * D : 4 * D, :])
    fetch(4).start()
    gain2, bias2 = norm_row(4), norm_row(5)

    @chunks_of()
    def _(index):
        rows = rows_at(index)
        values = hid0[rows, :] + acc[rows, :]
        mid0[rows, :] = values
        unit, _ = norm_parts(values)
        norm_b[rows, :] = low(unit * gain2 + bias2)

    fetch(2).wait()

    @pl.loop(0, 3)
    def _(part):
        at = pl.ds(pl.multiple_of(part * 1024, 1024), 1024)
        values = dot(norm_b[...], wbuf[2, at, :], 1, 1)
        if with_grads:
            pre[:, at] = low(values)
        act[:, at] = low(values * jax.nn.sigmoid(GELU_SLOPE * values))

    fetch(5).start()
    fetch(3).wait()
    acc[...] = dot(act[...], wbuf[0])
    fetch(6).start()
    gain3, bias3 = norm_row(6), norm_row(7)

    @chunks_of()
    def _(index):
        rows = rows_at(index)
        values = mid0[rows, :] + acc[rows, :]
        hid1[rows, :] = values
        unit, _ = norm_parts(values)
        norm_c[rows, :] = low(unit * gain3 + bias3)

    fetch(4).wait()

    @pl.loop(0, 2)
    def _(part):
        kv[:, pl.ds(pl.multiple_of(part * D, D), D)] = low(
            dot(norm_c[...], wbuf[1, pl.ds(pl.multiple_of(part * D + D, D), D), :])
        )

    class_hid = class_rows(hid1)
    unit_one, _ = norm_parts(class_hid)
    class_a = low(wide(unit_one * gain3 + bias3, 16))
    class_q = low(dot(class_a, wbuf[1, 0:D, :]))
    spread_q = low(spread_heads(class_q[:8].astype(jnp.float32)))
    bias_class = class_bias()
    class_probs, outs = [], []
    for pair in range(pairs):
        rows = slice(pair * PAIR, (pair + 1) * PAIR)
        scores = dot(spread_q[32 * pair : 32 * pair + 32], kv[rows, 0:D], 1, 1)
        probs = soft(scores * HEAD ** (-0.5) + bias_class)
        class_probs.append(probs)
        outs.append(dot(low(probs), kv[rows, D : 2 * D]))
    for _ in range(4 - pairs):
        outs.append(jnp.zeros((32, D), jnp.float32))
    class_mix = low(wide(unspread_heads(jnp.concatenate(outs, axis=0)), 16))
    class_mid = class_hid + dot(class_mix, wbuf[1, 3 * D : 4 * D, :])[:8]
    unit_two, _ = norm_parts(class_mid)
    gain4, bias4 = norm_row(8), norm_row(9)
    class_b = low(wide(unit_two * gain4 + bias4, 16))
    fetch(5).wait()
    class_pre = dot(class_b, wbuf[2], 1, 1)
    gate = jax.nn.sigmoid(GELU_SLOPE * class_pre)
    class_act = low(class_pre * gate)
    fetch(6).wait()
    class_out = class_mid + dot(class_act, wbuf[0])[:8]
    gain5, bias5 = norm_row(10), norm_row(11)
    unit_post, _ = norm_parts(class_out)
    pooled = low(wide(unit_post * gain5 + bias5, 16))

    pooled_out = dot(pooled, tail[...], 1, 1)
    pooled_out = jnp.concatenate([pooled_out, jnp.zeros((16, 640 - TAIL_ROWS), jnp.float32)], axis=1)
    embedded = pltpu.roll(pooled_out, 640 - HEAD_AT, 1)[:8, :EMB]
    length = lax.rsqrt(jnp.sum(embedded * embedded, -1, keepdims=True) + NORM_EPS)
    unit_rows = embedded * length
    logits = LOGIT_SCALE * dot(low(wide(unit_rows, 16)), text_ref[...], 1, 1)[:8]
    top = jnp.max(logits, -1, keepdims=True)
    log_total = top + jnp.log(jnp.sum(jnp.exp(logits - top), -1, keepdims=True))
    log_probs = logits - log_total
    classes = lax.broadcasted_iota(jnp.int32, logits.shape, 1)
    target = jnp.where(classes == label_ref[...], 1.0 - SMOOTH, 0.0) + SMOOTH / CLASSES
    live = live_ref[...]
    losses = -live * jnp.sum(target * log_probs, -1, keepdims=True)
    if not with_grads:
        loss_ref[...] = jnp.broadcast_to(losses, loss_ref.shape)
        return

    grad_raw = low(wide(LOGIT_SCALE * ((jnp.exp(log_probs) - target) * live), 16))
    grad_unit = dot(grad_raw, text_ref[...])[:8]
    along = jnp.sum(grad_unit * embedded, -1, keepdims=True)
    grad_embed = grad_unit * length - embedded * (length * length * length * along)
    grad_embed = low(wide(grad_embed, 16))
    grad_tail = jnp.concatenate(
        [grad_embed.astype(jnp.float32), jnp.zeros((16, 640 - EMB), jnp.float32)], axis=1
    )
    grad_tail = low(pltpu.roll(grad_tail, HEAD_AT, 1)[:, :TAIL_ROWS])
    grad_pooled = dot(grad_tail, tail[...])[:8]

    def put_extra(row, values):
        extra_ref[row : row + 1, :] = values

    extra_ref[...] = jnp.zeros_like(extra_ref)
    lane = lax.broadcasted_iota(jnp.int32, (1, D), 1)
    put_extra(12, jnp.where(lane == 0, jnp.sum(losses), jnp.where(lane == 1, jnp.sum(live), 0.0)))

    def class_norm_back(values, gain_row, grad):
        result, terms = norm_back(values, norm_row(gain_row), grad)
        put_extra(gain_row, jnp.sum(terms, 0, keepdims=True))
        put_extra(gain_row + 1, jnp.sum(grad, 0, keepdims=True))
        return result

    grad_out = class_norm_back(class_out, 10, grad_pooled)

    grad_b = low(wide(grad_out, 16))
    grad_act = dot(grad_b, wbuf[0], 1, 1)
    grad_pre = low(grad_act * (gate + GELU_SLOPE * class_pre * gate * (1.0 - gate)))
    fetch(7).start()
    grad_mid = grad_out + class_norm_back(class_mid, 8, dot(grad_pre, wbuf[2])[:8])
    fetch(8).start()
    grad_proj = low(wide(grad_mid, 16))
    grad_mix = low(dot(grad_proj, wbuf[1, 3 * D : 4 * D, :], 1, 1))
    spread_g = low(spread_heads(grad_mix[:8].astype(jnp.float32)))
    grad_qs = []
    for pair in range(pairs):
        rows = slice(pair * PAIR, (pair + 1) * PAIR)
        some_g, some_q = spread_g[32 * pair : 32 * pair + 32], spread_q[32 * pair : 32 * pair + 32]
        probs = class_probs[pair]
        grad_probs = dot(some_g, kv[rows, D : 2 * D], 1, 1)
        dqkv[rows, 2 * D : 3 * D] = low(dot(low(probs), some_g, 0, 0))
        grad_scores = probs * (grad_probs - jnp.sum(grad_probs * probs, -1, keepdims=True))
        grad_scores = low(grad_scores)
        grad_qs.append(dot(grad_scores, kv[rows, 0:D]))
        dqkv[rows, D : 2 * D] = low(dot(grad_scores, some_q, 0, 0) * HEAD ** (-0.5))
    grad_q = low(wide(unspread_heads(jnp.concatenate(grad_qs, axis=0)) * HEAD ** (-0.5), 16))

    def pack(first, second, at, width):
        factor_ref[:, at : at + width] = low(
            jnp.concatenate([first[:8].astype(jnp.float32), second[:8].astype(jnp.float32)], axis=0)
        )

    pack(grad_pre, class_act, 0, FF)
    pack(class_a, class_mix, FF, D)
    pack(grad_q, grad_proj, FF + D, D)
    pack(class_b, grad_b, FF + 2 * D, D)
    embed_wide = jnp.concatenate(
        [grad_embed.astype(jnp.float32), jnp.zeros((16, D - EMB), jnp.float32)], axis=1
    )
    pack(embed_wide, pooled, FF + 3 * D, D)

    started = [0]

    def push(slot, at):
        return pltpu.make_async_copy(stage.at[slot], g_hbm.at[pl.ds(at, D)], stage_sem.at[slot])

    def weight_grad(left, left_at, right, right_at, at, count):
        base = started[0]

        def one(block):
            slot = lax.rem(base + block, 2)

            @pl.when(base + block >= 2)
            def _():
                push(slot, at).wait()

            from_lane = pl.multiple_of(left_at + block * D, D) if count > 1 else left_at
            stage[slot] = low(dot(left[:, pl.ds(from_lane, D)], right[:, right_at : right_at + D], 0, 0))
            push(slot, pl.multiple_of(at + block * D, 16)).start()

        if count > 1:
            pl.loop(0, count)(one)
        else:
            one(0)
        started[0] = base + count

    def norm_back_rows(values, gain_row, grad, finish):
        gain = norm_row(gain_row)
        extra_ref[gain_row : gain_row + 2, :] = jnp.zeros((2, D), jnp.float32)

        @chunks_of()
        def _(index):
            rows = rows_at(index)
            grad_rows = grad[rows, :]
            result, terms = norm_back(values[rows, :], gain, grad_rows)
            at = slice(gain_row, gain_row + 1)
            extra_ref[at, :] = extra_ref[at, :] + jnp.sum(terms, 0, keepdims=True)
            at = slice(gain_row + 1, gain_row + 2)
            extra_ref[at, :] = extra_ref[at, :] + jnp.sum(grad_rows, 0, keepdims=True)
            finish(rows, result)

    weight_grad(norm_c, 0, dqkv, D, layer_at[1] + D, 1)
    weight_grad(norm_c, 0, dqkv, 2 * D, layer_at[1] + 2 * D, 1)
    acc[...] = dot(dqkv[:, D : 2 * D], wbuf[1, D : 2 * D, :], 1, 1)
    acc[...] = acc[...] + dot(dqkv[:, 2 * D : 3 * D], wbuf[1, 2 * D : 3 * D, :], 1, 1)
    add_class_rows(acc, dot(grad_q, wbuf[1, 0:D, :], 1, 1))
    fetch(9).start()

    def finish_second(rows, result):
        dhid[rows, :] = result

    norm_back_rows(hid1, 6, acc, finish_second)
    add_class_rows(dhid, grad_mid)

    gb[...] = low(dhid[...])
    fetch(7).wait()
    weight_grad(act, 0, gb, 0, layer_at[0] + 4 * D + FF, FF // D)

    @pl.loop(0, 3)
    def _(part):
        at = pl.ds(pl.multiple_of(part * 1024, 1024), 1024)
        grad_rows = dot(gb[...], wbuf[0, at, :], 1, 1)
        values = pre[:, at].astype(jnp.float32)
        gates = jax.nn.sigmoid(GELU_SLOPE * values)
        pre[:, at] = low(grad_rows * (gates + GELU_SLOPE * values * gates * (1.0 - gates)))

    weight_grad(pre, 0, norm_b, 0, layer_at[0] + 4 * D, FF // D)
    fetch(8).wait()
    acc[...] = dot(pre[...], wbuf[2])

    def finish_mid(rows, result):
        total = dhid[rows, :] + result
        dhid[rows, :] = total
        gb[rows, :] = low(total)

    norm_back_rows(mid0, 4, acc, finish_mid)
    weight_grad(mixed, 0, gb, 0, layer_at[0] + 3 * D, 1)
    fetch(9).wait()
    dmix[...] = low(dot(gb[...], wbuf[1, 3 * D : 4 * D, :], 1, 1))

    @pl.loop(0, pairs)
    def _(index):
        rows = rows_at(index)
        for group in range(3):
            queries = stack_heads(qkv[rows, lanes(0, group)])
            keys = qkv[rows, lanes(1, group)]
            probs = pair_soft(queries, keys)
            some_g = stack_heads(dmix[rows, lanes(0, group)])
            grad_probs = dot(some_g, qkv[rows, lanes(2, group)], 1, 1)
            dqkv[rows, lanes(2, group)] = low(dot(low(probs), some_g, 0, 0))
            grad_scores = probs * (grad_probs - jnp.sum(grad_probs * probs, -1, keepdims=True))
            grad_scores = low(grad_scores)
            grad_queries = fold_heads(dot(grad_scores, keys))
            dqkv[rows, lanes(0, group)] = low(grad_queries * HEAD ** (-0.5))
            grad_keys = dot(grad_scores, queries, 0, 0)
            dqkv[rows, lanes(1, group)] = low(grad_keys * HEAD ** (-0.5))

    for part in range(3):
        weight_grad(norm_a, 0, dqkv, part * D, layer_at[0] + part * D, 1)
    acc[...] = dot(dqkv[:, 0:D], wbuf[1, 0:D, :], 1, 1)
    for part in (1, 2):
        at = slice(part * D, (part + 1) * D)
        acc[...] = acc[...] + dot(dqkv[:, at], wbuf[1, at, :], 1, 1)

    def finish_first(rows, result):
        dhid[rows, :] = dhid[rows, :] + result

    norm_back_rows(hid0, 2, acc, finish_first)

    def finish_embedding(rows, result):
        dhid[rows, :] = result
        gb[rows, :] = low(result)

    norm_back_rows(emb, 0, dhid, finish_embedding)
    weight_grad(pix, 0, gb, 0, 0, PATCH_IN // D)
    grad_tokens = dhid[0:TOKENS, :]
    for i in range(1, images):
        grad_tokens = grad_tokens + dhid[TOKENS * i : TOKENS * (i + 1), :]
    class_grad = grad_tokens[CLASS_AT : CLASS_AT + 1]
    grad_tokens = jnp.concatenate(
        [grad_tokens, jnp.zeros((TABLE_ROWS - TOKENS, D), jnp.float32)], axis=0
    )
    grad_table = pltpu.roll(grad_tokens, 2, 0)
    row = lax.broadcasted_iota(jnp.int32, (TABLE_ROWS, D), 0)
    grad_table = jnp.where(row < 2, class_grad, jnp.where(row < SEQ + 1, grad_table, 0.0))
    table[...] = low(grad_table)
    put_table = pltpu.make_async_copy(table, g_hbm.at[pl.ds(BLOCK, TABLE_ROWS)], small_sem.at[0])
    put_table.start()
    put_table.wait()
    for slot in range(2):
        push(slot, 0).wait()


def run_tower(weights, pixel_rows, label_row, live_mask, text, with_grads):
    images = label_row.shape[0]
    rows_all = images * TOKENS
    bf16, f32 = jnp.bfloat16, jnp.float32
    labels = jnp.zeros((8, 1), jnp.int32).at[:images, 0].set(label_row)
    live = jnp.zeros((8, 1), f32).at[:images, 0].set(live_mask)
    scratch = [
        pltpu.VMEM((3, BLOCK, D), bf16),
        pltpu.VMEM((TAIL_ROWS, D), bf16),
        pltpu.VMEM((TABLE_ROWS, D), bf16),
        pltpu.VMEM((rows_all, PATCH_IN), bf16),
        pltpu.VMEM((rows_all, D), f32),
        pltpu.VMEM((rows_all, D), f32),
        pltpu.VMEM((rows_all, D), f32),
        pltpu.VMEM((rows_all, D), f32),
        pltpu.VMEM((rows_all, D), f32),
        pltpu.VMEM((rows_all, 3 * D), bf16),
        pltpu.VMEM((rows_all, D), bf16),
        pltpu.VMEM((rows_all, D), bf16),
        pltpu.VMEM((rows_all, D), bf16),
        pltpu.VMEM((rows_all if with_grads else 16, FF), bf16),
        pltpu.VMEM((rows_all, FF), bf16),
        pltpu.VMEM((rows_all, D), bf16),
        pltpu.VMEM((rows_all, 2 * D), bf16),
    ]
    if with_grads:
        scratch += [
            pltpu.VMEM((rows_all, D), f32),
            pltpu.VMEM((rows_all, 3 * D), bf16),
            pltpu.VMEM((rows_all, D), bf16),
            pltpu.VMEM((rows_all, D), bf16),
            pltpu.VMEM((2, D, D), bf16),
            pltpu.SemaphoreType.DMA((2,)),
        ]
        out_shape = (
            jax.ShapeDtypeStruct((grad_rows_kept(weights.shape[0]), D), bf16),
            jax.ShapeDtypeStruct((16, LOW_COLS), bf16),
            jax.ShapeDtypeStruct((16, D), f32),
        )
        out_specs = (
            pl.BlockSpec(memory_space=pl.ANY),
            pl.BlockSpec(memory_space=pltpu.VMEM),
            pl.BlockSpec(memory_space=pltpu.VMEM),
        )
    else:
        out_shape = jax.ShapeDtypeStruct((8, 128), f32)
        out_specs = pl.BlockSpec(memory_space=pltpu.VMEM)
    scratch += [pltpu.SemaphoreType.DMA((3,)), pltpu.SemaphoreType.DMA((3,))]
    vmem = pl.BlockSpec(memory_space=pltpu.VMEM)
    hbm = pl.BlockSpec(memory_space=pl.ANY)
    return pl.pallas_call(
        functools.partial(tower_kernel, images, with_grads),
        out_shape=out_shape,
        in_specs=[hbm, hbm, vmem, vmem, vmem],
        out_specs=out_specs,
        scratch_shapes=scratch,
        compiler_params=pltpu.CompilerParams(vmem_limit_bytes=60 * 2**20),
        name="train" if with_grads else "evaluate",
    )(weights, pixel_rows, text, labels, live)


def grad_rows_kept(rows):
    if not on_grid():
        return DENSE_END
    plane_rows = rows // 4
    return (DENSE_END + plane_rows - 1) // plane_rows * plane_rows


def on_grid():
    return lax.axis_size("group") == 4 and lax.axis_size("dp") == 8


def place():
    worker = lax.axis_index("group")
    rank = lax.axis_index("dp")
    return (worker // 2, worker % 2, rank // 2, rank % 2)


def device_at(y, c, z, x):
    return (y * 2 + c, z * 2 + x)


def chunk_rows(total, count):
    units = total // 16
    chunks = []
    start = 0
    for index in range(count):
        size = units * (index + 1) // count - units * index // count
        first = size // 2 if index % 2 else size - size // 2
        chunks.append((start * 16, first * 16, (size - first) * 16))
        start += size
    return chunks


def gather_kernel(chunks, part_ref, full_ref, local_sem, sends, recvs):
    half_cols = part_ref.shape[1]
    y, c, z, x = place()
    cols = pl.ds(pl.multiple_of(c * half_cols, half_cols), half_cols)
    over_x = device_at(y, c, z, 1 - x)
    over_y = device_at(1 - y, c, z, x)
    sibling = device_at(y, 1 - c, z, x)
    along_z = [device_at(y, c, (z + step) % 4, x) for step in (1, 2, 3)]
    barrier = pltpu.get_barrier_semaphore()
    for other in [over_x, over_y, sibling] + along_z:
        pl.semaphore_signal(barrier, inc=1, device_id=other, device_id_type=MESH)
    local = pltpu.make_async_copy(part_ref, full_ref.at[z, x, y, :, cols], local_sem)
    local.start()
    pl.semaphore_wait(barrier, 6)

    def send(piece, other, stage, index):
        pltpu.make_async_remote_copy(
            src_ref=piece,
            dst_ref=piece,
            send_sem=sends.at[stage, index],
            recv_sem=recvs.at[stage, index],
            device_id=other,
            device_id_type=MESH,
        ).start()

    def arrived(piece, stage, index):
        pltpu.make_async_copy(piece, piece, recvs.at[stage, index]).wait()

    def sent(piece, stage, index):
        pltpu.make_async_copy(piece, piece, sends.at[stage, index]).wait()

    def pieces(index):
        start, first, second = chunks[index]
        rows = pl.ds(start, first + second)
        rows_a = pl.ds(start, first)
        rows_b = pl.ds(start + first, second)
        return {
            0: full_ref.at[pl.ds(0, 3), 0, 0, rows, cols],
            1: full_ref.at[:, x, y, rows_a, cols],
            2: full_ref.at[:, x, y, rows_b, cols],
            3: full_ref.at[:, x, :, rows_a, cols],
            4: full_ref.at[:, :, y, rows_b, cols],
            5: full_ref.at[:, :, :, rows, cols],
        }

    total = len(chunks)
    for step in range(total + 5):
        if step < total:
            start, first, second = chunks[step]
            rows = pl.ds(start, first + second)
            for other in along_z:
                pltpu.make_async_remote_copy(
                    src_ref=part_ref.at[rows],
                    dst_ref=full_ref.at[z, x, y, rows, cols],
                    send_sem=sends.at[0, step],
                    recv_sem=recvs.at[0, step],
                    device_id=other,
                    device_id_type=MESH,
                ).start()
        if step == 0:
            local.wait()
        index = step - 1
        if 0 <= index < total:
            block = pieces(index)
            arrived(block[0], 0, index)
            send(block[1], over_y, 1, index)
            send(block[2], over_x, 2, index)
        index = step - 2
        if 0 <= index < total:
            block = pieces(index)
            arrived(block[1], 1, index)
            send(block[3], over_x, 3, index)
            arrived(block[2], 2, index)
            send(block[4], over_y, 4, index)
        index = step - 3
        if 0 <= index < total:
            block = pieces(index)
            arrived(block[3], 3, index)
            arrived(block[4], 4, index)
            send(block[5], sibling, 5, index)
    for index in range(total):
        block = pieces(index)
        arrived(block[5], 5, index)
        for stage in range(6):
            sent(block[stage], stage, index)


def gather_rows(part, shard_rows):
    chunks = chunk_rows(part.shape[0], 8)
    full = pl.pallas_call(
        functools.partial(gather_kernel, chunks),
        out_shape=jax.ShapeDtypeStruct((4, 2, 2, part.shape[0], 2 * part.shape[1]), part.dtype),
        in_specs=[pl.BlockSpec(memory_space=pl.ANY)],
        out_specs=pl.BlockSpec(memory_space=pl.ANY),
        scratch_shapes=[
            pltpu.SemaphoreType.DMA,
            pltpu.SemaphoreType.DMA((6, len(chunks))),
            pltpu.SemaphoreType.DMA((6, len(chunks))),
        ],
        compiler_params=pltpu.CompilerParams(collective_id=0, has_side_effects=True),
        name="gather",
    )(part)
    return full.reshape(8 * shard_rows, 2 * part.shape[1])


def reduce_kernel(
    chunks,
    low_from,
    grad_ref,
    factor_ref,
    extra_ref,
    own_ref,
    factors_ref,
    extras_ref,
    mine,
    first_sum,
    sum_a,
    sum_b,
    last_sum,
    load_sems,
    sends,
    recvs,
    small_sends,
    small_recvs,
):
    half_cols = mine.shape[-1]
    planes = grad_ref.shape[0]
    y, c, z, x = place()
    home_y, home_c = z % 2, z // 2
    at_home = jnp.logical_and(home_y == y, home_c == c)
    from_plane = 2 * c + y
    my_cols = pl.ds(pl.multiple_of(c * half_cols, half_cols), half_cols)
    other_cols = pl.ds(pl.multiple_of((1 - c) * half_cols, half_cols), half_cols)
    over_x = device_at(y, c, z, 1 - x)
    over_y = device_at(1 - y, c, z, x)
    sibling = device_at(y, 1 - c, z, x)
    barrier = pltpu.get_barrier_semaphore()
    for other in (over_x, over_y, sibling):
        pl.semaphore_signal(barrier, inc=1, device_id=other, device_id_type=MESH)
    for other in range(8):
        other_y, other_c, other_x = other // 4, other // 2 % 2, other % 2
        same = jnp.logical_and(y == other_y, jnp.logical_and(c == other_c, x == other_x))
        itself = jnp.logical_and(at_home, same)

        @pl.when(jnp.logical_not(itself))
        def _():
            pl.semaphore_signal(
                barrier,
                inc=1,
                device_id=device_at(other_y, other_c, from_plane, other_x),
                device_id_type=MESH,
            )

    def spans(index):
        start, first, second = chunks[index]
        start_a = sum(chunk[1] for chunk in chunks[:index])
        start_b = sum(chunk[2] for chunk in chunks[:index])
        return (
            pl.ds(start, first + second),
            pl.ds(start, first),
            pl.ds(start + first, second),
            pl.ds(start_a, first),
            pl.ds(start_b, second),
        )

    def send(source, target, other, stage, index):
        pltpu.make_async_remote_copy(
            src_ref=source,
            dst_ref=target,
            send_sem=sends.at[stage, index],
            recv_sem=recvs.at[stage, index],
            device_id=other,
            device_id_type=MESH,
        ).start()

    def arrived(piece, stage, index):
        pltpu.make_async_copy(piece, piece, recvs.at[stage, index]).wait()

    def sent(piece, stage, index):
        pltpu.make_async_copy(piece, piece, sends.at[stage, index]).wait()

    def load(index):
        rows = spans(index)[0]
        return pltpu.make_async_copy(
            grad_ref.at[:, :, :, rows, my_cols],
            mine.at[index % 2, :, :, :, pl.ds(0, rows.size)],
            load_sems.at[index % 2],
        )

    def send_core(index):
        rows = spans(index)[0]
        send(
            grad_ref.at[:, :, :, rows, other_cols],
            first_sum.at[:, :, :, rows],
            sibling,
            0,
            index,
        )

    def add(target, source):
        summed = target[...].astype(jnp.float32) + source[...].astype(jnp.float32)
        target[...] = summed.astype(target.dtype)

    total = len(chunks)
    load(0).start()
    pl.semaphore_wait(barrier, 3 + jnp.where(at_home, 7, 8))
    send_core(0)
    send_core(1)
    slot = (y * 2 + c) * 2 + x
    for other in range(8):
        other_z, other_x = other // 2, other % 2
        itself = jnp.logical_and(at_home, jnp.logical_and(z == other_z, x == other_x))
        for which, (source, target) in enumerate(
            ((extra_ref, extras_ref.at[slot]), (factor_ref, factors_ref.at[slot]))
        ):
            if which == 1 and other_z < low_from:
                continue

            @pl.when(jnp.logical_not(itself))
            def _():
                pltpu.make_async_remote_copy(
                    src_ref=source,
                    dst_ref=target,
                    send_sem=small_sends.at[which],
                    recv_sem=small_recvs.at[which],
                    device_id=device_at(home_y, home_c, other_z, other_x),
                    device_id_type=MESH,
                ).start()

            @pl.when(itself)
            def _():
                pltpu.make_async_copy(source, target, small_recvs.at[which]).start()

    for step in range(total + 4):
        index = step
        if index < total:
            if index + 1 < total:
                load(index + 1).start()
            if index + 2 < total:
                send_core(index + 2)
            rows, rows_a, rows_b, in_a, in_b = spans(index)
            load(index).wait()
            arrived(first_sum.at[:, :, :, rows], 0, index)

            @pl.loop(0, 4 * planes)
            def _(block):
                zz, rest = block // 4, block % 4
                add(
                    first_sum.at[zz, rest // 2, rest % 2, rows],
                    mine.at[index % 2, zz, rest // 2, rest % 2, pl.ds(0, rows.size)],
                )

            send(first_sum.at[:, 1 - x, :, rows_a], sum_a.at[:, :, in_a], over_x, 1, index)
            send(first_sum.at[:, :, 1 - y, rows_b], sum_b.at[:, :, in_b], over_y, 2, index)
        index = step - 1
        if 0 <= index < total:
            rows, rows_a, rows_b, in_a, in_b = spans(index)
            arrived(sum_a.at[:, :, in_a], 1, index)

            @pl.loop(0, 2 * planes)
            def _(block):
                add(
                    sum_a.at[block // 2, block % 2, in_a],
                    first_sum.at[block // 2, x, block % 2, rows_a],
                )

            send(sum_a.at[:, 1 - y, in_a], last_sum.at[:, rows_a], over_y, 3, index)
            arrived(sum_b.at[:, :, in_b], 2, index)

            @pl.loop(0, 2 * planes)
            def _(block):
                add(
                    sum_b.at[block // 2, block % 2, in_b],
                    first_sum.at[block // 2, block % 2, y, rows_b],
                )

            send(sum_b.at[:, 1 - x, in_b], last_sum.at[:, rows_b], over_x, 4, index)
        index = step - 2
        if 0 <= index < total:
            rows, rows_a, rows_b, in_a, in_b = spans(index)
            arrived(last_sum.at[:, rows_a], 3, index)
            arrived(last_sum.at[:, rows_b], 4, index)

            @pl.loop(0, planes)
            def _(block):
                add(last_sum.at[block, rows_a], sum_a.at[block, y, in_a])
                add(last_sum.at[block, rows_b], sum_b.at[block, x, in_b])

            for to_z in range(planes):
                itself = jnp.logical_and(at_home, z == to_z)
                source = last_sum.at[to_z, rows]
                target = own_ref.at[y, rows, my_cols]

                @pl.when(jnp.logical_not(itself))
                def _():
                    send(source, target, device_at(home_y, home_c, to_z, x), 5, index)

                @pl.when(itself)
                def _():
                    pltpu.make_async_copy(source, target, recvs.at[5, index]).start()

    for index in range(total):
        rows, rows_a, rows_b, in_a, in_b = spans(index)

        @pl.when(z < planes)
        def _():
            arrived(own_ref.at[:, rows], 5, index)

        sent(first_sum.at[:, :, :, rows], 0, index)
        sent(sum_a.at[:, :, in_a], 1, index)
        sent(sum_b.at[:, :, in_b], 2, index)
        sent(last_sum.at[:, rows_a], 3, index)
        sent(last_sum.at[:, rows_b], 4, index)

        kept = jnp.logical_and(at_home, z < planes)

        @pl.when(kept)
        def _():
            sent(last_sum.at[pl.ds(0, planes - 1), rows], 5, index)

        @pl.when(jnp.logical_not(kept))
        def _():
            sent(last_sum.at[:, rows], 5, index)

    def all_of(ref, count, sem):
        piece = ref.at[pl.ds(0, count)]
        pltpu.make_async_copy(piece, piece, sem).wait()

    all_of(extras_ref, 8, small_recvs.at[0])

    @pl.when(z >= low_from)
    def _():
        all_of(factors_ref, 8, small_recvs.at[1])

    @pl.when(at_home)
    def _():
        all_of(extras_ref, 7, small_sends.at[0])

    @pl.when(jnp.logical_not(at_home))
    def _():
        all_of(extras_ref, 8, small_sends.at[0])

    low_targets = 2 * (4 - low_from)
    low_kept = jnp.logical_and(at_home, z >= low_from)

    @pl.when(low_kept)
    def _():
        all_of(factors_ref, low_targets - 1, small_sends.at[1])

    @pl.when(jnp.logical_not(low_kept))
    def _():
        all_of(factors_ref, low_targets, small_sends.at[1])


def reduce_chunks(total, count, share):
    units = total // 16
    chunks = []
    start = 0
    for index in range(count):
        size = units * (index + 1) // count - units * index // count
        first = int(round(size * share))
        chunks.append((start * 16, first * 16, (size - first) * 16))
        start += size
    return chunks


def sum_on_plane(grad_rows, factors, extra, shard_rows):
    half_rows, width = shard_rows // 2, grad_rows.shape[1]
    planes = grad_rows.shape[0] // (2 * shard_rows)
    chunks = reduce_chunks(half_rows, 8, 0.75)
    most = max(first + second for _, first, second in chunks)
    half_cols = width // 2
    dtype = grad_rows.dtype
    low_from = (FIRST_LAYER + 4 * D + 2 * FF) // (2 * shard_rows)
    own, all_factors, all_extra = pl.pallas_call(
        functools.partial(reduce_kernel, chunks, low_from),
        out_shape=(
            jax.ShapeDtypeStruct((2, half_rows, width), dtype),
            jax.ShapeDtypeStruct((8,) + factors.shape, factors.dtype),
            jax.ShapeDtypeStruct((8,) + extra.shape, extra.dtype),
        ),
        in_specs=[pl.BlockSpec(memory_space=pl.ANY)] * 3,
        out_specs=[pl.BlockSpec(memory_space=pl.ANY)] * 3,
        scratch_shapes=[
            pltpu.VMEM((2, planes, 2, 2, most, half_cols), dtype),
            pltpu.VMEM((planes, 2, 2, half_rows, half_cols), dtype),
            pltpu.VMEM((planes, 2, sum(chunk[1] for chunk in chunks), half_cols), dtype),
            pltpu.VMEM((planes, 2, sum(chunk[2] for chunk in chunks), half_cols), dtype),
            pltpu.VMEM((planes, half_rows, half_cols), dtype),
            pltpu.SemaphoreType.DMA((2,)),
            pltpu.SemaphoreType.DMA((6, len(chunks))),
            pltpu.SemaphoreType.DMA((6, len(chunks))),
            pltpu.SemaphoreType.DMA((2,)),
            pltpu.SemaphoreType.DMA((2,)),
        ],
        compiler_params=pltpu.CompilerParams(
            collective_id=1, has_side_effects=True, vmem_limit_bytes=56 * 2**20
        ),
        name="reduce",
    )(grad_rows.reshape(planes, 2, 2, half_rows, width), factors, extra)
    return (own.reshape(shard_rows, width), all_factors, all_extra)


def to_planes(values):
    pairs = []
    for source in range(32):
        y, c, z, x = source // 16, source // 8 % 2, source // 2 % 4, source % 2
        pairs.append((source, (z % 2 * 2 + z // 2) * 8 + (2 * c + y) * 2 + x))
    return lax.ppermute(values, ("group", "dp"), pairs)


def fetch_weights(params):
    rows, width = params.shape
    ranks, rank = lax.axis_size("dp"), lax.axis_index("dp")
    before = lax.ppermute(params[-16:], "dp", [(source, source + 1) for source in range(ranks - 1)])
    longer = jnp.concatenate([before, params], axis=0)
    in_place = lax.broadcasted_iota(jnp.int32, (rows, 1), 0) + rank * rows < layout_rows()[1]
    if not on_grid():
        moved = jnp.where(in_place, params, longer[16 - SPARE :][:rows])
        return lax.all_gather(moved.astype(jnp.bfloat16), "dp", axis=0, tiled=True)
    y, c, _, _ = place()
    half, half_cols = rows // 2, width // 2
    part = lax.dynamic_slice(params, (y * half, c * half_cols), (half, half_cols))
    moved = lax.dynamic_slice(longer, (y * half + 16 - SPARE, c * half_cols), (half, half_cols))
    in_place = lax.dynamic_slice(in_place, (y * half, 0), (half, 1))
    return gather_rows(jnp.where(in_place, part, moved).astype(jnp.bfloat16), rows)


def low_rank_rows(factors, extra, first_row, count):
    last_layer = FIRST_LAYER + 4 * D + 2 * FF
    devices = factors.shape[0]

    def half(at, width, which):
        piece = factors[:, 8 * which : 8 * which + 8, at : at + width]
        return piece.reshape(devices * 8, width)

    norms = extra[:16].astype(jnp.bfloat16)
    sections = [
        (last_layer, half(FF, D, 0), half(FF + D, D, 0)),
        (last_layer + 3 * D, half(FF, D, 1), half(FF + D, D, 1)),
        (last_layer + 4 * D, half(0, FF, 0), half(FF + 2 * D, D, 0)),
        (last_layer + 4 * D + FF, half(0, FF, 1), half(FF + 2 * D, D, 1)),
        (TAIL_START, jnp.eye(16, HEAD_AT, dtype=jnp.bfloat16), norms),
        (TAIL_START + HEAD_AT, half(FF + 3 * D, EMB, 0), half(FF + 3 * D, D, 1)),
    ]
    row = first_row + jnp.arange(count)
    lefts, rights = [], []
    for start, left, right in sections:
        width = left.shape[1]
        padded = jnp.pad(left, ((0, 0), (count, count)))
        at = jnp.clip(first_row - start + count, 0, width + count)
        window = lax.dynamic_slice(padded, (0, at), (left.shape[0], count))
        inside = (row >= start) & (row < start + width)
        lefts.append(jnp.where(inside[None], window, jnp.zeros_like(window)))
        rights.append(right)
    return lax.dot_general(
        jnp.concatenate(lefts, axis=0),
        jnp.concatenate(rights, axis=0),
        (((0,), (0,)), ((), ())),
        preferred_element_type=jnp.float32,
    )


def reduce_rows(grad_rows, factors, extra, count):
    ranks, rank = lax.axis_size("dp"), lax.axis_index("dp")
    last_layer = FIRST_LAYER + 4 * D + 2 * FF
    flat_row = rank * count + lax.broadcasted_iota(jnp.int32, (count, 1), 0)
    if on_grid():
        shard, factors, extra = sum_on_plane(grad_rows, factors, extra, count)
        extra = jnp.sum(extra, axis=0)
    else:
        rest = low_rank_rows(factors[None], extra, 0, ranks * count).astype(jnp.bfloat16)
        whole = jnp.where(dense_row(jnp.arange(DENSE_END))[:, None], grad_rows, rest[:DENSE_END])
        whole = jnp.concatenate([whole, rest[DENSE_END:]], axis=0)
        shard = lax.psum_scatter(whole, "dp", scatter_dimension=0, tiled=True)
        extra = lax.psum(extra, "dp")
    following = lax.ppermute(shard[:16], "dp", [(source, source - 1) for source in range(1, ranks)])
    shifted = jnp.concatenate([shard[SPARE:], following[:SPARE]], axis=0)
    summed = jnp.where(flat_row < layout_rows()[1], shard, shifted).astype(jnp.float32)
    if on_grid():
        rest = low_rank_rows(factors, extra, rank * count + SPARE, count)
        spared = jnp.where(flat_row < layout_rows()[1], flat_row, flat_row + SPARE)
        summed = jnp.where(dense_row(spared), summed, rest)
    return (summed, extra)


def dense_row(row):
    last_layer = FIRST_LAYER + 4 * D + 2 * FF
    return (row < last_layer) | ((row >= last_layer + D) & (row < DENSE_END))


def adam_update(params, moment_one, moment_two, clipped, step_number):
    moment_one = BETA_ONE * moment_one + (1.0 - BETA_ONE) * clipped
    moment_two = BETA_TWO * moment_two + (1.0 - BETA_TWO) * clipped * clipped
    corrected_one = moment_one / (1.0 - BETA_ONE**step_number)
    corrected_two = moment_two / (1.0 - BETA_TWO**step_number)
    params = params - RATE * (corrected_one / (jnp.sqrt(corrected_two) + ADAM_EPS) + DECAY * params)
    return (params, moment_one, moment_two)


def nesterov(master_rows, momentum_rows, mean_delta):
    momentum_next = OUTER_MOM * momentum_rows + mean_delta
    return (master_rows - OUTER_RATE * (mean_delta + OUTER_MOM * momentum_next), momentum_next)


def token_rows(pixel_block):
    images, patches, _ = pixel_block.shape
    padded = jnp.pad(pixel_block, ((0, 0), (0, TOKENS - patches), (0, 0)))
    return padded.reshape(images * TOKENS, PATCH_IN)


def per_device(
    pixels,
    counts,
    labels,
    text,
    master,
    outer_momentum,
    first_moment,
    second_moment,
    eval_pixels,
    eval_counts,
    eval_labels,
):
    params = master
    moment_one = first_moment[0]
    moment_two = second_moment[0]
    norm_list, loss_list, count_list, post_list = ([], [], [], [])
    slots = pixels.shape[2]
    live = (jnp.arange(slots)[None, :] < counts[0]).astype(jnp.float32).reshape(-1)
    step_labels = labels[0].reshape(-1)
    step_pixels = token_rows(pixels[0].reshape((-1,) + pixels.shape[3:]))
    if on_grid():
        step_pixels, live, step_labels = [
            to_planes(values) for values in (step_pixels, live, step_labels)
        ]
    weights = fetch_weights(params)
    grad_rows, factors, extra = run_tower(weights, step_pixels, step_labels, live, text, True)
    reduced, extra = reduce_rows(grad_rows, factors, extra, params.shape[0])
    loss_all, count_all, post_all = extra[12, 0], extra[12, 1], extra[10:12]
    square_all = lax.psum(jnp.sum(reduced * reduced), "dp")
    gradient = reduced / count_all
    grad_norm = jnp.sqrt(square_all) / count_all
    clip_factor = CLIP_MAX / jnp.maximum(grad_norm, CLIP_MAX)
    clipped = gradient * clip_factor
    params, moment_one, moment_two = adam_update(params, moment_one, moment_two, clipped, STEP)
    norm_list.append(grad_norm)
    loss_list.append(loss_all)
    count_list.append(count_all)
    post_list.append(post_all / count_all * clip_factor)
    delta = master - params
    groups = lax.axis_size("group")
    mean_delta = lax.psum(delta.astype(jnp.bfloat16), "group").astype(jnp.float32) / groups
    new_master, new_outer = nesterov(master, outer_momentum, mean_delta)
    soup_rows = fetch_weights(new_master)
    eval_live = (jnp.arange(eval_pixels.shape[0]) < eval_counts[0]).astype(jnp.float32)
    eval_tile = run_tower(soup_rows, token_rows(eval_pixels), eval_labels, eval_live, text, False)
    eval_losses = eval_tile[: eval_labels.shape[0], 0]
    return (
        new_master,
        new_outer,
        moment_one[None],
        moment_two[None],
        jnp.stack(norm_list)[None],
        jnp.stack(loss_list)[None],
        jnp.stack(count_list)[None],
        jnp.stack(post_list)[None],
        eval_losses,
    )


def solution(mesh):
    return jax.shard_map(
        per_device,
        mesh=mesh,
        in_specs=(
            P(None, None, ("group", "dp"), None, None),
            P(None, None, ("group", "dp")),
            P(None, None, ("group", "dp")),
            P(),
            P("dp", None),
            P("dp", None),
            P("group", "dp", None),
            P("group", "dp", None),
            P(("group", "dp"), None, None),
            P(("group", "dp")),
            P(("group", "dp")),
        ),
        out_specs=(
            P("dp", None),
            P("dp", None),
            P("group", "dp", None),
            P("group", "dp", None),
            P("group", None),
            P("group", None),
            P("group", None),
            P("group", None, None, None),
            P(("group", "dp")),
        ),
        check_vma=False,
    )
```

time: 1340 us -> 963 us (0.72)
  local copies, waits for them, and re-layouts: 256 us -> 21.1 us
  matrix products: 185 us -> 10.4 us
  waiting for transfers between devices: 69.1 us -> 169 us
  other arithmetic: 121 us -> 57.6 us
  blocking collectives: 43.6 us -> 13.8 us
  starting transfers between devices: 11.3 us -> 33.2 us
  Pallas kernels: 611 us -> 630 us
    dot_general x56 -> x1, matrix products: 185 us -> 10.4 us  [low_rank_rows(): lax.dot_general(jnp.concatenate(lefts, axis=0), jnp.concatenate(rights, a...]
    concatenate x4 -> x1, local copies, waits for them, and re-layouts: 117 us -> 0.9 us  [low_rank_rows(): jnp.concatenate(rights, axis=0)]
    ppermute x3, waiting for transfers between devices: 0.01 us -> 80.2 us  [to_planes(): return lax.ppermute(values, ('group', 'dp'), pairs)]
    pallas_call x1 -> x3, Pallas kernels: 188 us -> 264 us  [the longest x1 162 us: sum_on_plane(): pl.pallas_call(functools.partial(reduce_kernel, chunks, low_from), out_sh...]
    pallas_call x2, Pallas kernels: 423 us -> 366 us  [gather_rows(): pl.pallas_call(functools.partial(gather_kernel, chunks), out_shape=jax.Sh...]
    reduce_sum x42 -> x1, other arithmetic: 39.9 us -> 1.02 us  [reduce_rows(): extra = jnp.sum(extra, axis=0)]
    convert_element_type x16 -> x3, other arithmetic: 43.1 us -> 5.63 us  [the longest x2 5.56 us: fetch_weights(): jnp.where(in_place, part, moved).astype(jnp.bfloat16)]
    broadcast_in_dim x1 -> x2, other arithmetic: 0.08 us -> 36 us  [the longest x1 18.9 us: per_device(): moment_two[None]]
  transfers between devices with their start and end apart: 5 -> 7, of which waited for: 2 -> 3; matrix products, arithmetic and copies ran while one was open for 3% -> 2% of each run, Pallas kernels for 18% -> 18%
where the time goes in v2:
time: 963 us; the launch traced here: 953 us
  Pallas kernels  630 us (65%)
  waiting for transfers between devices  169 us (18%)
  other arithmetic  57.6 us (6%)
  starting transfers between devices  33.2 us (3%)
  local copies, waits for them, and re-layouts  21.1 us (2%)
  between operations  17.9 us (2%)
  blocking collectives  13.8 us (1%)
  matrix products  10.4 us (1%)
    pallas_call x2, Pallas kernels, gather_rows(): pl.pallas_call(functools.partial(gather_kernel, chunks), out_shape=jax.Sh...  366 us
    pallas_call x1, Pallas kernels, sum_on_plane(): pl.pallas_call(functools.partial(reduce_kernel, chunks, low_from), out_sh...  162 us
    pallas_call x2, Pallas kernels, run_tower(): pl.pallas_call(functools.partial(tower_kernel, images, with_grads), out_s...  102 us
    psum x1, waiting for transfers between devices, per_device(): lax.psum(delta.astype(jnp.bfloat16), 'group').astype(jnp.float32) / groups  87.4 us
    ppermute x3, waiting for transfers between devices, to_planes(): return lax.ppermute(values, ('group', 'dp'), pairs)  80.2 us
  transfers between devices with their start and end apart: 7, of which 3 were waited for; matrix products, arithmetic and copies ran while one was open for 2% of the time, Pallas kernels for 18%

profile of v2, /device:TPU:25, one launch (start us, length us, event | category | flops | bytes accessed | tf_op | source)
XLA Modules:
  0.0 952.6 jit_solution(17174935117605190502)
XLA Ops:
  7.2 2.5 copy.32
  10.0 3.0 collective-permute-start.1
  13.2 3.1 collective-permute-start.3
  16.4 3.0 collective-permute-start.2
  20.3 3.1 collective-permute-start
  23.6 80.2 %collective-permute-done.3 = f32[8]{0:T(128)S(1)} collective-permute-done((f32[8]{0:T(128)S(1)}, f32[8]{0:T(128)S(1)}, u32[]{:S(2)}, u32[]{:S(2)}) %collective-permute-start.3) | collective-permute-done | bytes 64 | tf_op jit(solution)/shard_map/ppermute | solution.py:1058
  105.1 3.9 fusion.9.part_ref
  109.0 176.2 %gather.2 = bf16[4,2,2,1392,768]{4,3,2,1,0:T(8,128)(2,1)} custom-call(bf16[1392,384]{1,0:T(8,128)(2,1)} %fusion.9.part_ref), custom_call_target="tpu_custom_call" | custom-call | tf_op jit(solution)/shard_map/gather/pallas_call | solution.py:739
  285.2 79.3 %train.1 = (bf16[16704,768]{1,0:T(8,128)(2,1)}, bf16[16,6144]{1,0:T(8,128)(2,1)}, f32[16,768]{1,0:T(8,128)}) custom-call(bf16[22272,768]{1,0:T(8,128)(2,1)} %bitcast.62, bf16[448,3072]{1,0:T(8,128)(2,1)} %collective-permute-done.1.refs_1_, bf16[1000,512]{1,0:T(8,128)(2,1)} %refs_2_.3, s32[8,1]{1,0:T(8,128)} %copy.26.refs_3_, f32[8,1]{1,0:T(8,128)} %copy.27.refs_4_), custom_call_target="tpu_custom_call" | custom-call | tf_op jit(solution)/shard_map/train/pallas_call | solution.py:606
  364.5 162.0 %reduce.13 = (bf16[2,1392,768]{2,1,0:T(8,128)(2,1)}, bf16[8,16,6144]{2,1,0:T(8,128)(2,1)}, f32[8,16,768]{2,1,0:T(8,128)}) custom-call(bf16[3,2,2,1392,768]{4,3,2,1,0:T(8,128)(2,1)} %bitcast.64, bf16[16,6144]{1,0:T(8,128)(2,1)} %get-tuple-element.64.factor_ref, f32[16,768]{1,0:T(8,128)} %get-tuple-element.65.extra_ref), custom_call_target="tpu_custom_call" | custom-call | tf_op jit(solution)/shard_map/reduce/pallas_call | solution.py:1024
  531.2 17.6 %collective-permute-start.4 = (bf16[16,768]{1,0:T(8,128)(2,1)S(1)}, bf16[16,768]{1,0:T(8,128)(2,1)S(1)}, u32[]{:S(2)}, u32[]{:S(2)}) collective-permute-start(bf16[16,768]{1,0:T(8,128)(2,1)S(1)} %slice.137), channel_id=1, source_target_pairs={{1,0},{2,1},{3,2},{4,3},{5,4},{6,5},{7,6},{9,8},{10,9},{11,10},{12... | collective-permute-start | bytes 73736 | tf_op jit(solution)/shard_map/ppermute | solution.py:1126
  555.2 3.5 slice.136
  558.7 10.4 %multiply_reduce_fusion = (f32[]{:T(128)}, f32[2784,768]{1,0:T(8,128)}) fusion(pred[2784]{0:T(1024)(128)(4,1)S(1)} %get-tuple-element.84, bf16[13,768]{1,0:T(8,128)(2,1)S(1)} %bitcast.72, bf16[2771,768]{1,0:T(8,128)(2,1)S(1)} %slice.136, bf16[2,1392,768]{2,1,0:T(8,128)(2,1)S(1)} %bitcast.68, pred[2784]{0:T(1024)(128)(4,1)S(1)} %get-tuple-element.83, ...), kind=kOutput, calls=%fused_computation.12 | convolution fusion | flops 1456054272 | bytes 19497412 | tf_op jit(solution)/shard_map/dot_general | solution.py:1105
  569.2 13.8 %psum.14 = f32[]{:T(128)} all-reduce(f32[]{:T(128)} %get-tuple-element.81), channel_id=1, replica_groups=mesh['group'=4,'dp'=8] {'dp'}, use_global_device_ids=true, to_apply=%region_2.3 | all-reduce | flops 1 | bytes 8 | tf_op jit(solution)/shard_map/psum | solution.py:1190
  584.4 18.9 %fusion.3 = (f32[1,2784,768]{2,1,0:T(8,128)}, f32[2784,768]{1,0:T(8,128)S(1)}) fusion(f32[1,2784,768]{2,1,0:T(8,128)} %param.26, f32[]{:T(128)S(6)} %div.54, f32[]{:T(128)} %bitcast.18, f32[2784,768]{1,0:T(8,128)} %get-tuple-element.82, bf16[13,768]{1,0:T(8,128)(2,1)S(1)} %bitcast.73, bf16[2771,768]{1,0:T(8,128)(2,1)} %copy-done.1, ...), kind=kLoop, calls=%fused_computation.17 | loop fusion | flops 27795456 | bytes 42767816 | tf_op jit(solution)/shard_map/broadcast_in_dim | solution.py:1212
  603.3 17.1 %fusion.2 = (f32[1,2784,768]{2,1,0:T(8,128)}, bf16[2784,768]{1,0:T(8,128)(2,1)}) fusion(f32[2784,768]{1,0:T(8,128)S(1)} %get-tuple-element.70, f32[1,2784,768]{2,1,0:T(8,128)} %param.25, f32[2784,768]{1,0:T(8,128)} %param.23, f32[1,2784,768]{2,1,0:T(8,128)} %param.26), kind=kLoop, calls=%fused_computation.16 | loop fusion | flops 36347904 | bytes 47038464 | tf_op jit(solution)/shard_map/broadcast_in_dim | solution.py:1211
  622.3 1.3 pad.55.clone
  624.1 87.4 %all-reduce.12.cloned.1.call-done = bf16[2784,768]{1,0:T(8,128)(2,1)} async-done(((bf16[2784,768]{1,0:T(8,128)(2,1)}), bf16[2784,768]{1,0:T(8,128)(2,1)}) %all-reduce.12.cloned.1.call-update) | async-done | bytes 4276240 | tf_op jit(solution)/shard_map/psum | solution.py:1202
  711.5 11.8 %multiply_subtract_fusion = (f32[2784,768]{1,0:T(8,128)S(1)}, f32[2784,768]{1,0:T(8,128)}) fusion(f32[2784,768]{1,0:T(8,128)} %param.23, bf16[2784,768]{1,0:T(8,128)(2,1)} %all-reduce.12.cloned.1.call-done, f32[2784,768]{1,0:T(8,128)} %param.24), kind=kLoop, calls=%fused_computation.9 | loop fusion | flops 17104896 | bytes 38486016 | tf_op jit(solution)/shard_map/sub | solution.py:1152
  723.4 3.3 collective-permute-start.5
  728.9 1.7 fusion.6.part_ref
  730.5 189.8 %gather.3 = bf16[4,2,2,1392,768]{4,3,2,1,0:T(8,128)(2,1)} custom-call(bf16[1392,384]{1,0:T(8,128)(2,1)} %fusion.6.part_ref), custom_call_target="tpu_custom_call" | custom-call | tf_op jit(solution)/shard_map/gather/pallas_call | solution.py:739
  920.3 22.8 %evaluate.1 = f32[8,128]{1,0:T(8,128)} custom-call(bf16[22272,768]{1,0:T(8,128)(2,1)} %bitcast.63, bf16[224,3072]{1,0:T(8,128)(2,1)} %bitcast.70, bf16[1000,512]{1,0:T(8,128)(2,1)} %refs_2_.3, s32[8,1]{1,0:T(8,128)} %scatter.24.refs_3_, f32[8,1]{1,0:T(8,128)} %pad_convert_fusion.refs_4_), custom_call_target="tpu_custom_call" | custom-call | tf_op jit(solution)/shard_map/evaluate/pallas_call | solution.py:606
  943.1 1.3 slice_reduce_fusion
  (63 shorter events, 17.7 us)
Async XLA Ops:
  7.2 5.8 copy-start.5
  7.2 9.1 copy-start.4
  7.2 704.3 %all-reduce.12.cloned.1.call-start = ((), (), s32[]{:S(2)}) async-start(), calls=%async_computation | async-start | bytes 8552448 | tf_op jit(solution)/shard_map/psum | solution.py:1202
  10.0 275.2 %collective-permute-start.1 = (bf16[448,3072]{1,0:T(8,128)(2,1)S(1)}, bf16[448,3072]{1,0:T(8,128)(2,1)}, u32[]{:S(2)}, u32[]{:S(2)}) collective-permute-start(bf16[448,3072]{1,0:T(8,128)(2,1)S(1)} %bitcast.71), channel_id=1, source_target_pairs={{0,0},{1,1},{2,16},{3,17},{4,8},{5,9},{6,24},{7,25},{8,4},{9,5},{1... | collective-permute-start | bytes 8257544 | tf_op jit(solution)/shard_map/ppermute | solution.py:1058
  13.2 90.6 %collective-permute-start.3 = (f32[8]{0:T(128)S(1)}, f32[8]{0:T(128)S(1)}, u32[]{:S(2)}, u32[]{:S(2)}) collective-permute-start(f32[8]{0:T(128)S(1)} %reshape.260), channel_id=1, source_target_pairs={{0,0},{1,1},{2,16},{3,17},{4,8},{5,9},{6,24},{7,25},{8,4},{9,5},{1... | collective-permute-start | bytes 104 | tf_op jit(solution)/shard_map/ppermute | solution.py:1058
  16.4 88.0 %collective-permute-start.2 = (s32[8]{0:T(128)S(1)}, s32[8]{0:T(128)S(1)}, u32[]{:S(2)}, u32[]{:S(2)}) collective-permute-start(s32[8]{0:T(128)S(1)} %reshape_squeeze.7), channel_id=1, source_target_pairs={{0,0},{1,1},{2,16},{3,17},{4,8},{5,9},{6,24},{7,25},{8,4},{9,5},{1... | collective-permute-start | bytes 104 | tf_op jit(solution)/shard_map/ppermute | solution.py:1058
  20.3 84.9 %collective-permute-start = (bf16[16,768]{1,0:T(8,128)(2,1)S(1)}, bf16[16,768]{1,0:T(8,128)(2,1)S(1)}, u32[]{:S(2)}, u32[]{:S(2)}) collective-permute-start(bf16[16,768]{1,0:T(8,128)(2,1)S(1)} %slice.117), channel_id=1, source_target_pairs={{0,1},{1,2},{2,3},{3,4},{4,5},{5,6},{6,7},{8,9},{9,10},{10,11},{11... | collective-permute-start | bytes 73736 | tf_op jit(solution)/shard_map/ppermute | solution.py:1064
  531.2 27.5 %collective-permute-start.4 = (bf16[16,768]{1,0:T(8,128)(2,1)S(1)}, bf16[16,768]{1,0:T(8,128)(2,1)S(1)}, u32[]{:S(2)}, u32[]{:S(2)}) collective-permute-start(bf16[16,768]{1,0:T(8,128)(2,1)S(1)} %slice.137), channel_id=1, source_target_pairs={{1,0},{2,1},{3,2},{4,3},{5,4},{6,5},{7,6},{9,8},{10,9},{11,10},{12... | collective-permute-start | bytes 73736 | tf_op jit(solution)/shard_map/ppermute | solution.py:1126
  554.6 4.2 slice-start
  555.2 3.6 slice-start.1
  558.7 10.5 %copy-start.1 = (bf16[2771,768]{1,0:T(8,128)(2,1)}, bf16[2771,768]{1,0:T(8,128)(2,1)S(1)}, u32[]{:S(2)}) copy-start(bf16[2771,768]{1,0:T(8,128)(2,1)S(1)} %slice.136) | copy-start | bytes 12768772
  603.3 17.9 %copy-start.3 = (s32[4]{0:T(128)S(1)}, s32[4]{0:T(128)}, u32[]{:S(2)}) copy-start(s32[4]{0:T(128)} %param.29) | copy-start | bytes 52
  620.4 1.5 copy-start.2
  723.4 5.5 copy-start
  723.4 5.5 collective-permute-start.5
Sparse Core Ops, SparseCore 0:
  620.5 90.9 all-reduce.11

commit v3 on v2

--- a/solution.py
+++ b/solution.py
@@ -37,6 +37,11 @@
 OUTER_MOM = 0.9
 GELU_SLOPE = 1.702
 SPARE = 13
+FIRST_SHARE = 0.6
+LOOK_AHEAD = 3
+PARCEL_STEP = 1
+REDUCE_HEAD = [4, 6]
+REDUCE_TAIL = [4]
 
 
 def layout_rows():
@@ -148,14 +153,16 @@
     return jnp.sum(jnp.where(keep[None], values.reshape(8, 16, D), 0.0), axis=1)
 
 
-def tower_kernel(images, with_grads, *refs):
+def tower_kernel(images, with_grads, carry, *refs):
     rows_all = images * TOKENS
     pairs = images // 2
-    (w_hbm, pix_hbm, text_ref, label_ref, live_ref), refs = refs[:5], refs[5:]
+    (w_hbm, pix_hbm, text_ref, note_ref), refs = refs[:4], refs[4:]
     if with_grads:
         (g_hbm, factor_ref, extra_ref), refs = refs[:3], refs[3:]
     else:
+        carried, refs = refs[:carry], refs[carry:]
         (loss_ref,), refs = refs[:1], refs[1:]
+        carried_out, refs = refs[:carry], refs[carry:]
     (wbuf, tail, table, pix, emb, hid0, mid0, hid1, acc, qkv, norm_a, norm_b, mixed, pre, act), refs = (
         refs[:15],
         refs[15:],
@@ -163,6 +170,8 @@
     (norm_c, kv), refs = refs[:2], refs[2:]
     if with_grads:
         (dhid, dqkv, gb, dmix, stage, stage_sem), refs = refs[:6], refs[6:]
+    elif carry:
+        (hold, hold_sems), refs = refs[:2], refs[2:]
     (wsem, small_sem) = refs
 
     layer_at = [FIRST_LAYER + index * (4 * D + 2 * FF) for index in range(LAYERS)]
@@ -177,6 +186,37 @@
         return pltpu.make_async_copy(
             w_hbm.at[pl.ds(order[index], BLOCK)], wbuf.at[slot_of[index]], wsem.at[slot_of[index]]
         )
+
+    hops = []
+    if carry:
+        piece = hold.shape[1]
+        for source, target in zip(carried, carried_out):
+            for start in range(0, source.shape[0], piece):
+                hops.append((source.at[pl.ds(start, piece)], target.at[pl.ds(start, piece)]))
+
+    def hop_in(index):
+        slot = index % 4
+        return pltpu.make_async_copy(hops[index][0], hold.at[slot], hold_sems.at[0, slot])
+
+    def hop_out(index):
+        slot = index % 4
+        return pltpu.make_async_copy(hold.at[slot], hops[index][1], hold_sems.at[1, slot])
+
+    hopped = [0]
+
+    def hop():
+        index = hopped[0]
+        if index < len(hops):
+            hop_in(index).wait()
+            hop_out(index).start()
+            if index >= 2:
+                hop_out(index - 2).wait()
+            if 2 <= index and index + 2 < len(hops):
+                hop_in(index + 2).start()
+        hopped[0] = index + 1
+
+    for index in range(min(4, len(hops))):
+        hop_in(index).start()
 
     load_pix = pltpu.make_async_copy(pix_hbm, pix, small_sem.at[0])
     load_tail = pltpu.make_async_copy(
@@ -224,6 +264,7 @@
     load_pix.wait()
     fetch(0).wait()
     emb[...] = dot(pix[...], wbuf[0])
+    hop()
     fetch(3).start()
     rows_table = table[...].astype(jnp.float32)
     added = pltpu.roll(rows_table, TABLE_ROWS - 2, 0)[:TOKENS]
@@ -242,6 +283,7 @@
         hid0[rows, :] = unit * gain + bias
 
     layer_norm_into(hid0, norm_a, 2)
+    hop()
     fetch(1).wait()
 
     @pl.loop(0, 3)
@@ -250,6 +292,7 @@
         qkv[:, at] = low(dot(norm_a[...], wbuf[1, at, :]))
 
     bias_pair = pair_bias()
+    hop()
 
     def lanes(part, group):
         return slice(part * D + group * 256, part * D + (group + 1) * 256)
@@ -269,8 +312,10 @@
             mixed[rows, lanes(0, group)] = low(fold_heads(out))
 
     acc[...] = dot(mixed[...], wbuf[1, 3 * D : 4 * D, :])
+    hop()
     fetch(4).start()
     gain2, bias2 = norm_row(4), norm_row(5)
+    hop()
 
     @chunks_of()
     def _(index):
@@ -292,9 +337,11 @@
 
     fetch(5).start()
     fetch(3).wait()
+    hop()
     acc[...] = dot(act[...], wbuf[0])
     fetch(6).start()
     gain3, bias3 = norm_row(6), norm_row(7)
+    hop()
 
     @chunks_of()
     def _(index):
@@ -313,6 +360,7 @@
         )
 
     class_hid = class_rows(hid1)
+    hop()
     unit_one, _ = norm_parts(class_hid)
     class_a = low(wide(unit_one * gain3 + bias3, 16))
     class_q = low(dot(class_a, wbuf[1, 0:D, :]))
@@ -329,19 +377,23 @@
         outs.append(jnp.zeros((32, D), jnp.float32))
     class_mix = low(wide(unspread_heads(jnp.concatenate(outs, axis=0)), 16))
     class_mid = class_hid + dot(class_mix, wbuf[1, 3 * D : 4 * D, :])[:8]
+    hop()
     unit_two, _ = norm_parts(class_mid)
     gain4, bias4 = norm_row(8), norm_row(9)
     class_b = low(wide(unit_two * gain4 + bias4, 16))
     fetch(5).wait()
     class_pre = dot(class_b, wbuf[2], 1, 1)
+    hop()
     gate = jax.nn.sigmoid(GELU_SLOPE * class_pre)
     class_act = low(class_pre * gate)
     fetch(6).wait()
     class_out = class_mid + dot(class_act, wbuf[0])[:8]
+    hop()
     gain5, bias5 = norm_row(10), norm_row(11)
     unit_post, _ = norm_parts(class_out)
     pooled = low(wide(unit_post * gain5 + bias5, 16))
 
+    hop()
     pooled_out = dot(pooled, tail[...], 1, 1)
     pooled_out = jnp.concatenate([pooled_out, jnp.zeros((16, 640 - TAIL_ROWS), jnp.float32)], axis=1)
     embedded = pltpu.roll(pooled_out, 640 - HEAD_AT, 1)[:8, :EMB]
@@ -352,11 +404,16 @@
     log_total = top + jnp.log(jnp.sum(jnp.exp(logits - top), -1, keepdims=True))
     log_probs = logits - log_total
     classes = lax.broadcasted_iota(jnp.int32, logits.shape, 1)
-    target = jnp.where(classes == label_ref[...], 1.0 - SMOOTH, 0.0) + SMOOTH / CLASSES
-    live = live_ref[...]
+    label = note_ref[:, 0:1].astype(jnp.int32)
+    target = jnp.where(classes == label, 1.0 - SMOOTH, 0.0) + SMOOTH / CLASSES
+    live = note_ref[:, 1:2]
     losses = -live * jnp.sum(target * log_probs, -1, keepdims=True)
     if not with_grads:
         loss_ref[...] = jnp.broadcast_to(losses, loss_ref.shape)
+        while hopped[0] < len(hops):
+            hop()
+        for index in range(max(0, len(hops) - 2), len(hops)):
+            hop_out(index).wait()
         return
 
     grad_raw = low(wide(LOGIT_SCALE * ((jnp.exp(log_probs) - target) * live), 16))
@@ -553,12 +610,15 @@
         push(slot, 0).wait()
 
 
-def run_tower(weights, pixel_rows, label_row, live_mask, text, with_grads):
-    images = label_row.shape[0]
-    rows_all = images * TOKENS
+def image_notes(label_row, live_mask):
+    notes = jnp.stack([label_row.astype(jnp.float32), live_mask], axis=1)
+    return jnp.pad(notes, ((0, 8 - notes.shape[0]), (0, 126)))
+
+
+def run_tower(weights, pixel_rows, notes, text, with_grads, carried=()):
+    rows_all = pixel_rows.shape[0]
+    images = rows_all // TOKENS
     bf16, f32 = jnp.bfloat16, jnp.float32
-    labels = jnp.zeros((8, 1), jnp.int32).at[:images, 0].set(label_row)
-    live = jnp.zeros((8, 1), f32).at[:images, 0].set(live_mask)
     scratch = [
         pltpu.VMEM((3, BLOCK, D), bf16),
         pltpu.VMEM((TAIL_ROWS, D), bf16),
@@ -598,20 +658,32 @@
             pl.BlockSpec(memory_space=pltpu.VMEM),
         )
     else:
-        out_shape = jax.ShapeDtypeStruct((8, 128), f32)
-        out_specs = pl.BlockSpec(memory_space=pltpu.VMEM)
+        out_shape = (jax.ShapeDtypeStruct((8, 128), f32),)
+        out_shape += tuple(jax.ShapeDtypeStruct(array.shape, array.dtype) for array in carried)
+        out_specs = (pl.BlockSpec(memory_space=pltpu.VMEM),)
+        out_specs += (pl.BlockSpec(memory_space=pl.ANY),) * len(carried)
+        if carried:
+            scratch += [
+                pltpu.VMEM((4, carried[0].shape[0] // 6, carried[0].shape[1]), carried[0].dtype),
+                pltpu.SemaphoreType.DMA((2, 4)),
+            ]
     scratch += [pltpu.SemaphoreType.DMA((3,)), pltpu.SemaphoreType.DMA((3,))]
     vmem = pl.BlockSpec(memory_space=pltpu.VMEM)
     hbm = pl.BlockSpec(memory_space=pl.ANY)
     return pl.pallas_call(
-        functools.partial(tower_kernel, images, with_grads),
+        functools.partial(tower_kernel, images, with_grads, len(carried)),
         out_shape=out_shape,
-        in_specs=[hbm, hbm, vmem, vmem, vmem],
+        in_specs=[hbm, hbm, vmem, vmem] + [hbm] * len(carried),
         out_specs=out_specs,
         scratch_shapes=scratch,
         compiler_params=pltpu.CompilerParams(vmem_limit_bytes=60 * 2**20),
+        cost_estimate=pl.CostEstimate(
+            flops=(6 if with_grads else 2) * rows_all * weights.shape[0] * D,
+            bytes_accessed=2 * weights.shape[0] * D,
+            transcendentals=rows_all * 2 * FF,
+        ),
         name="train" if with_grads else "evaluate",
-    )(weights, pixel_rows, text, labels, live)
+    )(weights, pixel_rows, text, notes, *carried)
 
 
 def grad_rows_kept(rows):
@@ -635,19 +707,40 @@
     return (y * 2 + c, z * 2 + x)
 
 
-def chunk_rows(total, count):
+def chunk_rows(total, share):
     units = total // 16
+    sizes = [3, 4] + [6] * ((units - 15) // 6) + [4, 4 + (units - 15) % 6]
     chunks = []
-    start = 0
-    for index in range(count):
-        size = units * (index + 1) // count - units * index // count
-        first = size // 2 if index % 2 else size - size // 2
+    start = taken = 0
+    for size in sizes:
+        first = int(round((start + size) * share)) - taken
+        taken += first
         chunks.append((start * 16, first * 16, (size - first) * 16))
         start += size
     return chunks
 
 
-def gather_kernel(chunks, part_ref, full_ref, local_sem, sends, recvs):
+def image_device():
+    y, c, z, x = place()
+    return device_at((z + c) % 2, z // 2, 2 * c + y, x)
+
+
+def image_source():
+    y, c, z, x = place()
+    return device_at(z % 2, z // 2, 2 * c + (y + z // 2) % 2, x)
+
+
+def gather_kernel(chunks, images, *refs):
+    if images:
+        (part_ref, pixel_ref, note_ref, full_ref, moved_ref, moved_note_ref), refs = refs[:6], refs[6:]
+        (local_sem, sends, recvs, pixel_sems) = refs
+        count = pixel_ref.shape[0] // TOKENS
+        parcels = [(note_ref, moved_note_ref)]
+        for index in range(count):
+            rows = pl.ds(index * TOKENS, TOKENS)
+            parcels.append((pixel_ref.at[rows], moved_ref.at[rows]))
+    else:
+        (part_ref, full_ref, local_sem, sends, recvs) = refs
     half_cols = part_ref.shape[1]
     y, c, z, x = place()
     cols = pl.ds(pl.multiple_of(c * half_cols, half_cols), half_cols)
@@ -655,12 +748,27 @@
     over_y = device_at(1 - y, c, z, x)
     sibling = device_at(y, 1 - c, z, x)
     along_z = [device_at(y, c, (z + step) % 4, x) for step in (1, 2, 3)]
+    target = image_device()
+    stays = jnp.logical_and(target[0] == y * 2 + c, target[1] == z * 2 + x)
     barrier = pltpu.get_barrier_semaphore()
     for other in [over_x, over_y, sibling] + along_z:
         pl.semaphore_signal(barrier, inc=1, device_id=other, device_id_type=MESH)
-    local = pltpu.make_async_copy(part_ref, full_ref.at[z, x, y, :, cols], local_sem)
-    local.start()
-    pl.semaphore_wait(barrier, 6)
+    if images:
+
+        @pl.when(jnp.logical_not(stays))
+        def _():
+            pl.semaphore_signal(barrier, inc=1, device_id=image_source(), device_id_type=MESH)
+
+    def keep(index):
+        start, first, second = chunks[index]
+        rows = pl.ds(start, first + second)
+        return pltpu.make_async_copy(
+            part_ref.at[rows], full_ref.at[z, x, y, rows, cols], local_sem.at[index]
+        )
+
+    for index in range(len(chunks)):
+        keep(index).start()
+    pl.semaphore_wait(barrier, 6 + (jnp.where(stays, 0, 1) if images else 0))
 
     def send(piece, other, stage, index):
         pltpu.make_async_remote_copy(
@@ -671,6 +779,24 @@
             device_id=other,
             device_id_type=MESH,
         ).start()
+
+    def move_parcel(which):
+        source, place_at = parcels[which]
+
+        @pl.when(stays)
+        def _():
+            pltpu.make_async_copy(source, place_at, pixel_sems.at[0, which]).start()
+
+        @pl.when(jnp.logical_not(stays))
+        def _():
+            pltpu.make_async_remote_copy(
+                src_ref=source,
+                dst_ref=place_at,
+                send_sem=pixel_sems.at[1, which],
+                recv_sem=pixel_sems.at[0, which],
+                device_id=target,
+                device_id_type=MESH,
+            ).start()
 
     def arrived(piece, stage, index):
         pltpu.make_async_copy(piece, piece, recvs.at[stage, index]).wait()
@@ -693,25 +819,32 @@
         }
 
     total = len(chunks)
-    for step in range(total + 5):
-        if step < total:
-            start, first, second = chunks[step]
-            rows = pl.ds(start, first + second)
-            for other in along_z:
-                pltpu.make_async_remote_copy(
-                    src_ref=part_ref.at[rows],
-                    dst_ref=full_ref.at[z, x, y, rows, cols],
-                    send_sem=sends.at[0, step],
-                    recv_sem=recvs.at[0, step],
-                    device_id=other,
-                    device_id_type=MESH,
-                ).start()
-        if step == 0:
-            local.wait()
+
+    def send_along_z(index):
+        start, first, second = chunks[index]
+        rows = pl.ds(start, first + second)
+        for other in along_z:
+            pltpu.make_async_remote_copy(
+                src_ref=part_ref.at[rows],
+                dst_ref=full_ref.at[z, x, y, rows, cols],
+                send_sem=sends.at[0, index],
+                recv_sem=recvs.at[0, index],
+                device_id=other,
+                device_id_type=MESH,
+            ).start()
+
+    ahead = LOOK_AHEAD if images else 1
+    for step in range(total + 3):
+        for index in range(ahead) if step == 0 else [step + ahead - 1]:
+            if index < total:
+                send_along_z(index)
+        if images and step % PARCEL_STEP == 0 and step // PARCEL_STEP < len(parcels):
+            move_parcel(step // PARCEL_STEP)
         index = step - 1
         if 0 <= index < total:
             block = pieces(index)
             arrived(block[0], 0, index)
+            keep(index).wait()
             send(block[1], over_y, 1, index)
             send(block[2], over_x, 2, index)
         index = step - 2
@@ -732,24 +865,54 @@
         arrived(block[5], 5, index)
         for stage in range(6):
             sent(block[stage], stage, index)
-
-
-def gather_rows(part, shard_rows):
-    chunks = chunk_rows(part.shape[0], 8)
-    full = pl.pallas_call(
-        functools.partial(gather_kernel, chunks),
-        out_shape=jax.ShapeDtypeStruct((4, 2, 2, part.shape[0], 2 * part.shape[1]), part.dtype),
-        in_specs=[pl.BlockSpec(memory_space=pl.ANY)],
-        out_specs=pl.BlockSpec(memory_space=pl.ANY),
-        scratch_shapes=[
-            pltpu.SemaphoreType.DMA,
-            pltpu.SemaphoreType.DMA((6, len(chunks))),
-            pltpu.SemaphoreType.DMA((6, len(chunks))),
-        ],
-        compiler_params=pltpu.CompilerParams(collective_id=0, has_side_effects=True),
-        name="gather",
-    )(part)
-    return full.reshape(8 * shard_rows, 2 * part.shape[1])
+    if images:
+        for which, (_, place_at) in enumerate(parcels):
+            pltpu.make_async_copy(place_at, place_at, pixel_sems.at[0, which]).wait()
+
+        @pl.when(jnp.logical_not(stays))
+        def _():
+            for which, (_, place_at) in enumerate(parcels):
+                pltpu.make_async_copy(place_at, place_at, pixel_sems.at[1, which]).wait()
+
+
+def gather_rows(part, shard_rows, pixel_rows=None, notes=None):
+    images = pixel_rows is not None
+    chunks = chunk_rows(part.shape[0], FIRST_SHARE if images else 0.5)
+    hbm = pl.BlockSpec(memory_space=pl.ANY)
+    width = 2 * part.shape[1]
+    full_shape = jax.ShapeDtypeStruct((4, 2, 2, part.shape[0], width), part.dtype)
+    semaphores = [
+        pltpu.SemaphoreType.DMA((len(chunks),)),
+        pltpu.SemaphoreType.DMA((6, len(chunks))),
+        pltpu.SemaphoreType.DMA((6, len(chunks))),
+    ]
+    kernel = functools.partial(gather_kernel, chunks, images)
+    if not images:
+        full = pl.pallas_call(
+            kernel,
+            out_shape=full_shape,
+            in_specs=[hbm],
+            out_specs=hbm,
+            scratch_shapes=semaphores,
+            compiler_params=pltpu.CompilerParams(collective_id=0, has_side_effects=True),
+            name="gather",
+        )(part)
+        return full.reshape(8 * shard_rows, width)
+    full, moved, moved_notes = pl.pallas_call(
+        kernel,
+        out_shape=(
+            full_shape,
+            jax.ShapeDtypeStruct(pixel_rows.shape, pixel_rows.dtype),
+            jax.ShapeDtypeStruct(notes.shape, notes.dtype),
+        ),
+        in_specs=[hbm, hbm, hbm],
+        out_specs=[hbm, hbm, hbm],
+        scratch_shapes=semaphores
+        + [pltpu.SemaphoreType.DMA((2, 1 + pixel_rows.shape[0] // TOKENS))],
+        compiler_params=pltpu.CompilerParams(collective_id=2, has_side_effects=True),
+        name="gather_first",
+    )(part, pixel_rows, notes)
+    return (full.reshape(8 * shard_rows, width), moved, moved_notes)
 
 
 def reduce_kernel(
@@ -761,16 +924,22 @@
     own_ref,
     factors_ref,
     extras_ref,
+    squares_ref,
     mine,
     first_sum,
     sum_a,
     sum_b,
     last_sum,
+    squares,
+    passed_factor,
+    passed_extra,
     load_sems,
     sends,
     recvs,
     small_sends,
     small_recvs,
+    pass_sends,
+    pass_recvs,
 ):
     half_cols = mine.shape[-1]
     planes = grad_ref.shape[0]
@@ -855,22 +1024,20 @@
     pl.semaphore_wait(barrier, 3 + jnp.where(at_home, 7, 8))
     send_core(0)
     send_core(1)
-    slot = (y * 2 + c) * 2 + x
-    for other in range(8):
-        other_z, other_x = other // 2, other % 2
-        itself = jnp.logical_and(at_home, jnp.logical_and(z == other_z, x == other_x))
-        for which, (source, target) in enumerate(
-            ((extra_ref, extras_ref.at[slot]), (factor_ref, factors_ref.at[slot]))
-        ):
-            if which == 1 and other_z < low_from:
-                continue
+    def slot_of(from_y):
+        return (from_y * 2 + c) * 2 + x
+
+    def to_owners(source, target, which, first_z, way):
+        for other in range(2 * first_z, 8):
+            other_z, other_x = other // 2, other % 2
+            itself = jnp.logical_and(at_home, jnp.logical_and(z == other_z, x == other_x))
 
             @pl.when(jnp.logical_not(itself))
             def _():
                 pltpu.make_async_remote_copy(
                     src_ref=source,
                     dst_ref=target,
-                    send_sem=small_sends.at[which],
+                    send_sem=small_sends.at[way, which],
                     recv_sem=small_recvs.at[which],
                     device_id=device_at(home_y, home_c, other_z, other_x),
                     device_id_type=MESH,
@@ -879,6 +1046,50 @@
             @pl.when(itself)
             def _():
                 pltpu.make_async_copy(source, target, small_recvs.at[which]).start()
+
+    def passing(which):
+        source, target = ((extra_ref, passed_extra), (factor_ref, passed_factor))[which]
+        return pltpu.make_async_remote_copy(
+            src_ref=source,
+            dst_ref=target,
+            send_sem=pass_sends.at[which],
+            recv_sem=pass_recvs.at[which],
+            device_id=over_y,
+            device_id_type=MESH,
+        )
+
+    gives = y != home_y
+
+    @pl.when(gives)
+    def _():
+        for which in range(2):
+            passing(which).start()
+
+    @pl.when(jnp.logical_not(gives))
+    def _():
+        to_owners(extra_ref, extras_ref.at[slot_of(y)], 0, 0, 0)
+        to_owners(factor_ref, factors_ref.at[slot_of(y)], 1, low_from, 0)
+
+    def pass_on():
+        @pl.when(jnp.logical_not(gives))
+        def _():
+            for which in range(2):
+                passing(which).wait_recv()
+            to_owners(passed_extra, extras_ref.at[slot_of(1 - y)], 0, 0, 1)
+            to_owners(passed_factor, factors_ref.at[slot_of(1 - y)], 1, low_from, 1)
+
+    squares[...] = jnp.zeros_like(squares)
+    half_rows = grad_ref.shape[3]
+    last_layer = FIRST_LAYER + 4 * D + 2 * FF
+
+    def add_squares(block, rows):
+        values = last_sum[block, rows].astype(jnp.float32)
+        row = ((block * 2 + x) * 2 + y) * half_rows + rows.start
+        row = row + lax.broadcasted_iota(jnp.int32, values.shape, 0)
+        values = jnp.where(dense_row(row), values * values, 0.0)
+        values = jnp.sum(values.reshape(rows.size // 8, 8, half_cols), axis=0)
+        for part in range(half_cols // 128):
+            squares[...] += values[:, part * 128 : (part + 1) * 128]
 
     for step in range(total + 4):
         index = step
@@ -899,6 +1110,8 @@
                     mine.at[index % 2, zz, rest // 2, rest % 2, pl.ds(0, rows.size)],
                 )
 
+            if index == 1:
+                pass_on()
             send(first_sum.at[:, 1 - x, :, rows_a], sum_a.at[:, :, in_a], over_x, 1, index)
             send(first_sum.at[:, :, 1 - y, rows_b], sum_b.at[:, :, in_b], over_y, 2, index)
         index = step - 1
@@ -934,11 +1147,12 @@
             def _(block):
                 add(last_sum.at[block, rows_a], sum_a.at[block, y, in_a])
                 add(last_sum.at[block, rows_b], sum_b.at[block, x, in_b])
+                add_squares(block, rows)
 
             for to_z in range(planes):
                 itself = jnp.logical_and(at_home, z == to_z)
                 source = last_sum.at[to_z, rows]
-                target = own_ref.at[y, rows, my_cols]
+                target = own_ref.at[pl.ds(pl.multiple_of(y * half_rows + rows.start, 16), rows.size), my_cols]
 
                 @pl.when(jnp.logical_not(itself))
                 def _():
@@ -948,12 +1162,13 @@
                 def _():
                     pltpu.make_async_copy(source, target, recvs.at[5, index]).start()
 
+    to_owners(squares, squares_ref.at[slot_of(y)], 2, 0, 0)
     for index in range(total):
         rows, rows_a, rows_b, in_a, in_b = spans(index)
 
         @pl.when(z < planes)
         def _():
-            arrived(own_ref.at[:, rows], 5, index)
+            arrived(own_ref.at[pl.ds(0, 2 * rows.size)], 5, index)
 
         sent(first_sum.at[:, :, :, rows], 0, index)
         sent(sum_a.at[:, :, in_a], 1, index)
@@ -976,69 +1191,87 @@
         pltpu.make_async_copy(piece, piece, sem).wait()
 
     all_of(extras_ref, 8, small_recvs.at[0])
+    all_of(squares_ref, 8, small_recvs.at[2])
 
     @pl.when(z >= low_from)
     def _():
         all_of(factors_ref, 8, small_recvs.at[1])
 
-    @pl.when(at_home)
+    def sent_to_owners(ref, count, kept, which, way):
+        @pl.when(kept)
+        def _():
+            all_of(ref, count - 1, small_sends.at[way, which])
+
+        @pl.when(jnp.logical_not(kept))
+        def _():
+            all_of(ref, count, small_sends.at[way, which])
+
+    sent_to_owners(squares_ref, 8, at_home, 2, 0)
+
+    @pl.when(gives)
     def _():
-        all_of(extras_ref, 7, small_sends.at[0])
-
-    @pl.when(jnp.logical_not(at_home))
+        for which in range(2):
+            passing(which).wait_send()
+
+    @pl.when(jnp.logical_not(gives))
     def _():
-        all_of(extras_ref, 8, small_sends.at[0])
-
-    low_targets = 2 * (4 - low_from)
-    low_kept = jnp.logical_and(at_home, z >= low_from)
-
-    @pl.when(low_kept)
-    def _():
-        all_of(factors_ref, low_targets - 1, small_sends.at[1])
-
-    @pl.when(jnp.logical_not(low_kept))
-    def _():
-        all_of(factors_ref, low_targets, small_sends.at[1])
-
-
-def reduce_chunks(total, count, share):
+        low_kept = jnp.logical_and(at_home, z >= low_from)
+        for way in range(2):
+            sent_to_owners(extras_ref, 8, at_home, 0, way)
+            sent_to_owners(factors_ref, 2 * (4 - low_from), low_kept, 1, way)
+
+
+def reduce_chunks(total, share):
     units = total // 16
+    middle = units - sum(REDUCE_HEAD + REDUCE_TAIL)
+    sizes = [8] * (middle // 8)
+    sizes[-1] += middle % 8
+    sizes = REDUCE_HEAD + sizes + REDUCE_TAIL
     chunks = []
-    start = 0
-    for index in range(count):
-        size = units * (index + 1) // count - units * index // count
-        first = int(round(size * share))
+    start = taken = 0
+    for size in sizes:
+        first = int(round((start + size) * share)) - taken
+        taken += first
         chunks.append((start * 16, first * 16, (size - first) * 16))
         start += size
     return chunks
 
 
+def low_plane(shard_rows):
+    return (FIRST_LAYER + 4 * D + 2 * FF) // (2 * shard_rows)
+
+
 def sum_on_plane(grad_rows, factors, extra, shard_rows):
     half_rows, width = shard_rows // 2, grad_rows.shape[1]
     planes = grad_rows.shape[0] // (2 * shard_rows)
-    chunks = reduce_chunks(half_rows, 8, 0.75)
+    chunks = reduce_chunks(half_rows, 0.75)
     most = max(first + second for _, first, second in chunks)
     half_cols = width // 2
     dtype = grad_rows.dtype
-    low_from = (FIRST_LAYER + 4 * D + 2 * FF) // (2 * shard_rows)
-    own, all_factors, all_extra = pl.pallas_call(
-        functools.partial(reduce_kernel, chunks, low_from),
+    return pl.pallas_call(
+        functools.partial(reduce_kernel, chunks, low_plane(shard_rows)),
         out_shape=(
-            jax.ShapeDtypeStruct((2, half_rows, width), dtype),
+            jax.ShapeDtypeStruct((shard_rows + 16, width), dtype),
             jax.ShapeDtypeStruct((8,) + factors.shape, factors.dtype),
             jax.ShapeDtypeStruct((8,) + extra.shape, extra.dtype),
+            jax.ShapeDtypeStruct((8, 8, 128), jnp.float32),
         ),
         in_specs=[pl.BlockSpec(memory_space=pl.ANY)] * 3,
-        out_specs=[pl.BlockSpec(memory_space=pl.ANY)] * 3,
+        out_specs=[pl.BlockSpec(memory_space=pl.ANY)] * 4,
         scratch_shapes=[
             pltpu.VMEM((2, planes, 2, 2, most, half_cols), dtype),
             pltpu.VMEM((planes, 2, 2, half_rows, half_cols), dtype),
             pltpu.VMEM((planes, 2, sum(chunk[1] for chunk in chunks), half_cols), dtype),
             pltpu.VMEM((planes, 2, sum(chunk[2] for chunk in chunks), half_cols), dtype),
             pltpu.VMEM((planes, half_rows, half_cols), dtype),
+            pltpu.VMEM((8, 128), jnp.float32),
+            pltpu.VMEM(factors.shape, factors.dtype),
+            pltpu.VMEM(extra.shape, extra.dtype),
             pltpu.SemaphoreType.DMA((2,)),
             pltpu.SemaphoreType.DMA((6, len(chunks))),
             pltpu.SemaphoreType.DMA((6, len(chunks))),
+            pltpu.SemaphoreType.DMA((2, 3)),
+            pltpu.SemaphoreType.DMA((3,)),
             pltpu.SemaphoreType.DMA((2,)),
             pltpu.SemaphoreType.DMA((2,)),
         ],
@@ -1047,18 +1280,323 @@
         ),
         name="reduce",
     )(grad_rows.reshape(planes, 2, 2, half_rows, width), factors, extra)
-    return (own.reshape(shard_rows, width), all_factors, all_extra)
-
-
-def to_planes(values):
+
+
+def update_kernel(
+    shape,
+    own_hbm,
+    rest_hbm,
+    master_hbm,
+    first_hbm,
+    second_hbm,
+    factors_ref,
+    extras_ref,
+    squares_ref,
+    first_out,
+    second_out,
+    total_out,
+    summary_ref,
+    own,
+    rest,
+    weights,
+    first,
+    second,
+    new_first,
+    new_second,
+    mine,
+    other,
+    core_in,
+    y_out,
+    y_in,
+    load_sems,
+    store_sems,
+    sends,
+    recvs,
+    total_sem,
+    low_squares_ref,
+    low_sems,
+):
+    half_rows, piece, pieces, low_from = shape
+    half_cols = mine.shape[-1]
+    y, c, z, x = place()
+    over_y = device_at(1 - y, c, z, x)
+    sibling = device_at(y, 1 - c, z, x)
+    barrier = pltpu.get_barrier_semaphore()
+    for partner in (over_y, sibling):
+        pl.semaphore_signal(barrier, inc=1, device_id=partner, device_id_type=MESH)
+    has_factors = z >= low_from
+
+    @pl.when(z < 4 - low_from)
+    def _():
+        pl.semaphore_signal(
+            barrier, inc=1, device_id=device_at(y, c, z + low_from, x), device_id_type=MESH
+        )
+
+    def row_at(index):
+        half = jnp.where(index < pieces, 1 - y, y)
+        return pl.multiple_of(half * half_rows + index % pieces * piece, 16)
+
+    def loads(index):
+        slot = index % 2
+        rows = pl.ds(row_at(index), piece)
+        longer = pl.ds(row_at(index), piece + 16)
+        return [
+            pltpu.make_async_copy(own_hbm.at[longer], own.at[slot], load_sems.at[0, slot]),
+            pltpu.make_async_copy(rest_hbm.at[rows], rest.at[slot], load_sems.at[1, slot]),
+            pltpu.make_async_copy(master_hbm.at[rows], weights.at[slot], load_sems.at[2, slot]),
+            pltpu.make_async_copy(first_hbm.at[rows], first.at[slot], load_sems.at[3, slot]),
+            pltpu.make_async_copy(second_hbm.at[rows], second.at[slot], load_sems.at[4, slot]),
+        ]
+
+    def stores(index):
+        slot = index % 2
+        rows = pl.ds(row_at(index), piece)
+        return [
+            pltpu.make_async_copy(new_first.at[slot], first_out.at[rows], store_sems.at[0, slot]),
+            pltpu.make_async_copy(new_second.at[slot], second_out.at[rows], store_sems.at[1, slot]),
+        ]
+
+    for copy in loads(0):
+        copy.start()
+
+    def gram(at, width):
+        values = factors_ref[:, :, at : at + width].reshape(128, width)
+        return dot(values, values, 1, 1)
+
+    row = lax.broadcasted_iota(jnp.int32, (128, 128), 0) % 16
+    col = lax.broadcasted_iota(jnp.int32, (128, 128), 1) % 16
+    head = gram(FF + 3 * D, D)
+    shifted_head = pltpu.roll(pltpu.roll(head, 120, 0), 120, 1)
+    products = gram(0, FF) * gram(FF + 2 * D, D) + gram(FF, D) * gram(FF + D, D)
+    low_squares = jnp.where(row // 8 == col // 8, products, 0.0)
+    low_squares = low_squares + jnp.where((row < 8) & (col < 8), head * shifted_head, 0.0)
+    pl.semaphore_wait(barrier, 2 + jnp.where(has_factors, 1, 0))
+    to_low = pltpu.make_async_remote_copy(
+        src_ref=low_squares_ref,
+        dst_ref=low_squares_ref,
+        send_sem=low_sems.at[0],
+        recv_sem=low_sems.at[1],
+        device_id=device_at(y, c, z - low_from, x),
+        device_id_type=MESH,
+    )
+
+    @pl.when(has_factors)
+    def _():
+        low_squares_ref[...] = jnp.sum(low_squares.reshape(16, 8, 128), axis=0)
+        to_low.start()
+
+    @pl.when(jnp.logical_not(has_factors))
+    def _():
+        to_low.wait_recv()
+
+    extra = jnp.sum(extras_ref[...], axis=0)
+    norm_squares = extra[:HEAD_AT] * extra[:HEAD_AT]
+    square_all = jnp.sum(squares_ref[...]) + jnp.sum(low_squares_ref[...]) + jnp.sum(norm_squares)
+    count_all = extra[12:13, 1:2]
+    grad_norm = jnp.sqrt(jnp.zeros((1, 1), jnp.float32) + square_all) / count_all
+    factor = CLIP_MAX / jnp.maximum(grad_norm, CLIP_MAX) / count_all
+    summary_ref[...] = extra
+    summary_ref[10:12, :] = extra[10:12] * factor
+    summary_ref[13:14, :] = jnp.broadcast_to(grad_norm, (1, D))
+
+    flat_start = (z * 2 + x) * (2 * half_rows)
+    layer_start = BLOCK + SEQ + 1
+
+    def step(index):
+        slot = index % 2
+        for copy in loads(index):
+            copy.wait()
+
+        @pl.loop(0, piece // 16)
+        def _(block):
+            at = pl.multiple_of(block * 16, 16)
+            rows = pl.ds(at, 16)
+            longer = own[slot, pl.ds(at, 32), :].astype(jnp.float32)
+            flat = flat_start + row_at(index) + at + lax.broadcasted_iota(jnp.int32, (16, D), 0)
+            grads = jnp.where(flat < layer_start, longer[:16], longer[SPARE : SPARE + 16])
+            spared = jnp.where(flat < layer_start, flat, flat + SPARE)
+            grads = jnp.where(dense_row(spared), grads, rest[slot, rows, :].astype(jnp.float32))
+            clipped = grads * factor
+            moment_one = BETA_ONE * first[slot, rows, :] + (1.0 - BETA_ONE) * clipped
+            moment_two = BETA_TWO * second[slot, rows, :] + (1.0 - BETA_TWO) * clipped * clipped
+            new_first[slot, rows, :] = moment_one
+            new_second[slot, rows, :] = moment_two
+            corrected_one = moment_one * (1.0 / (1.0 - BETA_ONE**STEP))
+            corrected_two = moment_two * (1.0 / (1.0 - BETA_TWO**STEP))
+            change = corrected_one / (jnp.sqrt(corrected_two) + ADAM_EPS) + DECAY * weights[slot, rows, :]
+            change = low(RATE * change)
+            left, right = change[:, :half_cols], change[:, half_cols:]
+            mine[index, rows, :] = jnp.where(c == 0, left, right)
+            other[index, rows, :] = jnp.where(c == 0, right, left)
+
+        for copy in stores(index):
+            copy.start()
+        pltpu.make_async_remote_copy(
+            src_ref=other.at[index],
+            dst_ref=core_in.at[index],
+            send_sem=sends.at[index],
+            recv_sem=recvs.at[index],
+            device_id=sibling,
+            device_id_type=MESH,
+        ).start()
+
+    def fold(index):
+        pltpu.make_async_copy(core_in.at[index], core_in.at[index], recvs.at[index]).wait()
+        total = mine[index].astype(jnp.float32) + core_in[index].astype(jnp.float32)
+        if index < pieces:
+            y_out[index] = low(total)
+            pltpu.make_async_remote_copy(
+                src_ref=y_out.at[index],
+                dst_ref=y_in.at[index],
+                send_sem=sends.at[2 * pieces + index],
+                recv_sem=recvs.at[2 * pieces + index],
+                device_id=over_y,
+                device_id_type=MESH,
+            ).start()
+        else:
+            mine[index] = low(total)
+
+    steps = 2 * pieces
+    for index in range(steps):
+        if index + 1 < steps:
+            if index >= 1:
+                for copy in stores(index - 1):
+                    copy.wait()
+            for copy in loads(index + 1):
+                copy.start()
+        step(index)
+        if index >= 1:
+            fold(index - 1)
+    fold(steps - 1)
+
+    def hand_over(index):
+        rows = pl.ds(index * piece, piece)
+        return pltpu.make_async_copy(mine.at[pieces + index], total_out.at[rows], total_sem.at[index])
+
+    for index in range(pieces):
+        at = 2 * pieces + index
+        pltpu.make_async_copy(y_in.at[index], y_in.at[index], recvs.at[at]).wait()
+        total = mine[pieces + index].astype(jnp.float32) + y_in[index].astype(jnp.float32)
+        mine[pieces + index] = low(total)
+        hand_over(index).start()
+    for index in range(steps - 2, steps):
+        for copy in stores(index):
+            copy.wait()
+    for index in range(steps):
+        pltpu.make_async_copy(other.at[index], other.at[index], sends.at[index]).wait()
+    for index in range(pieces):
+        pltpu.make_async_copy(y_out.at[index], y_out.at[index], sends.at[steps + index]).wait()
+        hand_over(index).wait()
+
+    @pl.when(has_factors)
+    def _():
+        to_low.wait_send()
+
+
+def update_rows(own, rest, master, first, second, factors, extras, squares):
+    rows, width = master.shape
+    half_rows, half_cols = rows // 2, width // 2
+    pieces = 3
+    piece = half_rows // pieces
+    f32, bf16 = jnp.float32, jnp.bfloat16
+    hbm = pl.BlockSpec(memory_space=pl.ANY)
+    vmem = pl.BlockSpec(memory_space=pltpu.VMEM)
+    return pl.pallas_call(
+        functools.partial(update_kernel, (half_rows, piece, pieces, low_plane(rows))),
+        out_shape=(
+            jax.ShapeDtypeStruct((rows, width), f32),
+            jax.ShapeDtypeStruct((rows, width), f32),
+            jax.ShapeDtypeStruct((half_rows, half_cols), bf16),
+            jax.ShapeDtypeStruct((16, width), f32),
+        ),
+        in_specs=[hbm] * 5 + [vmem] * 3,
+        out_specs=[hbm] * 3 + [vmem],
+        scratch_shapes=[
+            pltpu.VMEM((2, piece + 16, width), bf16),
+            pltpu.VMEM((2, piece, width), bf16),
+            pltpu.VMEM((2, piece, width), f32),
+            pltpu.VMEM((2, piece, width), f32),
+            pltpu.VMEM((2, piece, width), f32),
+            pltpu.VMEM((2, piece, width), f32),
+            pltpu.VMEM((2, piece, width), f32),
+            pltpu.VMEM((2 * pieces, piece, half_cols), bf16),
+            pltpu.VMEM((2 * pieces, piece, half_cols), bf16),
+            pltpu.VMEM((2 * pieces, piece, half_cols), bf16),
+            pltpu.VMEM((pieces, piece, half_cols), bf16),
+            pltpu.VMEM((pieces, piece, half_cols), bf16),
+            pltpu.SemaphoreType.DMA((5, 2)),
+            pltpu.SemaphoreType.DMA((2, 2)),
+            pltpu.SemaphoreType.DMA((3 * pieces,)),
+            pltpu.SemaphoreType.DMA((3 * pieces,)),
+            pltpu.SemaphoreType.DMA((pieces,)),
+            pltpu.VMEM((8, 128), f32),
+            pltpu.SemaphoreType.DMA((2,)),
+        ],
+        compiler_params=pltpu.CompilerParams(
+            collective_id=3, has_side_effects=True, vmem_limit_bytes=48 * 2**20
+        ),
+        name="update",
+    )(own, rest, master, first, second, factors, extras, squares)
+
+
+def pairs_of(partner):
     pairs = []
     for source in range(32):
         y, c, z, x = source // 16, source // 8 % 2, source // 2 % 4, source % 2
-        pairs.append((source, (z % 2 * 2 + z // 2) * 8 + (2 * c + y) * 2 + x))
-    return lax.ppermute(values, ("group", "dp"), pairs)
-
-
-def fetch_weights(params):
+        target = partner(y, c, z, x)
+        if target is not None:
+            pairs.append((source, (target[0] * 2 + target[1]) * 8 + target[2] * 2 + target[3]))
+    return pairs
+
+
+def next_half(y, c, z, x):
+    place_in_row = (z * 2 + x) * 2 + y + 1
+    if place_in_row == 16:
+        return None
+    return (place_in_row % 2, c, place_in_row // 4, place_in_row // 2 % 2)
+
+
+def on_grid_step(grad_rows, factors, extra, master, outer_momentum, first, second):
+    rows, width = master.shape
+    half_rows, half_cols = rows // 2, width // 2
+    y, c, z, x = place()
+    rank = lax.axis_index("dp")
+    own, factors, extras, squares = sum_on_plane(grad_rows, factors, extra, rows)
+    following = lax.ppermute(own[:16], "dp", [(source, source - 1) for source in range(1, 8)])
+    own = lax.dynamic_update_slice(own, following, (rows, 0))
+    rest = low_rank_rows(factors, jnp.sum(extras, axis=0), rank * rows + SPARE, rows)
+    first, second, total, summary = update_rows(
+        own, rest.astype(jnp.bfloat16), master, first, second, factors, extras, squares
+    )
+    groups = lax.axis_size("group")
+    at = (y * half_rows, c * half_cols)
+    quarter = [lax.dynamic_slice(whole, at, (half_rows, half_cols)) for whole in (master, outer_momentum)]
+    part, _ = nesterov(*quarter, total.astype(jnp.float32) / groups)
+    before = lax.ppermute(part[-16:], ("group", "dp"), pairs_of(next_half))
+    moved = jnp.concatenate([before, part], axis=0)[16 - SPARE :][:half_rows]
+    flat_row = rank * rows + y * half_rows + lax.broadcasted_iota(jnp.int32, (half_rows, 1), 0)
+    part = jnp.where(flat_row < layout_rows()[1], part, moved).astype(jnp.bfloat16)
+    soup_rows = gather_rows(part, rows)
+    total, soup_rows = lax.optimization_barrier((total, soup_rows))
+    over_y = lax.ppermute(total, ("group", "dp"), pairs_of(lambda y, c, z, x: (1 - y, c, z, x)))
+
+    def finish(over_y):
+        column = jnp.where(y == 0, jnp.stack([total, over_y]), jnp.stack([over_y, total]))
+        column = column.reshape(rows, half_cols)
+        sibling = lax.ppermute(
+            column, ("group", "dp"), pairs_of(lambda y, c, z, x: (y, 1 - c, z, x))
+        )
+        whole = jnp.where(
+            c == 0,
+            jnp.concatenate([column, sibling], axis=1),
+            jnp.concatenate([sibling, column], axis=1),
+        )
+        return nesterov(master, outer_momentum, whole.astype(jnp.float32) / groups)
+
+    return (over_y, finish, first, second, summary, soup_rows)
+
+
+def fetch_weights(params, pixel_rows=None, notes=None):
     rows, width = params.shape
     ranks, rank = lax.axis_size("dp"), lax.axis_index("dp")
     before = lax.ppermute(params[-16:], "dp", [(source, source + 1) for source in range(ranks - 1)])
@@ -1066,13 +1604,14 @@
     in_place = lax.broadcasted_iota(jnp.int32, (rows, 1), 0) + rank * rows < layout_rows()[1]
     if not on_grid():
         moved = jnp.where(in_place, params, longer[16 - SPARE :][:rows])
-        return lax.all_gather(moved.astype(jnp.bfloat16), "dp", axis=0, tiled=True)
+        full = lax.all_gather(moved.astype(jnp.bfloat16), "dp", axis=0, tiled=True)
+        return full if pixel_rows is None else (full, pixel_rows, notes)
     y, c, _, _ = place()
     half, half_cols = rows // 2, width // 2
     part = lax.dynamic_slice(params, (y * half, c * half_cols), (half, half_cols))
     moved = lax.dynamic_slice(longer, (y * half + 16 - SPARE, c * half_cols), (half, half_cols))
     in_place = lax.dynamic_slice(in_place, (y * half, 0), (half, 1))
-    return gather_rows(jnp.where(in_place, part, moved).astype(jnp.bfloat16), rows)
+    return gather_rows(jnp.where(in_place, part, moved).astype(jnp.bfloat16), rows, pixel_rows, notes)
 
 
 def low_rank_rows(factors, extra, first_row, count):
@@ -1112,25 +1651,30 @@
 
 def reduce_rows(grad_rows, factors, extra, count):
     ranks, rank = lax.axis_size("dp"), lax.axis_index("dp")
-    last_layer = FIRST_LAYER + 4 * D + 2 * FF
     flat_row = rank * count + lax.broadcasted_iota(jnp.int32, (count, 1), 0)
-    if on_grid():
-        shard, factors, extra = sum_on_plane(grad_rows, factors, extra, count)
-        extra = jnp.sum(extra, axis=0)
-    else:
-        rest = low_rank_rows(factors[None], extra, 0, ranks * count).astype(jnp.bfloat16)
-        whole = jnp.where(dense_row(jnp.arange(DENSE_END))[:, None], grad_rows, rest[:DENSE_END])
-        whole = jnp.concatenate([whole, rest[DENSE_END:]], axis=0)
-        shard = lax.psum_scatter(whole, "dp", scatter_dimension=0, tiled=True)
-        extra = lax.psum(extra, "dp")
+    rest = low_rank_rows(factors[None], extra, 0, ranks * count).astype(jnp.bfloat16)
+    whole = jnp.where(dense_row(jnp.arange(DENSE_END))[:, None], grad_rows, rest[:DENSE_END])
+    whole = jnp.concatenate([whole, rest[DENSE_END:]], axis=0)
+    shard = lax.psum_scatter(whole, "dp", scatter_dimension=0, tiled=True)
     following = lax.ppermute(shard[:16], "dp", [(source, source - 1) for source in range(1, ranks)])
     shifted = jnp.concatenate([shard[SPARE:], following[:SPARE]], axis=0)
     summed = jnp.where(flat_row < layout_rows()[1], shard, shifted).astype(jnp.float32)
-    if on_grid():
-        rest = low_rank_rows(factors, extra, rank * count + SPARE, count)
-        spared = jnp.where(flat_row < layout_rows()[1], flat_row, flat_row + SPARE)
-        summed = jnp.where(dense_row(spared), summed, rest)
-    return (summed, extra)
+    return (summed, lax.psum(extra, "dp"))
+
+
+def any_grid_step(grad_rows, factors, extra, master, outer_momentum, first, second):
+    reduced, extra = reduce_rows(grad_rows, factors, extra, master.shape[0])
+    count_all = extra[12, 1]
+    grad_norm = jnp.sqrt(lax.psum(jnp.sum(reduced * reduced), "dp")) / count_all
+    factor = CLIP_MAX / jnp.maximum(grad_norm, CLIP_MAX) / count_all
+    params, first, second = adam_update(master, first, second, reduced * factor, STEP)
+    delta = (master - params).astype(jnp.bfloat16)
+    mean_delta = lax.psum(delta, "group").astype(jnp.float32) / lax.axis_size("group")
+    outer = nesterov(master, outer_momentum, mean_delta)
+    summary = jnp.concatenate(
+        [extra[:10], extra[10:12] * factor, extra[12:13], jnp.full((3, D), grad_norm)], axis=0
+    )
+    return (outer, lambda done: done, first, second, summary, fetch_weights(outer[0]))
 
 
 def dense_row(row):
@@ -1171,49 +1715,37 @@
     eval_counts,
     eval_labels,
 ):
-    params = master
-    moment_one = first_moment[0]
-    moment_two = second_moment[0]
-    norm_list, loss_list, count_list, post_list = ([], [], [], [])
     slots = pixels.shape[2]
     live = (jnp.arange(slots)[None, :] < counts[0]).astype(jnp.float32).reshape(-1)
     step_labels = labels[0].reshape(-1)
     step_pixels = token_rows(pixels[0].reshape((-1,) + pixels.shape[3:]))
+    notes = image_notes(step_labels, live)
+    weights, step_pixels, notes = fetch_weights(master, step_pixels, notes)
+    grad_rows, factors, extra = run_tower(weights, step_pixels, notes, text, True)
+    step = on_grid_step if on_grid() else any_grid_step
+    waiting, finish, moment_one, moment_two, summary, soup_rows = step(
+        grad_rows, factors, extra, master, outer_momentum, first_moment[0], second_moment[0]
+    )
+    eval_live = (jnp.arange(eval_pixels.shape[0]) < eval_counts[0]).astype(jnp.float32)
+    eval_notes = image_notes(eval_labels, eval_live)
+    carried = (moment_one, moment_two) if on_grid() else ()
+    eval_tile, *carried = run_tower(
+        soup_rows, token_rows(eval_pixels), eval_notes, text, False, carried
+    )
     if on_grid():
-        step_pixels, live, step_labels = [
-            to_planes(values) for values in (step_pixels, live, step_labels)
-        ]
-    weights = fetch_weights(params)
-    grad_rows, factors, extra = run_tower(weights, step_pixels, step_labels, live, text, True)
-    reduced, extra = reduce_rows(grad_rows, factors, extra, params.shape[0])
-    loss_all, count_all, post_all = extra[12, 0], extra[12, 1], extra[10:12]
-    square_all = lax.psum(jnp.sum(reduced * reduced), "dp")
-    gradient = reduced / count_all
-    grad_norm = jnp.sqrt(square_all) / count_all
-    clip_factor = CLIP_MAX / jnp.maximum(grad_norm, CLIP_MAX)
-    clipped = gradient * clip_factor
-    params, moment_one, moment_two = adam_update(params, moment_one, moment_two, clipped, STEP)
-    norm_list.append(grad_norm)
-    loss_list.append(loss_all)
-    count_list.append(count_all)
-    post_list.append(post_all / count_all * clip_factor)
-    delta = master - params
-    groups = lax.axis_size("group")
-    mean_delta = lax.psum(delta.astype(jnp.bfloat16), "group").astype(jnp.float32) / groups
-    new_master, new_outer = nesterov(master, outer_momentum, mean_delta)
-    soup_rows = fetch_weights(new_master)
-    eval_live = (jnp.arange(eval_pixels.shape[0]) < eval_counts[0]).astype(jnp.float32)
-    eval_tile = run_tower(soup_rows, token_rows(eval_pixels), eval_labels, eval_live, text, False)
+        moment_one, moment_two = carried
+    eval_tile, waiting = lax.optimization_barrier((eval_tile, waiting))
+    new_master, new_outer = finish(waiting)
     eval_losses = eval_tile[: eval_labels.shape[0], 0]
     return (
         new_master,
         new_outer,
         moment_one[None],
         moment_two[None],
-        jnp.stack(norm_list)[None],
-        jnp.stack(loss_list)[None],
-        jnp.stack(count_list)[None],
-        jnp.stack(post_list)[None],
+        summary[13:14, :1],
+        summary[12:13, :1],
+        summary[12:13, 1:2],
+        summary[10:12][None, None],
         eval_losses,
     )
 

time: 963 us -> 784 us (0.81)
  waiting for transfers between devices: 169 us -> 3.65 us
  Pallas kernels: 630 us -> 703 us
  other arithmetic: 57.6 us -> 29.3 us
  starting transfers between devices: 33.2 us -> 13.5 us
  between operations: 17.9 us -> 1.96 us
  blocking collectives: 13.8 us -> 0 us
    psum x1 -> x0, waiting for transfers between devices: 87.4 us -> none  [per_device(): lax.psum(delta.astype(jnp.bfloat16), 'group').astype(jnp.float32) / groups]
    ppermute x4, waiting for transfers between devices: 80.2 us -> 3.65 us  [the longest x1 2.38 us: finish(): lax.ppermute(column, ('group', 'dp'), pairs_of(lambda y, c, z, x: (y, 1 -...]
    pallas_call x5 -> x6, Pallas kernels: 630 us -> 703 us  [the longest x1 214 us: gather_rows(): pl.pallas_call(kernel, out_shape=(full_shape, jax.ShapeDtypeStruct(pixel_...]
    broadcast_in_dim x2 -> x0, other arithmetic: 36 us -> none  [the longest x1 18.9 us: per_device(): moment_two[None]]
    ppermute x4, starting transfers between devices: 26.8 us -> 10.4 us  [the longest x1 4.3 us: on_grid_step(): before = lax.ppermute(part[-16:], ('group', 'dp'), pairs_of(next_half))]
    psum x1 -> x0, blocking collectives: 13.8 us -> none  [per_device(): square_all = lax.psum(jnp.sum(reduced * reduced), 'dp')]
  transfers between devices with their start and end apart: 7 -> 5, of which waited for: 3 -> 2; matrix products, arithmetic and copies ran while one was open for 2% -> 3% of each run, Pallas kernels for 18% -> 4%
where the time goes in v3:
time: 784 us; the launch traced here: 775 us
  Pallas kernels  703 us (90%)
  other arithmetic  29.3 us (4%)
  local copies, waits for them, and re-layouts  18.7 us (2%)
  starting transfers between devices  13.5 us (2%)
    pallas_call x1, Pallas kernels, gather_rows(): pl.pallas_call(kernel, out_shape=(full_shape, jax.ShapeDtypeStruct(pixel_...  214 us
    pallas_call x1, Pallas kernels, sum_on_plane(): pl.pallas_call(functools.partial(reduce_kernel, chunks, low_plane(shard_r...  176 us
    pallas_call x1, Pallas kernels, gather_rows(): pl.pallas_call(kernel, out_shape=full_shape, in_specs=[hbm], out_specs=hb...  160 us
    pallas_call x2, Pallas kernels, run_tower(): pl.pallas_call(functools.partial(tower_kernel, images, with_grads, len(ca...  120 us
    pallas_call x1, Pallas kernels, update_rows(): pl.pallas_call(functools.partial(update_kernel, (half_rows, piece, pieces...  32.6 us
    sub x2, other arithmetic, nesterov(): master_rows - OUTER_RATE * (mean_delta + OUTER_MOM * momentum_next)  17.1 us
  transfers between devices with their start and end apart: 5, of which 2 were waited for; matrix products, arithmetic and copies ran while one was open for 3% of the time, Pallas kernels for 4%

profile of v3, /device:TPU:25, one launch (start us, length us, event | category | flops | bytes accessed | tf_op | source)
XLA Modules:
  0.0 774.9 jit_solution(9797763148357138670)
XLA Ops:
  1.4 3.1 collective-permute-start
  6.3 2.4 copy.37
  9.4 1.8 pad.41.clone
  11.3 3.9 fusion.2.refs_0_
  15.2 214.1 %gather_first.1 = (bf16[4,2,2,1392,768]{4,3,2,1,0:T(8,128)(2,1)}, bf16[448,3072]{1,0:T(8,128)(2,1)}, f32[8,128]{1,0:T(8,128)}) custom-call(bf16[1392,384]{1,0:T(8,128)(2,1)} %fusion.2.refs_0_, bf16[448,3072]{1,0:T(8,128)(2,1)} %bitcast.46, f32[8,128]{1,0:T(8,128)} %pad.42.refs_2_), custom_call_target="tpu_custom_call" | custom-call | tf_op jit(solution)/shard_map/gather_first/pallas_call | solution.py:901
  229.2 91.5 %train.1 = (bf16[16704,768]{1,0:T(8,128)(2,1)}, bf16[16,6144]{1,0:T(8,128)(2,1)}, f32[16,768]{1,0:T(8,128)}) custom-call(bf16[22272,768]{1,0:T(8,128)(2,1)} %bitcast.50, bf16[448,3072]{1,0:T(8,128)(2,1)} %get-tuple-element.31.refs_1_, bf16[1000,512]{1,0:T(8,128)(2,1)} %refs_2_.3, f32[8,128]{1,0:T(8,128)} %get-tuple-element.32.refs_3_), custom_call_target="tpu_custom_call" | custom-call | flops 45977960448 | bytes 34209792 | tf_op jit(solution)/shard_map/train/pallas_call | solution.py:673
  320.7 175.9 %reduce.5 = (bf16[2800,768]{1,0:T(8,128)(2,1)}, bf16[8,16,6144]{2,1,0:T(8,128)(2,1)}, f32[8,16,768]{2,1,0:T(8,128)}, f32[8,8,128]{2,1,0:T(8,128)}) custom-call(bf16[3,2,2,1392,768]{4,3,2,1,0:T(8,128)(2,1)} %bitcast.44, bf16[16,6144]{1,0:T(8,128)(2,1)} %get-tuple-element.34.factor_ref, f32[16,768]{1,0:T(8,128)} %get-tuple-element.35.extra_ref), custom_call_target="tpu_custom_call" | custom-call | tf_op jit(solution)/shard_map/reduce/pallas_call | solution.py:1251
  496.7 1.0 slice_bitcast_fusion.4
  498.6 1.5 bitcast_dynamic-update-slice_fusion.4
  500.2 1.2 slice_bitcast_fusion
  502.1 3.0 collective-permute-start.1
  509.5 4.5 convolution_convert_fusion.rest_hbm
  514.6 32.6 %update.1 = (f32[2784,768]{1,0:T(8,128)}, f32[2784,768]{1,0:T(8,128)}, bf16[1392,384]{1,0:T(8,128)(2,1)S(1)}, f32[16,768]{1,0:T(8,128)S(1)}) custom-call(bf16[2800,768]{1,0:T(8,128)(2,1)} %constant_dynamic-update-slice_fusion.1.own_hbm, bf16[2784,768]{1,0:T(8,128)(2,1)} %convolution_convert_fusion.rest_hbm, f32[2784,768]{1,0:T(8,128)} %master_hbm.1, ...), custom_call_target="tpu_custom_call" | custom-call | tf_op jit(solution)/shard_map/update/pallas_call | solution.py:1504
  547.2 2.9 multiply_subtract_fusion.1
  550.1 4.3 collective-permute-start.2
  555.1 1.3 collective-permute-done.2
  556.3 1.5 fusion.4.refs_0_
  557.8 160.3 %gather.1 = bf16[4,2,2,1392,768]{4,3,2,1,0:T(8,128)(2,1)} custom-call(bf16[1392,384]{1,0:T(8,128)(2,1)} %fusion.4.refs_0_), custom_call_target="tpu_custom_call" | custom-call | tf_op jit(solution)/shard_map/gather/pallas_call | solution.py:891
  718.1 2.7 collective-permute-start.3
  721.3 1.2 pad.50.clone
  723.2 29.0 %evaluate.1 = (f32[8,128]{1,0:T(8,128)}, f32[2784,768]{1,0:T(8,128)}, f32[2784,768]{1,0:T(8,128)}) custom-call(bf16[22272,768]{1,0:T(8,128)(2,1)} %bitcast.43, bf16[224,3072]{1,0:T(8,128)(2,1)} %bitcast.49, bf16[1000,512]{1,0:T(8,128)(2,1)} %refs_2_.3, f32[8,128]{1,0:T(8,128)} %select_maximum_fusion.refs_3_, f32[2784,768]{1,0:T(8,128)} %get-tuple-element.43.refs_4_, ...), custom_call_target="tpu_custom_call" | custom-call | flops 7662993408 | bytes 34209792 | tf_op jit(solution)/shard_map/evaluate/pallas_call | solution.py:673
  752.2 3.4 maximum_select_fusion.1
  757.9 2.4 collective-permute-done.4
  760.3 14.3 %multiply_subtract_fusion = (f32[2784,768]{1,0:T(8,128)}, f32[2784,768]{1,0:T(8,128)}) fusion(f32[2784,768]{1,0:T(8,128)} %master_hbm.1, bf16[2784,384]{1,0:T(8,128)(2,1)} %bitcast.22, bf16[2784,384]{1,0:T(8,128)(2,1)} %collective-permute-done.4, pred[]{:T(512)S(6)} %eq.12, f32[2784,768]{1,0:T(8,128)} %param.16), kind=kLoop, calls=%fused_computation.2 | loop fusion | flops 36347904 | bytes 38486016 | tf_op jit(solution)/shard_map/sub | solution.py:1696
  (56 shorter events, 13.3 us)
Async XLA Ops:
  1.4 9.8 %collective-permute-start = (bf16[16,768]{1,0:T(8,128)(2,1)S(1)}, bf16[16,768]{1,0:T(8,128)(2,1)S(1)}, u32[]{:S(2)}, u32[]{:S(2)}) collective-permute-start(bf16[16,768]{1,0:T(8,128)(2,1)S(1)} %slice.59), channel_id=1, source_target_pairs={{0,1},{1,2},{2,3},{3,4},{4,5},{5,6},{6,7},{8,9},{9,10},{10,11},{11... | collective-permute-start | bytes 73736 | tf_op jit(solution)/shard_map/ppermute | solution.py:1602
  496.7 5.4 copy-start.1
  496.7 8.4 %copy-start = (bf16[8,16,6144]{2,1,0:T(8,128)(2,1)S(1)}, bf16[8,16,6144]{2,1,0:T(8,128)(2,1)}, u32[]{:S(2)}) copy-start(bf16[8,16,6144]{2,1,0:T(8,128)(2,1)} %get-tuple-element.37.factors_ref) | copy-start | bytes 4718596
  502.1 11.8 %collective-permute-start.1 = (bf16[16,768]{1,0:T(8,128)(2,1)S(1)}, bf16[16,768]{1,0:T(8,128)(2,1)S(1)}, u32[]{:S(2)}, u32[]{:S(2)}) collective-permute-start(bf16[16,768]{1,0:T(8,128)(2,1)S(1)} %slice.60), channel_id=1, source_target_pairs={{1,0},{2,1},{3,2},{4,3},{5,4},{6,5},{7,6},{9,8},{10,9},{11,10},{12... | collective-permute-start | bytes 73736 | tf_op jit(solution)/shard_map/ppermute | solution.py:1565
  508.3 1.2 copy-start.4
  509.5 5.1 copy-start.2
  550.1 6.2 collective-permute-start.2
  557.8 163.0 %copy-start.6 = (s32[4]{0:T(128)S(1)}, s32[4]{0:T(128)}, u32[]{:S(2)}) copy-start(s32[4]{0:T(128)} %param.21) | copy-start | bytes 52
  557.8 163.1 %copy-start.3 = (bf16[4,49,3072]{2,0,1:T(4,128)(2,1)S(1)}, bf16[4,49,3072]{2,0,1:T(4,128)(2,1)}, u32[]{:S(2)}) copy-start(bf16[4,49,3072]{2,0,1:T(4,128)(2,1)} %param.19) | copy-start | bytes 3612676
  718.1 34.1 %collective-permute-start.3 = (bf16[1392,384]{1,0:T(8,128)(2,1)S(1)}, bf16[1392,384]{1,0:T(8,128)(2,1)}, u32[]{:S(2)}, u32[]{:S(2)}) collective-permute-start(bf16[1392,384]{1,0:T(8,128)(2,1)S(1)} %get-tuple-element.41), channel_id=1, source_target_pairs={{0,16},{1,17},{2,18},{3,19},{4,20},{5,21},{6,22},{7,23},{8,24},{9,... | collective-permute-start | bytes 3207176 | tf_op jit(solution)/shard_map/ppermute | solution.py:1581
  752.2 5.0 copy-start.5
  755.6 4.6 collective-permute-start.4

commit v4 on v3

--- a/solution.py
+++ b/solution.py
@@ -41,6 +41,7 @@
 LOOK_AHEAD = 3
 PARCEL_STEP = 1
 REDUCE_HEAD = [4, 6]
+RELAY_LAG = 2
 REDUCE_TAIL = [4]
 
 
@@ -676,9 +677,11 @@
         in_specs=[hbm, hbm, vmem, vmem] + [hbm] * len(carried),
         out_specs=out_specs,
         scratch_shapes=scratch,
-        compiler_params=pltpu.CompilerParams(vmem_limit_bytes=60 * 2**20),
-        cost_estimate=pl.CostEstimate(
-            flops=(6 if with_grads else 2) * rows_all * weights.shape[0] * D,
+        compiler_params=pltpu.CompilerParams(vmem_limit_bytes=(52 if with_grads else 40) * 2**20),
+        cost_estimate=None
+        if with_grads
+        else pl.CostEstimate(
+            flops=2 * rows_all * weights.shape[0] * D,
             bytes_accessed=2 * weights.shape[0] * D,
             transcendentals=rows_all * 2 * FF,
         ),
@@ -933,6 +936,7 @@
     squares,
     passed_factor,
     passed_extra,
+    relay,
     load_sems,
     sends,
     recvs,
@@ -941,7 +945,7 @@
     pass_sends,
     pass_recvs,
 ):
-    half_cols = mine.shape[-1]
+    half_cols = first_sum.shape[-1]
     planes = grad_ref.shape[0]
     y, c, z, x = place()
     home_y, home_c = z % 2, z // 2
@@ -969,6 +973,17 @@
                 device_id_type=MESH,
             )
 
+    through_self = z // 2 == c
+    for other in range(4):
+        from_z = 2 * c + other // 2
+        itself = jnp.logical_and(z == from_z, c == other % 2)
+
+        @pl.when(jnp.logical_not(itself))
+        def _():
+            pl.semaphore_signal(
+                barrier, inc=1, device_id=device_at(y, other % 2, from_z, x), device_id_type=MESH
+            )
+
     def spans(index):
         start, first, second = chunks[index]
         start_a = sum(chunk[1] for chunk in chunks[:index])
@@ -1000,7 +1015,7 @@
     def load(index):
         rows = spans(index)[0]
         return pltpu.make_async_copy(
-            grad_ref.at[:, :, :, rows, my_cols],
+            grad_ref.at[:, :, :, rows],
             mine.at[index % 2, :, :, :, pl.ds(0, rows.size)],
             load_sems.at[index % 2],
         )
@@ -1015,13 +1030,16 @@
             index,
         )
 
+    def own_rows(half, rows):
+        return pl.ds(pl.multiple_of(half * grad_ref.shape[3] + rows.start, 16), rows.size)
+
     def add(target, source):
         summed = target[...].astype(jnp.float32) + source[...].astype(jnp.float32)
         target[...] = summed.astype(target.dtype)
 
     total = len(chunks)
     load(0).start()
-    pl.semaphore_wait(barrier, 3 + jnp.where(at_home, 7, 8))
+    pl.semaphore_wait(barrier, 3 + jnp.where(at_home, 7, 8) + jnp.where(through_self, 3, 4))
     send_core(0)
     send_core(1)
     def slot_of(from_y):
@@ -1091,7 +1109,7 @@
         for part in range(half_cols // 128):
             squares[...] += values[:, part * 128 : (part + 1) * 128]
 
-    for step in range(total + 4):
+    for step in range(total + 2 + RELAY_LAG):
         index = step
         if index < total:
             if index + 1 < total:
@@ -1107,7 +1125,7 @@
                 zz, rest = block // 4, block % 4
                 add(
                     first_sum.at[zz, rest // 2, rest % 2, rows],
-                    mine.at[index % 2, zz, rest // 2, rest % 2, pl.ds(0, rows.size)],
+                    mine.at[index % 2, zz, rest // 2, rest % 2, pl.ds(0, rows.size), my_cols],
                 )
 
             if index == 1:
@@ -1149,18 +1167,38 @@
                 add(last_sum.at[block, rows_b], sum_b.at[block, x, in_b])
                 add_squares(block, rows)
 
+            on_home_y = y == home_y
             for to_z in range(planes):
-                itself = jnp.logical_and(at_home, z == to_z)
+                itself = jnp.logical_and(through_self, z == to_z)
                 source = last_sum.at[to_z, rows]
-                target = own_ref.at[pl.ds(pl.multiple_of(y * half_rows + rows.start, 16), rows.size), my_cols]
-
-                @pl.when(jnp.logical_not(itself))
-                def _():
-                    send(source, target, device_at(home_y, home_c, to_z, x), 5, index)
-
-                @pl.when(itself)
-                def _():
-                    pltpu.make_async_copy(source, target, recvs.at[5, index]).start()
+                for direct in (True, False):
+                    chosen = on_home_y if direct else jnp.logical_not(on_home_y)
+                    target = own_ref.at[own_rows(y, rows), my_cols] if direct else relay.at[rows, my_cols]
+                    way = 5 if direct else 6
+
+                    @pl.when(jnp.logical_and(chosen, jnp.logical_not(itself)))
+                    def _():
+                        pltpu.make_async_remote_copy(
+                            src_ref=source,
+                            dst_ref=target,
+                            send_sem=sends.at[5, index],
+                            recv_sem=recvs.at[way, index],
+                            device_id=device_at(y, home_c, to_z, x),
+                            device_id_type=MESH,
+                        ).start()
+
+                    @pl.when(jnp.logical_and(chosen, itself))
+                    def _():
+                        pltpu.make_async_copy(source, target, recvs.at[way, index]).start()
+
+        index = step - 2 - RELAY_LAG
+        if 0 <= index < total:
+            rows = spans(index)[0]
+
+            @pl.when(z < planes)
+            def _():
+                arrived(relay.at[rows], 6, index)
+                send(relay.at[rows], own_ref.at[own_rows(y, rows)], over_y, 7, index)
 
     to_owners(squares, squares_ref.at[slot_of(y)], 2, 0, 0)
     for index in range(total):
@@ -1168,7 +1206,9 @@
 
         @pl.when(z < planes)
         def _():
-            arrived(own_ref.at[pl.ds(0, 2 * rows.size)], 5, index)
+            arrived(own_ref.at[pl.ds(0, rows.size)], 5, index)
+            arrived(own_ref.at[pl.ds(0, rows.size)], 7, index)
+            sent(relay.at[rows], 7, index)
 
         sent(first_sum.at[:, :, :, rows], 0, index)
         sent(sum_a.at[:, :, in_a], 1, index)
@@ -1176,7 +1216,7 @@
         sent(last_sum.at[:, rows_a], 3, index)
         sent(last_sum.at[:, rows_b], 4, index)
 
-        kept = jnp.logical_and(at_home, z < planes)
+        kept = jnp.logical_and(through_self, z < planes)
 
         @pl.when(kept)
         def _():
@@ -1259,7 +1299,7 @@
         in_specs=[pl.BlockSpec(memory_space=pl.ANY)] * 3,
         out_specs=[pl.BlockSpec(memory_space=pl.ANY)] * 4,
         scratch_shapes=[
-            pltpu.VMEM((2, planes, 2, 2, most, half_cols), dtype),
+            pltpu.VMEM((2, planes, 2, 2, most, width), dtype),
             pltpu.VMEM((planes, 2, 2, half_rows, half_cols), dtype),
             pltpu.VMEM((planes, 2, sum(chunk[1] for chunk in chunks), half_cols), dtype),
             pltpu.VMEM((planes, 2, sum(chunk[2] for chunk in chunks), half_cols), dtype),
@@ -1267,9 +1307,10 @@
             pltpu.VMEM((8, 128), jnp.float32),
             pltpu.VMEM(factors.shape, factors.dtype),
             pltpu.VMEM(extra.shape, extra.dtype),
+            pltpu.VMEM((half_rows, width), dtype),
             pltpu.SemaphoreType.DMA((2,)),
-            pltpu.SemaphoreType.DMA((6, len(chunks))),
-            pltpu.SemaphoreType.DMA((6, len(chunks))),
+            pltpu.SemaphoreType.DMA((8, len(chunks))),
+            pltpu.SemaphoreType.DMA((8, len(chunks))),
             pltpu.SemaphoreType.DMA((2, 3)),
             pltpu.SemaphoreType.DMA((3,)),
             pltpu.SemaphoreType.DMA((2,)),

time: 784 us -> 774 us (0.987)
  Pallas kernels: 703 us -> 679 us
  starting transfers between devices: 13.5 us -> 23.7 us
    pallas_call x2, Pallas kernels: 120 us -> 103 us  [run_tower(): pl.pallas_call(functools.partial(tower_kernel, images, with_grads, len(ca...]
    ppermute x1, starting transfers between devices: 2.95 us -> 13 us  [on_grid_step(): lax.ppermute(own[:16], 'dp', [(source, source - 1) for source in range(1,...]
  transfers between devices with their start and end apart: 5 -> 5, of which waited for: 2 -> 2; matrix products, arithmetic and copies ran while one was open for 3% -> 3% of each run, Pallas kernels for 4% -> 3%
where the time goes in v4:
time: 774 us; the launch traced here: 765 us
  Pallas kernels  679 us (88%)
  other arithmetic  28.5 us (4%)
  local copies, waits for them, and re-layouts  24.3 us (3%)
  starting transfers between devices  23.7 us (3%)
    pallas_call x1, Pallas kernels, gather_rows(): pl.pallas_call(kernel, out_shape=(full_shape, jax.ShapeDtypeStruct(pixel_...  214 us
    pallas_call x1, Pallas kernels, sum_on_plane(): pl.pallas_call(functools.partial(reduce_kernel, chunks, low_plane(shard_r...  171 us
    pallas_call x1, Pallas kernels, gather_rows(): pl.pallas_call(kernel, out_shape=full_shape, in_specs=[hbm], out_specs=hb...  160 us
    pallas_call x2, Pallas kernels, run_tower(): pl.pallas_call(functools.partial(tower_kernel, images, with_grads, len(ca...  103 us
    pallas_call x1, Pallas kernels, update_rows(): pl.pallas_call(functools.partial(update_kernel, (half_rows, piece, pieces...  31.1 us
    sub x2, other arithmetic, nesterov(): master_rows - OUTER_RATE * (mean_delta + OUTER_MOM * momentum_next)  17.1 us
  transfers between devices with their start and end apart: 5, of which 2 were waited for; matrix products, arithmetic and copies ran while one was open for 3% of the time, Pallas kernels for 3%

profile of v4, /device:TPU:25, one launch (start us, length us, event | category | flops | bytes accessed | tf_op | source)
XLA Modules:
  0.0 765.2 jit_solution(2002438009498347810)
XLA Ops:
  1.4 3.1 collective-permute-start
  6.3 2.4 copy.37
  9.4 1.8 pad.41.clone
  11.3 3.9 fusion.2.refs_0_
  15.2 214.1 %gather_first.1 = (bf16[4,2,2,1392,768]{4,3,2,1,0:T(8,128)(2,1)}, bf16[448,3072]{1,0:T(8,128)(2,1)}, f32[8,128]{1,0:T(8,128)}) custom-call(bf16[1392,384]{1,0:T(8,128)(2,1)} %fusion.2.refs_0_, bf16[448,3072]{1,0:T(8,128)(2,1)} %bitcast.48, f32[8,128]{1,0:T(8,128)} %pad.42.refs_2_), custom_call_target="tpu_custom_call" | custom-call | tf_op jit(solution)/shard_map/gather_first/pallas_call | solution.py:904
  229.9 77.6 %train.1 = (bf16[16704,768]{1,0:T(8,128)(2,1)}, bf16[16,6144]{1,0:T(8,128)(2,1)S(1)}, f32[16,768]{1,0:T(8,128)S(1)}) custom-call(bf16[22272,768]{1,0:T(8,128)(2,1)} %bitcast.45, bf16[448,3072]{1,0:T(8,128)(2,1)} %get-tuple-element.31.refs_1_, bf16[1000,512]{1,0:T(8,128)(2,1)S(1)} %copy-done.2, f32[8,128]{1,0:T(8,128)S(1)} %copy-done.8), custom_call_target="tpu_custom_call" | custom-call | tf_op jit(solution)/shard_map/train/pallas_call | solution.py:674
  308.8 170.5 %reduce.5 = (bf16[2800,768]{1,0:T(8,128)(2,1)}, bf16[8,16,6144]{2,1,0:T(8,128)(2,1)}, f32[8,16,768]{2,1,0:T(8,128)}, f32[8,8,128]{2,1,0:T(8,128)}) custom-call(bf16[3,2,2,1392,768]{4,3,2,1,0:T(8,128)(2,1)} %bitcast.46, bf16[16,6144]{1,0:T(8,128)(2,1)} %copy-done.5, f32[16,768]{1,0:T(8,128)} %copy-done.6), custom_call_target="tpu_custom_call" | custom-call | tf_op jit(solution)/shard_map/reduce/pallas_call | solution.py:1291
  479.4 1.0 slice_bitcast_fusion.4
  481.3 1.5 bitcast_dynamic-update-slice_fusion.4
  482.9 1.2 slice_bitcast_fusion
  484.8 13.0 %collective-permute-start.1 = (bf16[16,768]{1,0:T(8,128)(2,1)S(1)}, bf16[16,768]{1,0:T(8,128)(2,1)S(1)}, u32[]{:S(2)}, u32[]{:S(2)}) collective-permute-start(bf16[16,768]{1,0:T(8,128)(2,1)S(1)} %slice.60), channel_id=1, source_target_pairs={{1,0},{2,1},{3,2},{4,3},{5,4},{6,5},{7,6},{9,8},{10,9},{11,10},{12... | collective-permute-start | bytes 73736 | tf_op jit(solution)/shard_map/ppermute | solution.py:1606
  502.2 4.5 convolution_convert_fusion.rest_hbm
  507.3 31.1 %update.1 = (f32[2784,768]{1,0:T(8,128)}, f32[2784,768]{1,0:T(8,128)}, bf16[1392,384]{1,0:T(8,128)(2,1)S(1)}, f32[16,768]{1,0:T(8,128)S(1)}) custom-call(bf16[2800,768]{1,0:T(8,128)(2,1)} %constant_dynamic-update-slice_fusion.1.own_hbm, bf16[2784,768]{1,0:T(8,128)(2,1)} %convolution_convert_fusion.rest_hbm, f32[2784,768]{1,0:T(8,128)} %master_hbm.1, ...), custom_call_target="tpu_custom_call" | custom-call | tf_op jit(solution)/shard_map/update/pallas_call | solution.py:1545
  538.4 2.9 multiply_subtract_fusion.1
  541.3 4.6 collective-permute-start.2
  547.6 1.5 fusion.4.refs_0_
  549.0 159.7 %gather.1 = bf16[4,2,2,1392,768]{4,3,2,1,0:T(8,128)(2,1)} custom-call(bf16[1392,384]{1,0:T(8,128)(2,1)} %fusion.4.refs_0_), custom_call_target="tpu_custom_call" | custom-call | tf_op jit(solution)/shard_map/gather/pallas_call | solution.py:894
  708.8 2.6 collective-permute-start.3
  711.4 1.8 copy.36
  713.4 3.4 copy-done
  716.8 25.7 %evaluate.1 = (f32[8,128]{1,0:T(8,128)S(1)}, f32[2784,768]{1,0:T(8,128)}, f32[2784,768]{1,0:T(8,128)}) custom-call(bf16[22272,768]{1,0:T(8,128)(2,1)} %bitcast.44, bf16[224,3072]{1,0:T(8,128)(2,1)S(1)} %bitcast.42, bf16[1000,512]{1,0:T(8,128)(2,1)S(1)} %copy-done.3, f32[8,128]{1,0:T(8,128)S(1)} %select_maximum_fusion.refs_3_, f32[2784,768]{1,0:T(8,128)S(1)} %copy-done, ...), custom_call_target="tpu_custom_call" | custom-call | flops 7662993408 | bytes 34209792 | tf_op jit(solution)/shard_map/evaluate/pallas_call | solution.py:674
  742.6 3.3 maximum_select_fusion.1
  748.1 2.4 collective-permute-done.4
  750.5 14.3 %multiply_subtract_fusion = (f32[2784,768]{1,0:T(8,128)}, f32[2784,768]{1,0:T(8,128)}) fusion(f32[2784,768]{1,0:T(8,128)} %master_hbm.1, bf16[2784,384]{1,0:T(8,128)(2,1)} %bitcast.22, bf16[2784,384]{1,0:T(8,128)(2,1)} %collective-permute-done.4, pred[]{:T(512)S(6)} %eq.12, f32[2784,768]{1,0:T(8,128)} %param.16), kind=kLoop, calls=%fused_computation.2 | loop fusion | flops 36347904 | bytes 38486016 | tf_op jit(solution)/shard_map/sub | solution.py:1737
  (64 shorter events, 15.3 us)
Async XLA Ops:
  1.4 9.8 %collective-permute-start = (bf16[16,768]{1,0:T(8,128)(2,1)S(1)}, bf16[16,768]{1,0:T(8,128)(2,1)S(1)}, u32[]{:S(2)}, u32[]{:S(2)}) collective-permute-start(bf16[16,768]{1,0:T(8,128)(2,1)S(1)} %slice.59), channel_id=1, source_target_pairs={{0,1},{1,2},{2,3},{3,4},{4,5},{5,6},{6,7},{8,9},{9,10},{10,11},{11... | collective-permute-start | bytes 73736 | tf_op jit(solution)/shard_map/ppermute | solution.py:1643
  15.2 214.1 %copy-start.2 = (bf16[1000,512]{1,0:T(8,128)(2,1)S(1)}, bf16[1000,512]{1,0:T(8,128)(2,1)}, u32[]{:S(2)}) copy-start(bf16[1000,512]{1,0:T(8,128)(2,1)} %refs_2_.3) | copy-start | bytes 3072004
  229.3 0.7 copy-start.8
  307.5 0.7 copy-start.5
  308.2 0.6 copy-start.6
  479.4 5.4 copy-start.4
  479.4 18.4 %copy-start.1 = (bf16[8,16,6144]{2,1,0:T(8,128)(2,1)S(1)}, bf16[8,16,6144]{2,1,0:T(8,128)(2,1)}, u32[]{:S(2)}) copy-start(bf16[8,16,6144]{2,1,0:T(8,128)(2,1)} %get-tuple-element.37.factors_ref) | copy-start | bytes 4718596
  484.8 21.9 %collective-permute-start.1 = (bf16[16,768]{1,0:T(8,128)(2,1)S(1)}, bf16[16,768]{1,0:T(8,128)(2,1)S(1)}, u32[]{:S(2)}, u32[]{:S(2)}) collective-permute-start(bf16[16,768]{1,0:T(8,128)(2,1)S(1)} %slice.60), channel_id=1, source_target_pairs={{1,0},{2,1},{3,2},{4,3},{5,4},{6,5},{7,6},{9,8},{10,9},{11,10},{12... | collective-permute-start | bytes 73736 | tf_op jit(solution)/shard_map/ppermute | solution.py:1606
  501.0 1.2 copy-start.9
  502.2 5.1 copy-start.7
  541.3 6.2 collective-permute-start.2
  549.0 162.3 %copy-start.10 = (s32[4]{0:T(128)S(1)}, s32[4]{0:T(128)}, u32[]{:S(2)}) copy-start(s32[4]{0:T(128)} %param.21) | copy-start | bytes 52
  708.8 33.8 %collective-permute-start.3 = (bf16[1392,384]{1,0:T(8,128)(2,1)S(1)}, bf16[1392,384]{1,0:T(8,128)(2,1)}, u32[]{:S(2)}, u32[]{:S(2)}) collective-permute-start(bf16[1392,384]{1,0:T(8,128)(2,1)S(1)} %get-tuple-element.41), channel_id=1, source_target_pairs={{0,16},{1,17},{2,18},{3,19},{4,20},{5,21},{6,22},{7,23},{8,24},{9,... | collective-permute-start | bytes 3207176 | tf_op jit(solution)/shard_map/ppermute | solution.py:1622
  711.4 2.0 copy-start.3
  713.4 3.4 copy-start
  745.9 4.6 collective-permute-start.4

commit v5 on v4

--- a/solution.py
+++ b/solution.py
@@ -41,7 +41,7 @@
 LOOK_AHEAD = 3
 PARCEL_STEP = 1
 REDUCE_HEAD = [4, 6]
-RELAY_LAG = 2
+RELAY_LAG = 1
 REDUCE_TAIL = [4]
 
 
@@ -1284,7 +1284,7 @@
 def sum_on_plane(grad_rows, factors, extra, shard_rows):
     half_rows, width = shard_rows // 2, grad_rows.shape[1]
     planes = grad_rows.shape[0] // (2 * shard_rows)
-    chunks = reduce_chunks(half_rows, 0.75)
+    chunks = reduce_chunks(half_rows, 0.65)
     most = max(first + second for _, first, second in chunks)
     half_cols = width // 2
     dtype = grad_rows.dtype
@@ -1505,9 +1505,9 @@
                     copy.wait()
             for copy in loads(index + 1):
                 copy.start()
-        step(index)
         if index >= 1:
             fold(index - 1)
+        step(index)
     fold(steps - 1)
 
     def hand_over(index):

time: 774 us -> 771 us (level)
  no operation moved by 1% of the time
where the time goes in v5:
time: 771 us; the launch traced here: 762 us
  Pallas kernels  678 us (88%)
  other arithmetic  28.5 us (4%)
  local copies, waits for them, and re-layouts  24.3 us (3%)
  starting transfers between devices  21.6 us (3%)
    pallas_call x1, Pallas kernels, gather_rows(): pl.pallas_call(kernel, out_shape=(full_shape, jax.ShapeDtypeStruct(pixel_...  214 us
    pallas_call x1, Pallas kernels, sum_on_plane(): pl.pallas_call(functools.partial(reduce_kernel, chunks, low_plane(shard_r...  170 us
    pallas_call x1, Pallas kernels, gather_rows(): pl.pallas_call(kernel, out_shape=full_shape, in_specs=[hbm], out_specs=hb...  160 us
    pallas_call x2, Pallas kernels, run_tower(): pl.pallas_call(functools.partial(tower_kernel, images, with_grads, len(ca...  103 us
    pallas_call x1, Pallas kernels, update_rows(): pl.pallas_call(functools.partial(update_kernel, (half_rows, piece, pieces...  30.2 us
    sub x2, other arithmetic, nesterov(): master_rows - OUTER_RATE * (mean_delta + OUTER_MOM * momentum_next)  17.1 us
  transfers between devices with their start and end apart: 5, of which 2 were waited for; matrix products, arithmetic and copies ran while one was open for 3% of the time, Pallas kernels for 3%

profile of v5, /device:TPU:25, one launch (start us, length us, event | category | flops | bytes accessed | tf_op | source)
XLA Modules:
  0.0 762.2 jit_solution(15814450824895827118)
XLA Ops:
  1.4 3.1 collective-permute-start
  6.3 2.4 copy.37
  9.4 1.8 pad.41.clone
  11.3 3.9 fusion.2.refs_0_
  15.2 214.1 %gather_first.1 = (bf16[4,2,2,1392,768]{4,3,2,1,0:T(8,128)(2,1)}, bf16[448,3072]{1,0:T(8,128)(2,1)}, f32[8,128]{1,0:T(8,128)}) custom-call(bf16[1392,384]{1,0:T(8,128)(2,1)} %fusion.2.refs_0_, bf16[448,3072]{1,0:T(8,128)(2,1)} %bitcast.48, f32[8,128]{1,0:T(8,128)} %pad.42.refs_2_), custom_call_target="tpu_custom_call" | custom-call | tf_op jit(solution)/shard_map/gather_first/pallas_call | solution.py:904
  229.9 77.6 %train.1 = (bf16[16704,768]{1,0:T(8,128)(2,1)}, bf16[16,6144]{1,0:T(8,128)(2,1)S(1)}, f32[16,768]{1,0:T(8,128)S(1)}) custom-call(bf16[22272,768]{1,0:T(8,128)(2,1)} %bitcast.45, bf16[448,3072]{1,0:T(8,128)(2,1)} %get-tuple-element.31.refs_1_, bf16[1000,512]{1,0:T(8,128)(2,1)S(1)} %copy-done.2, f32[8,128]{1,0:T(8,128)S(1)} %copy-done.8), custom_call_target="tpu_custom_call" | custom-call | tf_op jit(solution)/shard_map/train/pallas_call | solution.py:674
  308.8 169.9 %reduce.5 = (bf16[2800,768]{1,0:T(8,128)(2,1)}, bf16[8,16,6144]{2,1,0:T(8,128)(2,1)}, f32[8,16,768]{2,1,0:T(8,128)}, f32[8,8,128]{2,1,0:T(8,128)}) custom-call(bf16[3,2,2,1392,768]{4,3,2,1,0:T(8,128)(2,1)} %bitcast.46, bf16[16,6144]{1,0:T(8,128)(2,1)} %copy-done.5, f32[16,768]{1,0:T(8,128)} %copy-done.6), custom_call_target="tpu_custom_call" | custom-call | tf_op jit(solution)/shard_map/reduce/pallas_call | solution.py:1291
  480.7 1.5 bitcast_dynamic-update-slice_fusion.4
  482.2 1.2 slice_bitcast_fusion
  484.2 10.2 %collective-permute-start.1 = (bf16[16,768]{1,0:T(8,128)(2,1)S(1)}, bf16[16,768]{1,0:T(8,128)(2,1)S(1)}, u32[]{:S(2)}, u32[]{:S(2)}) collective-permute-start(bf16[16,768]{1,0:T(8,128)(2,1)S(1)} %slice.60), channel_id=1, source_target_pairs={{1,0},{2,1},{3,2},{4,3},{5,4},{6,5},{7,6},{9,8},{10,9},{11,10},{12... | collective-permute-start | bytes 73736 | tf_op jit(solution)/shard_map/ppermute | solution.py:1606
  498.8 4.5 convolution_convert_fusion.rest_hbm
  503.9 30.2 %update.1 = (f32[2784,768]{1,0:T(8,128)}, f32[2784,768]{1,0:T(8,128)}, bf16[1392,384]{1,0:T(8,128)(2,1)S(1)}, f32[16,768]{1,0:T(8,128)S(1)}) custom-call(bf16[2800,768]{1,0:T(8,128)(2,1)} %constant_dynamic-update-slice_fusion.1.own_hbm, bf16[2784,768]{1,0:T(8,128)(2,1)} %convolution_convert_fusion.rest_hbm, f32[2784,768]{1,0:T(8,128)} %master_hbm.1, ...), custom_call_target="tpu_custom_call" | custom-call | tf_op jit(solution)/shard_map/update/pallas_call | solution.py:1545
  534.1 2.9 multiply_subtract_fusion.1
  536.9 4.5 collective-permute-start.2
  542.1 1.1 collective-permute-done.2
  543.2 1.5 fusion.4.refs_0_
  544.6 160.4 %gather.1 = bf16[4,2,2,1392,768]{4,3,2,1,0:T(8,128)(2,1)} custom-call(bf16[1392,384]{1,0:T(8,128)(2,1)} %fusion.4.refs_0_), custom_call_target="tpu_custom_call" | custom-call | tf_op jit(solution)/shard_map/gather/pallas_call | solution.py:894
  705.0 3.3 collective-permute-start.3
  708.4 1.8 copy.36
  710.4 3.4 copy-done
  713.8 25.7 %evaluate.1 = (f32[8,128]{1,0:T(8,128)S(1)}, f32[2784,768]{1,0:T(8,128)}, f32[2784,768]{1,0:T(8,128)}) custom-call(bf16[22272,768]{1,0:T(8,128)(2,1)} %bitcast.44, bf16[224,3072]{1,0:T(8,128)(2,1)S(1)} %bitcast.42, bf16[1000,512]{1,0:T(8,128)(2,1)S(1)} %copy-done.3, f32[8,128]{1,0:T(8,128)S(1)} %select_maximum_fusion.refs_3_, f32[2784,768]{1,0:T(8,128)S(1)} %copy-done, ...), custom_call_target="tpu_custom_call" | custom-call | flops 7662993408 | bytes 34209792 | tf_op jit(solution)/shard_map/evaluate/pallas_call | solution.py:674
  739.6 3.3 maximum_select_fusion.1
  745.1 2.4 collective-permute-done.4
  747.5 14.3 %multiply_subtract_fusion = (f32[2784,768]{1,0:T(8,128)}, f32[2784,768]{1,0:T(8,128)}) fusion(f32[2784,768]{1,0:T(8,128)} %master_hbm.1, bf16[2784,384]{1,0:T(8,128)(2,1)} %bitcast.22, bf16[2784,384]{1,0:T(8,128)(2,1)} %collective-permute-done.4, pred[]{:T(512)S(6)} %eq.12, f32[2784,768]{1,0:T(8,128)} %param.16), kind=kLoop, calls=%fused_computation.2 | loop fusion | flops 36347904 | bytes 38486016 | tf_op jit(solution)/shard_map/sub | solution.py:1737
  (64 shorter events, 15.4 us)
Async XLA Ops:
  1.4 9.8 %collective-permute-start = (bf16[16,768]{1,0:T(8,128)(2,1)S(1)}, bf16[16,768]{1,0:T(8,128)(2,1)S(1)}, u32[]{:S(2)}, u32[]{:S(2)}) collective-permute-start(bf16[16,768]{1,0:T(8,128)(2,1)S(1)} %slice.59), channel_id=1, source_target_pairs={{0,1},{1,2},{2,3},{3,4},{4,5},{5,6},{6,7},{8,9},{9,10},{10,11},{11... | collective-permute-start | bytes 73736 | tf_op jit(solution)/shard_map/ppermute | solution.py:1643
  15.2 214.1 %copy-start.2 = (bf16[1000,512]{1,0:T(8,128)(2,1)S(1)}, bf16[1000,512]{1,0:T(8,128)(2,1)}, u32[]{:S(2)}) copy-start(bf16[1000,512]{1,0:T(8,128)(2,1)} %refs_2_.3) | copy-start | bytes 3072004
  229.3 0.7 copy-start.8
  307.5 0.7 copy-start.5
  308.2 0.6 copy-start.6
  478.7 5.4 copy-start.4
  478.7 15.7 %copy-start.1 = (bf16[8,16,6144]{2,1,0:T(8,128)(2,1)S(1)}, bf16[8,16,6144]{2,1,0:T(8,128)(2,1)}, u32[]{:S(2)}) copy-start(bf16[8,16,6144]{2,1,0:T(8,128)(2,1)} %get-tuple-element.37.factors_ref) | copy-start | bytes 4718596
  484.2 19.1 %collective-permute-start.1 = (bf16[16,768]{1,0:T(8,128)(2,1)S(1)}, bf16[16,768]{1,0:T(8,128)(2,1)S(1)}, u32[]{:S(2)}, u32[]{:S(2)}) collective-permute-start(bf16[16,768]{1,0:T(8,128)(2,1)S(1)} %slice.60), channel_id=1, source_target_pairs={{1,0},{2,1},{3,2},{4,3},{5,4},{6,5},{7,6},{9,8},{10,9},{11,10},{12... | collective-permute-start | bytes 73736 | tf_op jit(solution)/shard_map/ppermute | solution.py:1606
  497.6 1.2 copy-start.9
  498.8 5.1 copy-start.7
  536.9 6.2 collective-permute-start.2
  544.6 163.7 %copy-start.10 = (s32[4]{0:T(128)S(1)}, s32[4]{0:T(128)}, u32[]{:S(2)}) copy-start(s32[4]{0:T(128)} %param.21) | copy-start | bytes 52
  705.0 34.6 %collective-permute-start.3 = (bf16[1392,384]{1,0:T(8,128)(2,1)S(1)}, bf16[1392,384]{1,0:T(8,128)(2,1)}, u32[]{:S(2)}, u32[]{:S(2)}) collective-permute-start(bf16[1392,384]{1,0:T(8,128)(2,1)S(1)} %get-tuple-element.41), channel_id=1, source_target_pairs={{0,16},{1,17},{2,18},{3,19},{4,20},{5,21},{6,22},{7,23},{8,24},{9,... | collective-permute-start | bytes 3207176 | tf_op jit(solution)/shard_map/ppermute | solution.py:1622
  708.4 2.0 copy-start.3
  710.4 3.4 copy-start
  742.9 4.6 collective-permute-start.4
